TPU v7x, 32 devices: a whole 2x2x4 slice. The times are simulated.
32 devices in a mesh: scene: 2 (over y), curve: 4 (over z), slab: 4 (over x, core).
Axes of the slice: x: 2, y: 2, z: 4, core: 2. Of those that a mesh axis runs over, the one named last changes fastest.
Arguments:
- features: bfloat16 [256, 32, 512], P(('scene', 'curve', 'slab')), parts along dimension 0, may hold values from -6 to 6
- voxel_mask: int32 [256, 512], P(('scene', 'curve', 'slab')), parts along dimension 0, may hold values 0 or 1
- weights: bfloat16 [27, 32, 32], replicated, may hold values from -0.21875 to 0.21875
- grad_out: bfloat16 [256, 32, 512], P(('scene', 'curve', 'slab')), parts along dimension 0, may hold values from -6 to 6
- send_list: int32 [32, 8, 2], P(('scene', 'curve', 'slab')), parts along dimension 0, may hold values from -1 to 7, as said below
- kernel_map: int32 [256, 27], P(('scene', 'curve', 'slab')), parts along dimension 0, may hold values from -1 to 23, as said below
Outputs:
- convolved: bfloat16 [256, 32, 512], P(('scene', 'curve', 'slab')), parts along dimension 0
- grad_features: float32 [256, 32, 512], P(('scene', 'curve', 'slab')), parts along dimension 0
- grad_weights: float32 [54, 32, 32], P('scene'), parts along dimension 0
There are 2 independent parts, one for each index of `scene`. A program takes and returns all parts, laid end to end along the dimension named above; an argument that names none is the same for every part. Nothing has to cross between parts.
Inputs may be any that keep to these rules, and one draw needn't show every extreme that they name: send_list[q, u, k] lists, in slot k, a brick of range q (as an index within the range) that range (q + d(u)) mod 16 receives; -1 marks an empty slot. The slot with u = 7 and k = 1 is filled in every row. `kernel_map`: entry [b, j] for brick b of range r is -1 (no brick), an index i below 8 (brick r * 8 + i), or 8 + u * 2 + k, which names slot k of send_list[(r - d(u)) mod 16, u], never an empty slot. Column 13 holds the brick's own index within its range.
All inputs are finite; a program needn't handle non-finite values. No bound on the sum of `voxel_mask` on one device may be relied on, other than what follows from the above.
Results may differ from a plain program's by a relative error of at most 0.002.
Values may be sent and summed in bfloat16 or wider, within the bound.
No kernel may reach another device: no remote copies, remote signals or barrier semaphores. Data moves between devices by JAX's collectives and lax.ppermute only.
A program may use at most 64 MiB of HBM per device.

v0:
```python
import functools
import math

import jax
import jax.numpy as jnp
from jax import lax
from jax.experimental import pallas as pl
from jax.experimental.pallas import tpu as pltpu
from jax.sharding import PartitionSpec as P

F32 = jnp.float32
BF16 = jnp.bfloat16
RANGE_AXES = ("curve", "slab")
VMEM = pl.BlockSpec(memory_space=pltpu.VMEM)
SMEM = pl.BlockSpec(memory_space=pltpu.SMEM)
NT = (((1,), (1,)), ((), ()))
NN = (((1,), (0,)), ((), ()))
TN = (((0,), (0,)), ((), ()))

BLOCK = 192
DUMMY = 24


def iota(shape, axis):
    return lax.broadcasted_iota(jnp.int32, shape, axis)


def dot(a, b, dims):
    return lax.dot_general(a, b, dims, preferred_element_type=F32)


def col(jx, jy, jz):
    return 9 * (jx + 1) + 3 * (jy + 1) + (jz + 1)


def voxel_order():
    row = iota((512, 512), 0)
    return jnp.where(iota((512, 512), 1) == ((row & 63) << 3) + (row >> 6), 1.0, 0.0).astype(BF16)


def swap_blocks(parts):
    lane = iota((64, 128), 1)
    half = [[p[:, :128], p[:, 128:]] for p in parts]
    now = [[half[(h << 2) | (i & 3)][i >> 2] for h in range(2)] for i in range(8)]
    for bit, shift in ((1, 64), (0, 32)):
        low = (lane & shift) == 0
        for i in range(8):
            if i >> bit & 1:
                continue
            j = i | (1 << bit)
            for h in range(2):
                p, q = now[i][h], now[j][h]
                now[i][h] = jnp.where(low, p, pltpu.roll(q, shift, 1))
                now[j][h] = jnp.where(low, pltpu.roll(p, 128 - shift, 1), q)
    return [jnp.concatenate(n, axis=1) for n in now]


def to_rows(values, order):
    swapped = dot(order, values, NT)
    return swap_blocks([swapped[64 * z : 64 * z + 64] for z in range(8)])


def masked_values(values, mask):
    return (values.astype(F32) * mask.astype(F32)[:, None, :]).astype(BF16).reshape(256, 512)


def parity():
    return (lax.axis_index("curve") * lax.axis_size("slab") + lax.axis_index("slab")) & 1


def entry_of(kmap, b, j, flip):
    e = kmap[b, j]
    far = ((e - 8) ^ flip) + 8
    return jnp.where(e < 0, DUMMY, jnp.where(e < 8, e, far))


def pack_kernel(feat, mask, send, first, own, center, xf, yf, zf):
    bricks = to_rows(masked_values(feat[...], mask[...]), voxel_order())
    lane = iota((64, 128), 1)
    for b in range(8):
        c = bricks[b]
        for h in range(2):
            center[b, h] = c[:, 128 * h : 128 * h + 128]
        xf[b, 0:8] = c[0:8]
        xf[b, 8:16] = c[56:64]
        for h in range(2):
            s = slice(128 * h, 128 * h + 128)
            yf[b, 0:8, s] = center[b, h, pl.ds(0, 8, 8), :]
            yf[b, 8:16, s] = center[b, h, pl.ds(7, 8, 8), :]
        lo, hi = c[:, :128], c[:, 128:]
        even = jnp.where(lane < 64, pltpu.roll(hi, 32, 1), pltpu.roll(hi, 96, 1))
        odd = jnp.where(lane < 64, pltpu.roll(lo, 32, 1), pltpu.roll(lo, 96, 1))
        zf[b] = jnp.where((lane & 32) == 0, even, odd)
    flip = parity() * 4

    def put(out, at, u):
        pick = [jnp.maximum(send[0, u, k], 0) for k in range(2)]
        for k in range(2):
            xy = jnp.concatenate([xf[pick[k]], yf[pick[k]]], axis=0).astype(BF16)
            out[at, 64 * k : 64 * k + 32] = xy[:, :128]
            out[at, 64 * k + 32 : 64 * k + 64] = xy[:, 128:]
        out[at, 128:192] = jnp.where(lane < 64, zf[pick[0]], zf[pick[1]]).astype(BF16)

    for n in range(4):
        put(first, n, (4 + n) ^ flip)
    put(first, 4, flip)
    for n in range(3):
        put(own, n, (1 + n) ^ flip)


def sublane_masks(rows):
    y = iota((rows, 8, 128), 1)
    return y == 0, y == 7


def back_kernel(cot, mask, weights, kmap, wide, stack, stack_t, center, xg, yg, zg, first, own, gp, xa, ya, za):
    flip = parity() * 8
    bricks = to_rows(masked_values(cot[...], mask[...]), voxel_order())
    for b in range(8):
        c = bricks[b]
        for d in range(3):
            before, after = jnp.zeros((8 * d, 256), F32), jnp.zeros((16 - 8 * d, 256), F32)
            pieces = [p for p in (before, c, after) if p.shape[0]]
            stack[80 * b : 80 * b + 80, 256 * d : 256 * d + 256] = jnp.concatenate(pieces, axis=0).astype(BF16)
    for d in range(3):
        stack_t[256 * d : 256 * d + 256] = stack[:, 256 * d : 256 * d + 256].T

    tile = jnp.where((iota((32, 256), 1) & 31) == iota((32, 256), 0), 1.0, 0.0).astype(BF16)
    tiled = dot(weights[...].reshape(864, 32), tile, NN)
    block = iota((32, 256), 1) >> 5

    def tap(dx, dy, dz):
        t = col(dx - 1, dy - 1, dz - 1)
        return tiled[32 * t : 32 * t + 32]

    for dx in range(3):
        for z in range(8):
            rows = slice(256 * dx + 32 * z, 256 * dx + 32 * z + 32)
            for dy in range(3):
                w = jnp.zeros((32, 256), F32)
                for dz in range(3):
                    if 0 <= z + dz - 1 <= 7:
                        w = jnp.where(block == z + dz - 1, tap(dx, dy, dz), w)
                wide[rows, 256 * dy : 256 * dy + 256] = w.astype(BF16)
            w = jnp.zeros((32, 256), F32)
            if z in (0, 7):
                for dy in range(3):
                    w = jnp.where(block == 2 * dy + (z == 7), tap(dx, dy, 0 if z == 0 else 2), w)
            wide[rows, 768:1024] = w.astype(BF16)

    for n in range(4):
        s = slice(256 * n, 256 * n + 256)
        g = dot(stack[...], wide[:, s], NN)
        gp[2 * n] = g[:, :128]
        gp[2 * n + 1] = g[:, 128:]

    xa[...] = jnp.zeros_like(xa)
    ya[...] = jnp.zeros_like(ya)
    za[...] = jnp.zeros_like(za)
    low3 = iota((10, 8, 128), 2) < 32
    lane_low = iota((8, 128), 1) < 32
    y2 = iota((8, 128), 0)

    def brick(b, carry):
        base = pl.multiple_of(80 * b, 80)
        e = lambda *j: entry_of(kmap, b, col(*j), flip)
        y0, y7 = sublane_masks(10)
        for h in range(2):
            s = slice(128 * h, 128 * h + 128)

            def part(n):
                return gp[2 * n + h, pl.ds(base, 80)].reshape(10, 8, 128)

            below, above = part(0), part(2)
            r = (
                part(1)
                + jnp.where(y7, 0.0, pltpu.roll(below, 7, 1))
                + jnp.where(y0, 0.0, pltpu.roll(above, 1, 1))
            )
            center[b, h] = r[1:9].reshape(64, 128)
            xa[e(-1, 0, 0), 8:16, s] += r[0]
            xa[e(1, 0, 0), 0:8, s] += r[9]
            ya[e(0, -1, 0), 8:16, s] += gp[h, pl.ds(base + 8, 8, 8), :]
            ya[e(0, 1, 0), 0:8, s] += gp[4 + h, pl.ds(base + 15, 8, 8), :]
            xa[e(-1, -1, 0), 15:16, s] += below[0, 0:1]
            xa[e(1, -1, 0), 7:8, s] += below[9, 0:1]
            xa[e(-1, 1, 0), 8:9, s] += above[0, 7:8]
            xa[e(1, 1, 0), 0:1, s] += above[9, 7:8]
        a = gp[6, pl.ds(base, 80)].reshape(10, 8, 128)
        below = pltpu.roll(a, 7, 1)
        above = pltpu.roll(gp[7, pl.ds(base, 80)].reshape(10, 8, 128), 1, 1)
        r = pltpu.roll(a, 64, 2) + jnp.where(y7, 0.0, below) + jnp.where(y0, 0.0, above)
        below = jnp.where(y7, below, 0.0)
        above = jnp.where(y0, above, 0.0)
        for jy, v in ((0, r), (-1, below), (1, above)):
            for jz in (-1, 1):
                w = jnp.where(low3 if jz < 0 else ~low3, v, 0.0)
                za[e(0, jy, jz)] += w[1:9].reshape(64, 128)
                za[e(-1, jy, jz), 56:64] += w[0]
                za[e(1, jy, jz), 0:8] += w[9]
        return carry

    lax.fori_loop(0, 8, brick, 0)
    for i in range(8):
        xg[i] = xa[i]
        yg[i] = ya[i]
        zg[i] = za[i]

    lane = iota((64, 128), 1)

    def put(out, at, n):
        entry = 8 + 2 * (n ^ 4)
        for k in range(2):
            xy = jnp.concatenate([xa[entry + k], ya[entry + k]], axis=0).astype(BF16)
            out[at, 64 * k : 64 * k + 32] = xy[:, :128]
            out[at, 64 * k + 32 : 64 * k + 64] = xy[:, 128:]
        out[at, 128:192] = jnp.where(lane < 64, za[entry], pltpu.roll(za[entry + 1], 64, 1)).astype(BF16)

    for n in range(4):
        put(first, n, 4 + n)
    put(first, 4, 0)
    for n in range(3):
        put(own, n, 1 + n)


def received(first, near, far, last):
    return [(near, 2), (near, 0), (far, 1), (far, 0), (first, 4), (last, 1), (last, 0), (last, 2)]


def conv_kernel(
    center, xf, yf, zf, kmap, mask, wide, stack_t, first, near, far, last, conv, grad_w, xt, yt, zt, taps
):
    flip = parity() * 8
    for i in range(8):
        xt[i] = xf[i]
        yt[i] = yf[i]
        zt[i] = zf[i]
    xt[DUMMY] = jnp.zeros((16, 256), F32)
    yt[DUMMY] = jnp.zeros((16, 256), F32)
    zt[DUMMY] = jnp.zeros((64, 128), F32)
    lane = iota((64, 128), 1)
    for n, (ref, at) in enumerate(received(first, near, far, last)):
        for k in range(2):
            entry = 8 + 2 * n + k
            for h in range(2):
                xy = ref[at, 64 * k + 32 * h : 64 * k + 32 * h + 32].astype(F32)
                xt[entry, :, 128 * h : 128 * h + 128] = xy[:16]
                yt[entry, :, 128 * h : 128 * h + 128] = xy[16:]
        z = ref[at, 128:192].astype(F32)
        turned = pltpu.roll(z, 64, 1)
        zt[8 + 2 * n] = jnp.where(lane < 64, z, turned)
        zt[9 + 2 * n] = jnp.where(lane < 64, turned, z)

    low3 = (iota((8, 8, 128), 2) & 32) == 0
    low2 = (iota((8, 128), 1) & 32) == 0
    left3 = iota((10, 8, 128), 2) < 64

    def brick(b, carry):
        base = pl.multiple_of(80 * b, 16)
        e = lambda *j: entry_of(kmap, b, col(*j), flip)
        y0, y7 = sublane_masks(10)
        for h in range(2):
            s = slice(128 * h, 128 * h + 128)
            r = jnp.concatenate(
                [
                    xt[e(-1, 0, 0), 8:16, s].reshape(1, 8, 128),
                    center[b, h].reshape(8, 8, 128),
                    xt[e(1, 0, 0), 0:8, s].reshape(1, 8, 128),
                ],
                axis=0,
            )

            def edge(jy, y_rows, x_row):
                first_row = xt[e(-1, jy, 0), 8 + x_row : 9 + x_row, s]
                last_row = xt[e(1, jy, 0), x_row : x_row + 1, s]
                entry = e(0, jy, 0)
                middle = [yt[entry, y_rows + x : y_rows + x + 1, s] for x in range(8)]
                rows = [first_row] + middle + [last_row]
                return jnp.stack([jnp.broadcast_to(row, (8, 128)) for row in rows], axis=0)

            below = jnp.where(y0, edge(-1, 8, 7), pltpu.roll(r, 1, 1))
            above = jnp.where(y7, edge(1, 0, 0), pltpu.roll(r, 7, 1))
            for n, v in enumerate((below, r, above)):
                taps[pl.ds(base, 80), 256 * n + 128 * h : 256 * n + 128 * h + 128] = v.reshape(80, 128).astype(BF16)

        def halo(jy):
            lo, hi = e(0, jy, -1), e(0, jy, 1)
            middle = jnp.where(low3, zt[lo].reshape(8, 8, 128), zt[hi].reshape(8, 8, 128))
            start = jnp.where(low2, zt[e(-1, jy, -1), 56:64], zt[e(-1, jy, 1), 56:64])
            end = jnp.where(low2, zt[e(1, jy, -1), 0:8], zt[e(1, jy, 1), 0:8])
            return jnp.concatenate([start[None], middle, end[None]], axis=0)

        r = halo(0)
        below = pltpu.roll(jnp.where(y7, halo(-1), r), 1, 1)
        above = pltpu.roll(jnp.where(y0, halo(1), r), 7, 1)
        taps[pl.ds(base, 80), 768:896] = jnp.where(left3, below, r).reshape(80, 128).astype(BF16)
        taps[pl.ds(base, 80), 896:1024] = jnp.where(left3, above, 0.0).reshape(80, 128).astype(BF16)
        return carry

    lax.fori_loop(0, 8, brick, 0)

    tap_lane = iota((32, 128), 1)
    pieces = []
    for dx in range(3):
        full = dot(stack_t[256 * dx : 256 * dx + 256], taps[...], NN)
        for dy in range(3):
            total = jnp.zeros((32, 128), F32)
            for z in range(8):
                rows = full[32 * z : 32 * z + 32]
                lo = rows[:, 256 * dy : 256 * dy + 128]
                hi = rows[:, 256 * dy + 128 : 256 * dy + 256]
                edge_tile = rows[:, 768 + 128 * (dy // 2) : 896 + 128 * (dy // 2)]
                at = 64 * (dy % 2)
                if z == 0:
                    v = jnp.where(tap_lane < 32, pltpu.roll(edge_tile, (128 - at) % 128, 1), pltpu.roll(lo, 32, 1))
                elif z == 7:
                    v = jnp.where(tap_lane < 64, pltpu.roll(hi, 64, 1), pltpu.roll(edge_tile, (32 - at) % 128, 1))
                else:
                    q = 32 * (z - 1)
                    left, right = (lo, lo) if q < 64 else (lo, hi) if q < 128 else (hi, hi)
                    if left is right:
                        v = pltpu.roll(left, (256 - q) % 128, 1) if q % 128 else left
                    else:
                        v = jnp.where(
                            tap_lane < 128 - q,
                            pltpu.roll(left, 128 - q, 1),
                            pltpu.roll(right, 128 - q, 1),
                        )
                total = total + v
            pieces.append(jnp.where(tap_lane < 96, total, 0.0))
    tiles = [jnp.zeros((32, 128), F32) for _ in range(7)]
    for n, piece in enumerate(pieces):
        start = 96 * n
        at, tile = start % 128, start // 128
        turned = pltpu.roll(piece, at, 1) if at else piece
        if at + 96 <= 128:
            tiles[tile] = tiles[tile] + turned
        else:
            tiles[tile] = tiles[tile] + jnp.where(tap_lane >= at, turned, 0.0)
            tiles[tile + 1] = tiles[tile + 1] + jnp.where(tap_lane < at, turned, 0.0)
    for n in range(7):
        grad_w[:, 128 * n : 128 * n + 128] = tiles[n]

    pre = jnp.zeros((8, 8, 8, 256), F32)
    for dx in range(3):
        u = dot(taps[...], wide[256 * dx : 256 * dx + 256], NT).reshape(8, 10, 8, 256)
        pre = pre + u[:, dx : dx + 8]
    by_z = swap_blocks([pre[b].reshape(64, 256) for b in range(8)])
    stacked = jnp.concatenate([v.astype(BF16) for v in by_z], axis=0)
    out = dot(stacked.T, voxel_order(), NN).reshape(8, 32, 512)
    conv[...] = (out * mask[...].astype(F32)[:, None, :]).astype(BF16)


def fold_kernel(center, xg, yg, zg, mask, send, first, near, far, last, out, xa, ya, za):
    flip = parity() * 4
    xa[...] = xg[...]
    ya[...] = yg[...]
    za[...] = zg[...]
    for n, (ref, at) in enumerate(received(first, near, far, last)):
        u = n ^ 4 ^ flip
        z = ref[at, 128:192].astype(F32)
        for k in range(2):
            i = jnp.maximum(send[0, u, k], 0)
            for h in range(2):
                xy = ref[at, 64 * k + 32 * h : 64 * k + 32 * h + 32].astype(F32)
                xa[i, :, 128 * h : 128 * h + 128] += xy[:16]
                ya[i, :, 128 * h : 128 * h + 128] += xy[16:]
            za[i] += pltpu.roll(z, 64, 1) if k else z
    y0, y7 = sublane_masks(8)
    lane = iota((64, 128), 1)
    bricks = []
    for b in range(8):
        turned = pltpu.roll(za[b], 96, 1)
        halves = []
        for h in range(2):
            s = slice(128 * h, 128 * h + 128)
            c = center[b, h] + jnp.where(lane >= 96 if h else lane < 32, turned, 0.0)
            c = c.reshape(8, 8, 128)
            c = jnp.concatenate([c[0:1] + xa[b, 0:8, s][None], c[1:7], c[7:8] + xa[b, 8:16, s][None]], axis=0)
            low = jnp.stack([jnp.broadcast_to(ya[b, x : x + 1, s], (8, 128)) for x in range(8)], axis=0)
            high = jnp.stack([jnp.broadcast_to(ya[b, 8 + x : 9 + x, s], (8, 128)) for x in range(8)], axis=0)
            c = c + jnp.where(y0, low, 0.0) + jnp.where(y7, high, 0.0)
            halves.append(c.reshape(64, 128))
        bricks.append(jnp.concatenate(halves, axis=1))
    rows = jnp.concatenate(swap_blocks(bricks), axis=0).T
    coarse = rows.astype(BF16)
    fine = (rows - coarse.astype(F32)).astype(BF16)
    order = voxel_order()
    full = dot(coarse, order, NN) + dot(fine, order, NN)
    out[...] = full.reshape(8, 32, 512) * mask[...].astype(F32)[:, None, :]


def spread_kernel(scale, wide, out):
    for t in range(27):
        at, tile = 32 * t % 128, 32 * t // 128
        v = wide[:, 128 * tile : 128 * tile + 128]
        v = pltpu.roll(v, 128 - at, 1) if at else v
        out[t] = v[:, :32] * scale


def call(kernel, outs, scratch, ins, flops=0, size=0):
    return pl.pallas_call(
        kernel,
        out_shape=[jax.ShapeDtypeStruct(s, d) for s, d in outs],
        in_specs=ins,
        out_specs=[VMEM] * len(outs),
        scratch_shapes=[pltpu.VMEM(s, d) for s, d in scratch],
        compiler_params=pltpu.CompilerParams(vmem_limit_bytes=40 * 1024 * 1024),
        cost_estimate=pl.CostEstimate(flops=flops, bytes_accessed=size, transcendentals=0),
    )


def permute(value, target):
    count = lax.axis_size(RANGE_AXES)
    return lax.ppermute(value, RANGE_AXES, [(r, target(r, count)) for r in range(count)])


def swap(value, bit=1):
    return permute(value, lambda r, count: r ^ bit)


def onward(value, pairs):
    return permute(value, lambda r, count: (r + (-2 * pairs if r & 1 else 2 * pairs)) % count)


def exchange(first, own):
    first = swap(first)
    near = onward(jnp.concatenate([own[0:2], first[0:2]], axis=0), 1)
    far = onward(jnp.concatenate([own[2:3], first[2:4]], axis=0), 2)
    last = swap(jnp.concatenate([near[1:2], near[3:4], far[2:3]], axis=0))
    return first, near, far, last


def total_over_ranges(value):
    bit = 1
    while bit < lax.axis_size(RANGE_AXES):
        value = value + swap(value, bit)
        bit *= 2
    return value


def body(features, voxel_mask, weights, grad_out, send_list, kernel_map):
    block = lambda n: ((n, BLOCK, 128), BF16)
    faces = [((8, 16, 256), F32), ((8, 16, 256), F32), ((8, 64, 128), F32)]
    center_shape = ((8, 2, 64, 128), F32)

    first, own, center, xf, yf, zf = call(
        pack_kernel, [block(5), block(3), center_shape] + faces, [], [VMEM, VMEM, SMEM], 2 * 512 * 512 * 256, 1 << 21
    )(features, voxel_mask, send_list)
    got = exchange(first, own)

    accumulators = [((25, 16, 256), F32), ((25, 16, 256), F32), ((25, 64, 128), F32)]
    wide, stack, stack_t, grad_center, xg, yg, zg, grad_first, grad_own = call(
        back_kernel,
        [((768, 1024), BF16), ((640, 768), BF16), ((768, 640), BF16), center_shape] + faces + [block(5), block(3)],
        [((8, 640, 128), F32)] + accumulators,
        [VMEM, VMEM, VMEM, SMEM],
        2 * 640 * 768 * 1024,
        8 << 20,
    )(grad_out, voxel_mask, weights, kernel_map)
    grad_got = exchange(grad_first, grad_own)

    conv, grad_w = call(
        conv_kernel,
        [((8, 32, 512), BF16), ((32, 896), F32)],
        accumulators + [((640, 1024), BF16)],
        [VMEM] * 4 + [SMEM] + [VMEM] * 7,
        4 * 640 * 768 * 1024,
        8 << 20,
    )(center, xf, yf, zf, kernel_map, voxel_mask, wide, stack_t, *got)
    grad_w = total_over_ranges(grad_w)

    (grad_features,) = call(
        fold_kernel,
        [((8, 32, 512), F32)],
        faces,
        [VMEM] * 5 + [SMEM] + [VMEM] * 4,
        2 * 512 * 512 * 512,
        4 << 20,
    )(grad_center, xg, yg, zg, voxel_mask, send_list, *grad_got)

    brick_count, _, voxels = features.shape
    scale = 1.0 / math.sqrt(brick_count * lax.axis_size(RANGE_AXES) * voxels)
    (grad_weights,) = call(functools.partial(spread_kernel, scale), [((27, 32, 32), F32)], [], [VMEM])(grad_w)
    return conv, grad_features, grad_weights


def solution(mesh):
    bricks = ("scene", "curve", "slab")
    return jax.shard_map(
        body,
        mesh=mesh,
        in_specs=(
            P(bricks, None, None),
            P(bricks, None),
            P(),
            P(bricks, None, None),
            P(bricks, None, None),
            P(bricks, None),
        ),
        out_specs=(
            P(bricks, None, None),
            P(bricks, None, None),
            P("scene", None, None),
        ),
        check_vma=False,
    )
```

profile of v0, /device:TPU:0, one launch (start us, length us, event | category | flops | bytes accessed | tf_op | source)
XLA Modules:
  0.0 54.4 jit_solution(11443542024008245645)
XLA Ops:
  0.6 0.8 %copy.9.send = s32[1,8,2]{2,1,0:T(8,128)S(1)} copy(s32[1,8,2]{1,2,0:T(2,128)} %param.10) | data formatting | bytes 128 | tf_op args[4]
  1.4 0.7 %copy-done = s32[8,512]{1,0:T(8,128)S(1)} copy-done((s32[8,512]{1,0:T(8,128)S(1)}, s32[8,512]{1,0:T(8,128)}, u32[]{:S(2)}) %copy-start) | copy-done | bytes 16408
  2.1 0.9 %copy-done.2 = bf16[8,32,512]{2,1,0:T(8,128)(2,1)S(1)} copy-done((bf16[8,32,512]{2,1,0:T(8,128)(2,1)S(1)}, bf16[8,32,512]{2,1,0:T(8,128)(2,1)}, u32[]{:S(2)}) %copy-start.2) | copy-done | bytes 262168
  3.1 1.5 %shard_map.85 = (bf16[5,192,128]{2,1,0:T(8,128)(2,1)S(1)}, bf16[3,192,128]{2,1,0:T(8,128)(2,1)S(1)}, f32[8,2,64,128]{3,2,1,0:T(8,128)S(1)}, f32[8,16,256]{2,1,0:...) custom-call(bf16[8,32,512]{2,1,0:T(8,128)(2,1)S(1)} %copy-done.2, s32[8,512]{1,0:T(8,128)S(1)} %copy-done, ...), custom_call_target="tpu_custom_call" | custom-call | flops 134217728 | bytes 2097152 | tf_op jit(solution)/shard_map/pallas_call | solution.py:447
  4.5 0.5 collective-permute-start
  5.0 0.7 %copy-done.1 = s32[8,512]{1,0:T(8,128)S(1)} copy-done((s32[8,512]{1,0:T(8,128)S(1)}, s32[8,512]{1,0:T(8,128)}, u32[]{:S(2)}) %copy-start.1) | copy-done | bytes 16408
  5.8 0.9 %copy-done.3 = bf16[8,32,512]{2,1,0:T(8,128)(2,1)S(1)} copy-done((bf16[8,32,512]{2,1,0:T(8,128)(2,1)S(1)}, bf16[8,32,512]{2,1,0:T(8,128)(2,1)}, u32[]{:S(2)}) %copy-start.3) | copy-done | bytes 262168
  6.7 0.9 %copy-done.4 = bf16[27,32,32]{2,1,0:T(8,128)(2,1)S(1)} copy-done((bf16[27,32,32]{2,1,0:T(8,128)(2,1)S(1)}, bf16[27,32,32]{2,1,0:T(8,128)(2,1)}, u32[]{:S(2)}) %copy-start.4) | copy-done | bytes 55320
  7.6 0.7 %copy-done.5 = s32[8,27]{1,0:T(8,128)S(1)} copy-done((s32[8,27]{1,0:T(8,128)S(1)}, s32[8,27]{1,0:T(8,128)}, u32[]{:S(2)}) %copy-start.5) | copy-done | bytes 888
  8.3 5.0 %shard_map.86 = (bf16[768,1024]{1,0:T(8,128)(2,1)S(1)}, bf16[640,768]{1,0:T(8,128)(2,1)}, bf16[768,640]{1,0:T(8,128)(2,1)S(1)}, f32[8,2,64,128]{3,2,1,0:T(8,128)...) custom-call(bf16[8,32,512]{2,1,0:T(8,128)(2,1)S(1)} %copy-done.3, ...), custom_call_target="tpu_custom_call" | custom-call | flops 1006632960 | bytes 8388608 | tf_op jit(solution)/shard_map/pallas_call | solution.py:453
  13.4 0.1 collective-permute-start.4
  13.5 0.0 collective-permute-done.first
  13.6 3.0 %collective-permute-start.1 = (bf16[4,192,128]{2,1,0:T(8,128)(2,1)S(1)}, bf16[4,192,128]{2,1,0:T(8,128)(2,1)S(1)}, u32[]{:S(2)}, u32[]{:S(2)}) collective-permute-start(bf16[4,192,128]{2,1,0:T(8,128)(2,1)S(1)} %pad_maximum_fusion), channel_id=1, source_target_pairs={{0,2},{1,15},{2,4},{3,1},{4,6},{5,3},{6,8},{7,5},{8,10},{9,7},{10,... | collective-permute-start | bytes 589832 | tf_op jit(solution)/shard_map/ppermute | solution.py:415
  16.6 1.6 %collective-permute-start.2 = (bf16[3,192,128]{2,1,0:T(8,128)(2,1)S(1)}, bf16[3,192,128]{2,1,0:T(8,128)(2,1)S(1)}, u32[]{:S(2)}, u32[]{:S(2)}) collective-permute-start(bf16[3,192,128]{2,1,0:T(8,128)(2,1)S(1)} %pad_maximum_fusion.2), channel_id=1, source_target_pairs={{0,4},{1,13},{2,6},{3,15},{4,8},{5,1},{6,10},{7,3},{8,12},{9,5},{1... | collective-permute-start | bytes 442376 | tf_op jit(solution)/shard_map/ppermute | solution.py:415
  18.2 7.0 %collective-permute-done.2.far = bf16[3,192,128]{2,1,0:T(8,128)(2,1)S(1)} collective-permute-done((bf16[3,192,128]{2,1,0:T(8,128)(2,1)S(1)}, bf16[3,192,128]{2,1,0:T(8,128)(2,1)S(1)}, u32[]{:S(2)}, u32[]{:S(2)}) %collective-permute-start.2) | collective-permute-done | bytes 147488 | tf_op jit(solution)/shard_map/ppermute | solution.py:415
  25.2 0.0 collective-permute-done.1.near
  25.2 0.1 collective-permute-start.3
  25.4 1.6 %collective-permute-start.5 = (bf16[4,192,128]{2,1,0:T(8,128)(2,1)S(1)}, bf16[4,192,128]{2,1,0:T(8,128)(2,1)S(1)}, u32[]{:S(2)}, u32[]{:S(2)}) collective-permute-start(bf16[4,192,128]{2,1,0:T(8,128)(2,1)S(1)} %pad_maximum_fusion.1), channel_id=1, source_target_pairs={{0,2},{1,15},{2,4},{3,1},{4,6},{5,3},{6,8},{7,5},{8,10},{9,7},{10,... | collective-permute-start | bytes 589832 | tf_op jit(solution)/shard_map/ppermute | solution.py:415
  27.0 0.3 collective-permute-start.6
  27.3 5.6 %shard_map.87 = (bf16[8,32,512]{2,1,0:T(8,128)(2,1)}, f32[32,896]{1,0:T(8,128)S(1)}) custom-call(f32[8,2,64,128]{3,2,1,0:T(8,128)S(1)} %get-tuple-element.19.center, f32[8,16,256]{2,1,0:T(8,128)S(1)} %get-tuple-element.20.xf, f32[8,16,256]{2,1,0:T(8,128)S(1)} %get-tuple-element.21.yf, f32[8,64,128]{2,1,0:T(8,128)S(1)} %get-tuple-element.22.zf, ...), custom_call_target="tpu_custom_call" | custom-call | flops 2013265920 | bytes 8388608 | tf_op jit(solution)/shard_map/pallas_call | solution.py:463
  32.8 2.3 %collective-permute-start.8 = (f32[32,896]{1,0:T(8,128)S(1)}, f32[32,896]{1,0:T(8,128)S(1)}, u32[]{:S(2)}, u32[]{:S(2)}) collective-permute-start(f32[32,896]{1,0:T(8,128)S(1)} %get-tuple-element.34), channel_id=1, source_target_pairs={{0,1},{1,0},{2,3},{3,2},{4,5},{5,4},{6,7},{7,6},{8,9},{9,8},{10,11... | collective-permute-start | bytes 344072 | tf_op jit(solution)/shard_map/ppermute | solution.py:415
  35.1 0.5 collective-permute-done.6.far
  35.6 0.5 collective-permute-done.8
  36.1 1.8 %collective-permute-start.9 = (f32[32,896]{1,0:T(8,128)S(1)}, f32[32,896]{1,0:T(8,128)S(1)}, u32[]{:S(2)}, u32[]{:S(2)}) collective-permute-start(f32[32,896]{1,0:T(8,128)S(1)} %add.12), channel_id=1, source_target_pairs={{0,2},{1,3},{2,0},{3,1},{4,6},{5,7},{6,4},{7,5},{8,10},{9,11},{10,... | collective-permute-start | bytes 344072 | tf_op jit(solution)/shard_map/ppermute | solution.py:415
  37.9 3.7 %collective-permute-done.9 = f32[32,896]{1,0:T(8,128)S(1)} collective-permute-done((f32[32,896]{1,0:T(8,128)S(1)}, f32[32,896]{1,0:T(8,128)S(1)}, u32[]{:S(2)}, u32[]{:S(2)}) %collective-permute-start.9) | collective-permute-done | bytes 114720 | tf_op jit(solution)/shard_map/ppermute | solution.py:415
  41.6 1.2 %collective-permute-start.10 = (f32[32,896]{1,0:T(8,128)S(1)}, f32[32,896]{1,0:T(8,128)S(1)}, u32[]{:S(2)}, u32[]{:S(2)}) collective-permute-start(f32[32,896]{1,0:T(8,128)S(1)} %add.13), channel_id=1, source_target_pairs={{0,4},{1,5},{2,6},{3,7},{4,0},{5,1},{6,2},{7,3},{8,12},{9,13},{10,... | collective-permute-start | bytes 344072 | tf_op jit(solution)/shard_map/ppermute | solution.py:415
  42.8 0.1 collective-permute-start.7
  42.9 3.6 %collective-permute-done.10 = f32[32,896]{1,0:T(8,128)S(1)} collective-permute-done((f32[32,896]{1,0:T(8,128)S(1)}, f32[32,896]{1,0:T(8,128)S(1)}, u32[]{:S(2)}, u32[]{:S(2)}) %collective-permute-start.10) | collective-permute-done | bytes 114720 | tf_op jit(solution)/shard_map/ppermute | solution.py:415
  46.5 0.6 %collective-permute-start.11 = (f32[32,896]{1,0:T(8,128)S(1)}, f32[32,896]{1,0:T(8,128)S(1)}, u32[]{:S(2)}, u32[]{:S(2)}) collective-permute-start(f32[32,896]{1,0:T(8,128)S(1)} %add.14), channel_id=1, source_target_pairs={{0,8},{1,9},{2,10},{3,11},{4,12},{5,13},{6,14},{7,15},{8,0},{9,1},... | collective-permute-start | bytes 344072 | tf_op jit(solution)/shard_map/ppermute | solution.py:415
  47.1 2.6 %shard_map.88 = f32[8,32,512]{2,1,0:T(8,128)} custom-call(f32[8,2,64,128]{3,2,1,0:T(8,128)S(1)} %get-tuple-element.28.center, f32[8,16,256]{2,1,0:T(8,128)S(1)} %get-tuple-element.29.xg, f32[8,16,256]{2,1,0:T(8,128)S(1)} %get-tuple-element.30.yg, f32[8,64,128]{2,1,0:T(8,128)S(1)} %get-tuple-element.31.zg, s32[8,512]{1,0:T(8,128)S(1)} %copy-done.1, ...), custom_call_target="tpu_custom_call" | custom-call | flops 268435456 | bytes 4194304 | tf_op jit(solution)/shard_map/pallas_call | solution.py:473
  49.7 3.8 %collective-permute-done.11 = f32[32,896]{1,0:T(8,128)S(1)} collective-permute-done((f32[32,896]{1,0:T(8,128)S(1)}, f32[32,896]{1,0:T(8,128)S(1)}, u32[]{:S(2)}, u32[]{:S(2)}) %collective-permute-start.11) | collective-permute-done | bytes 114720 | tf_op jit(solution)/shard_map/ppermute | solution.py:415
  53.5 0.9 %shard_map.89 = f32[27,32,32]{2,1,0:T(8,128)} custom-call(f32[32,896]{1,0:T(8,128)S(1)} %add.15.wide), custom_call_target="tpu_custom_call" | custom-call | tf_op jit(solution)/shard_map/pallas_call | solution.py:484
  (32 shorter events, 0.3 us)
Async XLA Ops:
  1.4 0.7 %copy-start = (s32[8,512]{1,0:T(8,128)S(1)}, s32[8,512]{1,0:T(8,128)}, u32[]{:S(2)}) copy-start(s32[8,512]{1,0:T(8,128)} %mask.7) | copy-start | bytes 49156
  2.1 0.9 %copy-start.2 = (bf16[8,32,512]{2,1,0:T(8,128)(2,1)S(1)}, bf16[8,32,512]{2,1,0:T(8,128)(2,1)}, u32[]{:S(2)}) copy-start(bf16[8,32,512]{2,1,0:T(8,128)(2,1)} %feat.1) | copy-start | bytes 786436
  4.5 9.0 %collective-permute-start = (bf16[5,192,128]{2,1,0:T(8,128)(2,1)S(1)}, bf16[5,192,128]{2,1,0:T(8,128)(2,1)S(1)}, u32[]{:S(2)}, u32[]{:S(2)}) collective-permute-start(bf16[5,192,128]{2,1,0:T(8,128)(2,1)S(1)} %get-tuple-element.25), channel_id=1, source_target_pairs={{0,1},{1,0},{2,3},{3,2},{4,5},{5,4},{6,7},{7,6},{8,9},{9,8},{10,11... | collective-permute-start | bytes 737288 | tf_op jit(solution)/shard_map/ppermute | solution.py:415
  5.0 0.7 %copy-start.1 = (s32[8,512]{1,0:T(8,128)S(1)}, s32[8,512]{1,0:T(8,128)}, u32[]{:S(2)}) copy-start(s32[8,512]{1,0:T(8,128)} %mask.7) | copy-start | bytes 49156
  5.8 0.9 %copy-start.3 = (bf16[8,32,512]{2,1,0:T(8,128)(2,1)S(1)}, bf16[8,32,512]{2,1,0:T(8,128)(2,1)}, u32[]{:S(2)}) copy-start(bf16[8,32,512]{2,1,0:T(8,128)(2,1)} %cot.1) | copy-start | bytes 786436
  6.7 0.9 %copy-start.4 = (bf16[27,32,32]{2,1,0:T(8,128)(2,1)S(1)}, bf16[27,32,32]{2,1,0:T(8,128)(2,1)}, u32[]{:S(2)}) copy-start(bf16[27,32,32]{2,1,0:T(8,128)(2,1)} %weights.1) | copy-start | bytes 165892
  7.6 0.7 %copy-start.5 = (s32[8,27]{1,0:T(8,128)S(1)}, s32[8,27]{1,0:T(8,128)}, u32[]{:S(2)}) copy-start(s32[8,27]{1,0:T(8,128)} %kmap.3) | copy-start | bytes 2596
  13.4 4.8 %collective-permute-start.4 = (bf16[5,192,128]{2,1,0:T(8,128)(2,1)S(1)}, bf16[5,192,128]{2,1,0:T(8,128)(2,1)S(1)}, u32[]{:S(2)}, u32[]{:S(2)}) collective-permute-start(bf16[5,192,128]{2,1,0:T(8,128)(2,1)S(1)} %get-tuple-element.32), channel_id=1, source_target_pairs={{0,1},{1,0},{2,3},{3,2},{4,5},{5,4},{6,7},{7,6},{8,9},{9,8},{10,11... | collective-permute-start | bytes 737288 | tf_op jit(solution)/shard_map/ppermute | solution.py:415
  13.5 13.8 %copy-start.6 = (s32[8,27]{1,0:T(8,128)S(1)}, s32[8,27]{1,0:T(8,128)}, u32[]{:S(2)}) copy-start(s32[8,27]{1,0:T(8,128)} %kmap.3) | copy-start | bytes 2596
  13.6 11.6 %collective-permute-start.1 = (bf16[4,192,128]{2,1,0:T(8,128)(2,1)S(1)}, bf16[4,192,128]{2,1,0:T(8,128)(2,1)S(1)}, u32[]{:S(2)}, u32[]{:S(2)}) collective-permute-start(bf16[4,192,128]{2,1,0:T(8,128)(2,1)S(1)} %pad_maximum_fusion), channel_id=1, source_target_pairs={{0,2},{1,15},{2,4},{3,1},{4,6},{5,3},{6,8},{7,5},{8,10},{9,7},{10,... | collective-permute-start | bytes 589832 | tf_op jit(solution)/shard_map/ppermute | solution.py:415
  16.6 8.6 %collective-permute-start.2 = (bf16[3,192,128]{2,1,0:T(8,128)(2,1)S(1)}, bf16[3,192,128]{2,1,0:T(8,128)(2,1)S(1)}, u32[]{:S(2)}, u32[]{:S(2)}) collective-permute-start(bf16[3,192,128]{2,1,0:T(8,128)(2,1)S(1)} %pad_maximum_fusion.2), channel_id=1, source_target_pairs={{0,4},{1,13},{2,6},{3,15},{4,8},{5,1},{6,10},{7,3},{8,12},{9,5},{1... | collective-permute-start | bytes 442376 | tf_op jit(solution)/shard_map/ppermute | solution.py:415
  25.2 2.0 %collective-permute-start.3 = (bf16[3,192,128]{2,1,0:T(8,128)(2,1)S(1)}, bf16[3,192,128]{2,1,0:T(8,128)(2,1)S(1)}, u32[]{:S(2)}, u32[]{:S(2)}) collective-permute-start(bf16[3,192,128]{2,1,0:T(8,128)(2,1)S(1)} %pad_maximum_fusion.3), channel_id=1, source_target_pairs={{0,1},{1,0},{2,3},{3,2},{4,5},{5,4},{6,7},{7,6},{8,9},{9,8},{10,11... | collective-permute-start | bytes 442376 | tf_op jit(solution)/shard_map/ppermute | solution.py:415
  25.4 12.6 %collective-permute-start.5 = (bf16[4,192,128]{2,1,0:T(8,128)(2,1)S(1)}, bf16[4,192,128]{2,1,0:T(8,128)(2,1)S(1)}, u32[]{:S(2)}, u32[]{:S(2)}) collective-permute-start(bf16[4,192,128]{2,1,0:T(8,128)(2,1)S(1)} %pad_maximum_fusion.1), channel_id=1, source_target_pairs={{0,2},{1,15},{2,4},{3,1},{4,6},{5,3},{6,8},{7,5},{8,10},{9,7},{10,... | collective-permute-start | bytes 589832 | tf_op jit(solution)/shard_map/ppermute | solution.py:415
  27.0 8.6 %collective-permute-start.6 = (bf16[3,192,128]{2,1,0:T(8,128)(2,1)S(1)}, bf16[3,192,128]{2,1,0:T(8,128)(2,1)S(1)}, u32[]{:S(2)}, u32[]{:S(2)}) collective-permute-start(bf16[3,192,128]{2,1,0:T(8,128)(2,1)S(1)} %pad_maximum_fusion.4), channel_id=1, source_target_pairs={{0,4},{1,13},{2,6},{3,15},{4,8},{5,1},{6,10},{7,3},{8,12},{9,5},{1... | collective-permute-start | bytes 442376 | tf_op jit(solution)/shard_map/ppermute | solution.py:415
  32.8 3.3 %collective-permute-start.8 = (f32[32,896]{1,0:T(8,128)S(1)}, f32[32,896]{1,0:T(8,128)S(1)}, u32[]{:S(2)}, u32[]{:S(2)}) collective-permute-start(f32[32,896]{1,0:T(8,128)S(1)} %get-tuple-element.34), channel_id=1, source_target_pairs={{0,1},{1,0},{2,3},{3,2},{4,5},{5,4},{6,7},{7,6},{8,9},{9,8},{10,11... | collective-permute-start | bytes 344072 | tf_op jit(solution)/shard_map/ppermute | solution.py:415
  36.1 5.5 %collective-permute-start.9 = (f32[32,896]{1,0:T(8,128)S(1)}, f32[32,896]{1,0:T(8,128)S(1)}, u32[]{:S(2)}, u32[]{:S(2)}) collective-permute-start(f32[32,896]{1,0:T(8,128)S(1)} %add.12), channel_id=1, source_target_pairs={{0,2},{1,3},{2,0},{3,1},{4,6},{5,7},{6,4},{7,5},{8,10},{9,11},{10,... | collective-permute-start | bytes 344072 | tf_op jit(solution)/shard_map/ppermute | solution.py:415
  41.6 4.9 %collective-permute-start.10 = (f32[32,896]{1,0:T(8,128)S(1)}, f32[32,896]{1,0:T(8,128)S(1)}, u32[]{:S(2)}, u32[]{:S(2)}) collective-permute-start(f32[32,896]{1,0:T(8,128)S(1)} %add.13), channel_id=1, source_target_pairs={{0,4},{1,5},{2,6},{3,7},{4,0},{5,1},{6,2},{7,3},{8,12},{9,13},{10,... | collective-permute-start | bytes 344072 | tf_op jit(solution)/shard_map/ppermute | solution.py:415
  42.8 4.3 %collective-permute-start.7 = (bf16[3,192,128]{2,1,0:T(8,128)(2,1)S(1)}, bf16[3,192,128]{2,1,0:T(8,128)(2,1)S(1)}, u32[]{:S(2)}, u32[]{:S(2)}) collective-permute-start(bf16[3,192,128]{2,1,0:T(8,128)(2,1)S(1)} %pad_maximum_fusion.5), channel_id=1, source_target_pairs={{0,1},{1,0},{2,3},{3,2},{4,5},{5,4},{6,7},{7,6},{8,9},{9,8},{10,11... | collective-permute-start | bytes 442376 | tf_op jit(solution)/shard_map/ppermute | solution.py:415
  46.5 7.0 %collective-permute-start.11 = (f32[32,896]{1,0:T(8,128)S(1)}, f32[32,896]{1,0:T(8,128)S(1)}, u32[]{:S(2)}, u32[]{:S(2)}) collective-permute-start(f32[32,896]{1,0:T(8,128)S(1)} %add.14), channel_id=1, source_target_pairs={{0,8},{1,9},{2,10},{3,11},{4,12},{5,13},{6,14},{7,15},{8,0},{9,1},... | collective-permute-start | bytes 344072 | tf_op jit(solution)/shard_map/ppermute | solution.py:415
where the time goes:
time: 54.8 us; the launch traced here: 54.4 us
  waiting for transfers between devices  19 us (35%)
  Pallas kernels  15.6 us (28%)
  starting transfers between devices  13.1 us (24%)
  local copies, waits for them, and re-layouts  5.79 us (11%)
  between operations  0.77 us (1%)
    ppermute x12, waiting for transfers between devices, permute(): lax.ppermute(value, RANGE_AXES, [(r, target(r, count)) for r in range(cou...  19 us
    ppermute x12, starting transfers between devices, permute(): lax.ppermute(value, RANGE_AXES, [(r, target(r, count)) for r in range(cou...  13.1 us
    unnamed x15, local copies, waits for them, and re-layouts  5.71 us
    pallas_call x1, Pallas kernels, body(): call(conv_kernel, [((8, 32, 512), BF16), ((32, 896), F32)], accumulators...  5.55 us
    pallas_call x1, Pallas kernels, body(): call(back_kernel, [((768, 1024), BF16), ((640, 768), BF16), ((768, 640),...  5.04 us
    pallas_call x1, Pallas kernels, body(): call(fold_kernel, [((8, 32, 512), F32)], faces, [VMEM] * 5 + [SMEM] + [VM...  2.58 us
    pallas_call x1, Pallas kernels, body(): call(pack_kernel, [block(5), block(3), center_shape] + faces, [], [VMEM,...  1.46 us
  transfers between devices with their start and end apart: 12, of which 6 were waited for; matrix products, arithmetic and copies ran while one was open for 0% of the time, Pallas kernels for 24%

commit v1 on v0

--- a/solution.py
+++ b/solution.py
@@ -12,7 +12,7 @@
 BF16 = jnp.bfloat16
 RANGE_AXES = ("curve", "slab")
 VMEM = pl.BlockSpec(memory_space=pltpu.VMEM)
-SMEM = pl.BlockSpec(memory_space=pltpu.SMEM)
+HBM = pl.BlockSpec(memory_space=pltpu.HBM)
 NT = (((1,), (1,)), ((), ()))
 NN = (((1,), (0,)), ((), ()))
 TN = (((0,), (0,)), ((), ()))
@@ -68,14 +68,19 @@
     return (lax.axis_index("curve") * lax.axis_size("slab") + lax.axis_index("slab")) & 1
 
 
-def entry_of(kmap, b, j, flip):
-    e = kmap[b, j]
-    far = ((e - 8) ^ flip) + 8
-    return jnp.where(e < 0, DUMMY, jnp.where(e < 8, e, far))
-
-
-def pack_kernel(feat, mask, send, first, own, center, xf, yf, zf):
-    bricks = to_rows(masked_values(feat[...], mask[...]), voxel_order())
+def fetch(*pairs):
+    copies = [pltpu.make_async_copy(src, dst, sem) for src, dst, sem in pairs]
+    for c in copies:
+        c.start()
+    return copies
+
+
+def pack_kernel(feat_hbm, mask_hbm, send_hbm, first, own_near, own_far, center, xf, yf, zf, feat, mask, send, sems):
+    copies = fetch((feat_hbm, feat, sems.at[0]), (mask_hbm, mask, sems.at[1]), (send_hbm, send, sems.at[2]))
+    order = voxel_order()
+    for c in copies:
+        c.wait()
+    bricks = to_rows(masked_values(feat[...], mask[...]), order)
     lane = iota((64, 128), 1)
     for b in range(8):
         c = bricks[b]
@@ -94,7 +99,7 @@
     flip = parity() * 4
 
     def put(out, at, u):
-        pick = [jnp.maximum(send[0, u, k], 0) for k in range(2)]
+        pick = [jnp.maximum(send[k, u], 0) for k in range(2)]
         for k in range(2):
             xy = jnp.concatenate([xf[pick[k]], yf[pick[k]]], axis=0).astype(BF16)
             out[at, 64 * k : 64 * k + 32] = xy[:, :128]
@@ -104,8 +109,9 @@
     for n in range(4):
         put(first, n, (4 + n) ^ flip)
     put(first, 4, flip)
-    for n in range(3):
-        put(own, n, (1 + n) ^ flip)
+    for n in range(2):
+        put(own_near, n, (1 + n) ^ flip)
+    put(own_far, 0, 3 ^ flip)
 
 
 def sublane_masks(rows):
@@ -113,18 +119,19 @@
     return y == 0, y == 7
 
 
-def back_kernel(cot, mask, weights, kmap, wide, stack, stack_t, center, xg, yg, zg, first, own, gp, xa, ya, za):
-    flip = parity() * 8
-    bricks = to_rows(masked_values(cot[...], mask[...]), voxel_order())
-    for b in range(8):
-        c = bricks[b]
-        for d in range(3):
-            before, after = jnp.zeros((8 * d, 256), F32), jnp.zeros((16 - 8 * d, 256), F32)
-            pieces = [p for p in (before, c, after) if p.shape[0]]
-            stack[80 * b : 80 * b + 80, 256 * d : 256 * d + 256] = jnp.concatenate(pieces, axis=0).astype(BF16)
-    for d in range(3):
-        stack_t[256 * d : 256 * d + 256] = stack[:, 256 * d : 256 * d + 256].T
-
+def back_kernel(
+    cot_hbm, mask_hbm, weights_hbm, kmap_hbm,
+    wide, stack_t, center, xg, yg, zg, entries, first, own_near, own_far,
+    cot, mask, weights, kmap, stack, gp, xa, ya, za, table, sems,
+):
+    copies = fetch(
+        (weights_hbm, weights, sems.at[0]),
+        (kmap_hbm, kmap, sems.at[1]),
+        (cot_hbm, cot, sems.at[2]),
+        (mask_hbm, mask, sems.at[3]),
+    )
+    order = voxel_order()
+    copies[0].wait()
     tile = jnp.where((iota((32, 256), 1) & 31) == iota((32, 256), 0), 1.0, 0.0).astype(BF16)
     tiled = dot(weights[...].reshape(864, 32), tile, NN)
     block = iota((32, 256), 1) >> 5
@@ -148,6 +155,23 @@
                     w = jnp.where(block == 2 * dy + (z == 7), tap(dx, dy, 0 if z == 0 else 2), w)
             wide[rows, 768:1024] = w.astype(BF16)
 
+    copies[1].wait()
+    e = kmap[...]
+    entries[...] = jnp.where(e < 0, DUMMY, jnp.where(e < 8, e, ((e - 8) ^ (parity() * 8)) + 8))
+    to_table = fetch((entries, table, sems.at[1]))[0]
+
+    copies[2].wait()
+    copies[3].wait()
+    bricks = to_rows(masked_values(cot[...], mask[...]), order)
+    for b in range(8):
+        c = bricks[b]
+        for d in range(3):
+            before, after = jnp.zeros((8 * d, 256), F32), jnp.zeros((16 - 8 * d, 256), F32)
+            pieces = [p for p in (before, c, after) if p.shape[0]]
+            stack[80 * b : 80 * b + 80, 256 * d : 256 * d + 256] = jnp.concatenate(pieces, axis=0).astype(BF16)
+    for d in range(3):
+        stack_t[256 * d : 256 * d + 256] = stack[:, 256 * d : 256 * d + 256].T
+
     for n in range(4):
         s = slice(256 * n, 256 * n + 256)
         g = dot(stack[...], wide[:, s], NN)
@@ -157,13 +181,12 @@
     xa[...] = jnp.zeros_like(xa)
     ya[...] = jnp.zeros_like(ya)
     za[...] = jnp.zeros_like(za)
+    to_table.wait()
     low3 = iota((10, 8, 128), 2) < 32
-    lane_low = iota((8, 128), 1) < 32
-    y2 = iota((8, 128), 0)
 
     def brick(b, carry):
         base = pl.multiple_of(80 * b, 80)
-        e = lambda *j: entry_of(kmap, b, col(*j), flip)
+        e = lambda *j: table[b, col(*j)]
         y0, y7 = sublane_masks(10)
         for h in range(2):
             s = slice(128 * h, 128 * h + 128)
@@ -219,18 +242,19 @@
     for n in range(4):
         put(first, n, 4 + n)
     put(first, 4, 0)
-    for n in range(3):
-        put(own, n, 1 + n)
+    for n in range(2):
+        put(own_near, n, 1 + n)
+    put(own_far, 0, 3)
 
 
 def received(first, near, far, last):
-    return [(near, 2), (near, 0), (far, 1), (far, 0), (first, 4), (last, 1), (last, 0), (last, 2)]
-
-
-def conv_kernel(
-    center, xf, yf, zf, kmap, mask, wide, stack_t, first, near, far, last, conv, grad_w, xt, yt, zt, taps
+    return [(last, 1), (last, 0), (far, 1), (far, 0), (first, 4), (near, 3), (near, 1), (last, 2)]
+
+
+def taps_kernel(
+    center, xf, yf, zf, entries, stack_t, first, near, far, last, taps, keep, give, xt, yt, zt, table, sem
 ):
-    flip = parity() * 8
+    to_table = fetch((entries, table, sem.at[0]))[0]
     for i in range(8):
         xt[i] = xf[i]
         yt[i] = yf[i]
@@ -251,13 +275,14 @@
         zt[8 + 2 * n] = jnp.where(lane < 64, z, turned)
         zt[9 + 2 * n] = jnp.where(lane < 64, turned, z)
 
+    to_table.wait()
     low3 = (iota((8, 8, 128), 2) & 32) == 0
     low2 = (iota((8, 128), 1) & 32) == 0
     left3 = iota((10, 8, 128), 2) < 64
 
     def brick(b, carry):
         base = pl.multiple_of(80 * b, 16)
-        e = lambda *j: entry_of(kmap, b, col(*j), flip)
+        e = lambda *j: table[b, col(*j)]
         y0, y7 = sublane_masks(10)
         for h in range(2):
             s = slice(128 * h, 128 * h + 128)
@@ -301,8 +326,9 @@
 
     tap_lane = iota((32, 128), 1)
     pieces = []
+    product = dot(stack_t[...], taps[...], NN)
     for dx in range(3):
-        full = dot(stack_t[256 * dx : 256 * dx + 256], taps[...], NN)
+        full = product[256 * dx : 256 * dx + 256]
         for dy in range(3):
             total = jnp.zeros((32, 128), F32)
             for z in range(8):
@@ -338,9 +364,14 @@
         else:
             tiles[tile] = tiles[tile] + jnp.where(tap_lane >= at, turned, 0.0)
             tiles[tile + 1] = tiles[tile + 1] + jnp.where(tap_lane < at, turned, 0.0)
+    odd = parity() == 1
     for n in range(7):
-        grad_w[:, 128 * n : 128 * n + 128] = tiles[n]
-
+        top, bottom = tiles[n][:16], tiles[n][16:]
+        keep[:, 128 * n : 128 * n + 128] = jnp.where(odd, bottom, top)
+        give[:, 128 * n : 128 * n + 128] = jnp.where(odd, top, bottom)
+
+
+def conv_kernel(taps, wide, mask, conv):
     pre = jnp.zeros((8, 8, 8, 256), F32)
     for dx in range(3):
         u = dot(taps[...], wide[256 * dx : 256 * dx + 256], NT).reshape(8, 10, 8, 256)
@@ -351,16 +382,18 @@
     conv[...] = (out * mask[...].astype(F32)[:, None, :]).astype(BF16)
 
 
-def fold_kernel(center, xg, yg, zg, mask, send, first, near, far, last, out, xa, ya, za):
+def fold_kernel(center, xg, yg, zg, mask, send_hbm, first, near, far, last, out, xa, ya, za, send, sem):
+    to_send = fetch((send_hbm, send, sem.at[0]))[0]
     flip = parity() * 4
     xa[...] = xg[...]
     ya[...] = yg[...]
     za[...] = zg[...]
+    to_send.wait()
     for n, (ref, at) in enumerate(received(first, near, far, last)):
         u = n ^ 4 ^ flip
         z = ref[at, 128:192].astype(F32)
         for k in range(2):
-            i = jnp.maximum(send[0, u, k], 0)
+            i = jnp.maximum(send[k, u], 0)
             for h in range(2):
                 xy = ref[at, 64 * k + 32 * h : 64 * k + 32 * h + 32].astype(F32)
                 xa[i, :, 128 * h : 128 * h + 128] += xy[:16]
@@ -390,12 +423,15 @@
     out[...] = full.reshape(8, 32, 512) * mask[...].astype(F32)[:, None, :]
 
 
-def spread_kernel(scale, wide, out):
+def spread_kernel(scale, mine, other, out):
+    odd = parity() == 1
+    a, b = mine[...], other[...]
+    wide = jnp.concatenate([jnp.where(odd, b, a), jnp.where(odd, a, b)], axis=0) * scale
     for t in range(27):
         at, tile = 32 * t % 128, 32 * t // 128
         v = wide[:, 128 * tile : 128 * tile + 128]
         v = pltpu.roll(v, 128 - at, 1) if at else v
-        out[t] = v[:, :32] * scale
+        out[t] = v[:, :32]
 
 
 def call(kernel, outs, scratch, ins, flops=0, size=0):
@@ -404,7 +440,7 @@
         out_shape=[jax.ShapeDtypeStruct(s, d) for s, d in outs],
         in_specs=ins,
         out_specs=[VMEM] * len(outs),
-        scratch_shapes=[pltpu.VMEM(s, d) for s, d in scratch],
+        scratch_shapes=scratch,
         compiler_params=pltpu.CompilerParams(vmem_limit_bytes=40 * 1024 * 1024),
         cost_estimate=pl.CostEstimate(flops=flops, bytes_accessed=size, transcendentals=0),
     )
@@ -415,73 +451,102 @@
     return lax.ppermute(value, RANGE_AXES, [(r, target(r, count)) for r in range(count)])
 
 
+def in_hbm(value):
+    return pltpu.with_memory_space_constraint(value, pltpu.HBM)
+
+
 def swap(value, bit=1):
     return permute(value, lambda r, count: r ^ bit)
 
 
-def onward(value, pairs):
-    return permute(value, lambda r, count: (r + (-2 * pairs if r & 1 else 2 * pairs)) % count)
-
-
-def exchange(first, own):
-    first = swap(first)
-    near = onward(jnp.concatenate([own[0:2], first[0:2]], axis=0), 1)
-    far = onward(jnp.concatenate([own[2:3], first[2:4]], axis=0), 2)
-    last = swap(jnp.concatenate([near[1:2], near[3:4], far[2:3]], axis=0))
-    return first, near, far, last
-
-
-def total_over_ranges(value):
-    bit = 1
-    while bit < lax.axis_size(RANGE_AXES):
-        value = value + swap(value, bit)
-        bit *= 2
-    return value
+def onward(value, pairs, cross):
+    return permute(value, lambda r, count: ((r + (-2 * pairs if r & 1 else 2 * pairs)) % count) ^ cross)
+
+
+def exchange(first, near, far, later):
+    near = jnp.concatenate([near, first[0:2]], axis=0)
+    far = jnp.concatenate([far, first[2:4]], axis=0)
+    near, far, later = lax.optimization_barrier((near, far, later))
+    near = onward(near, 1, 1)
+    far = onward(far, 2, 0)
+    last = swap(jnp.concatenate([near[0:1], near[2:3], far[2:3]], axis=0))
+    return (first, near, far, last), later
 
 
 def body(features, voxel_mask, weights, grad_out, send_list, kernel_map):
     block = lambda n: ((n, BLOCK, 128), BF16)
-    faces = [((8, 16, 256), F32), ((8, 16, 256), F32), ((8, 64, 128), F32)]
+    vm = lambda *shape: pltpu.VMEM(shape, F32)
     center_shape = ((8, 2, 64, 128), F32)
-
-    first, own, center, xf, yf, zf = call(
-        pack_kernel, [block(5), block(3), center_shape] + faces, [], [VMEM, VMEM, SMEM], 2 * 512 * 512 * 256, 1 << 21
-    )(features, voxel_mask, send_list)
-    got = exchange(first, own)
-
-    accumulators = [((25, 16, 256), F32), ((25, 16, 256), F32), ((25, 64, 128), F32)]
-    wide, stack, stack_t, grad_center, xg, yg, zg, grad_first, grad_own = call(
+    face_shapes = [((8, 16, 256), F32), ((8, 16, 256), F32), ((8, 64, 128), F32)]
+    accumulators = [vm(25, 16, 256), vm(25, 16, 256), vm(25, 64, 128)]
+    values = [pltpu.VMEM((8, 32, 512), BF16), pltpu.VMEM((8, 512), jnp.int32)]
+    send_space = pltpu.SMEM((2, 8), jnp.int32)
+    table = pltpu.SMEM((8, 27), jnp.int32)
+    sems = lambda n: pltpu.SemaphoreType.DMA((n,))
+    send = in_hbm(send_list[0].T)
+
+    first, own_near, own_far, center, xf, yf, zf = call(
+        pack_kernel,
+        [block(5), block(2), block(1), center_shape] + face_shapes,
+        values + [send_space, sems(3)],
+        [HBM] * 3,
+        2 * 512 * 512 * 256,
+        1 << 21,
+    )(in_hbm(features), in_hbm(voxel_mask), send)
+    got, kernel_map = exchange(swap(first), own_near, own_far, kernel_map)
+
+    wide, stack_t, grad_center, xg, yg, zg, entries, grad_first, grad_near, grad_far = call(
         back_kernel,
-        [((768, 1024), BF16), ((640, 768), BF16), ((768, 640), BF16), center_shape] + faces + [block(5), block(3)],
-        [((8, 640, 128), F32)] + accumulators,
-        [VMEM, VMEM, VMEM, SMEM],
+        [((768, 1024), BF16), ((768, 640), BF16), center_shape]
+        + face_shapes
+        + [((8, 27), jnp.int32), block(5), block(2), block(1)],
+        values
+        + [pltpu.VMEM((27, 32, 32), BF16), pltpu.VMEM((8, 27), jnp.int32), pltpu.VMEM((640, 768), BF16), vm(8, 640, 128)]
+        + accumulators
+        + [table, sems(4)],
+        [HBM] * 4,
         2 * 640 * 768 * 1024,
         8 << 20,
-    )(grad_out, voxel_mask, weights, kernel_map)
-    grad_got = exchange(grad_first, grad_own)
-
-    conv, grad_w = call(
-        conv_kernel,
-        [((8, 32, 512), BF16), ((32, 896), F32)],
-        accumulators + [((640, 1024), BF16)],
-        [VMEM] * 4 + [SMEM] + [VMEM] * 7,
-        4 * 640 * 768 * 1024,
+    )(*(in_hbm(v) for v in (grad_out, voxel_mask, weights, kernel_map)))
+
+    taps, keep, give = call(
+        taps_kernel,
+        [((640, 1024), BF16), ((16, 896), F32), ((16, 896), F32)],
+        accumulators + [table, sems(1)],
+        [VMEM] * 10,
+        2 * 640 * 768 * 1024,
         8 << 20,
-    )(center, xf, yf, zf, kernel_map, voxel_mask, wide, stack_t, *got)
-    grad_w = total_over_ranges(grad_w)
-
+    )(center, xf, yf, zf, entries, stack_t, *got)
+
+    (conv,) = call(
+        conv_kernel, [((8, 32, 512), BF16)], [], [VMEM] * 3, 2 * 640 * 768 * 1024, 4 << 20
+    )(taps, wide, voxel_mask)
+
+    grad_got, _ = exchange(swap(grad_first), grad_near, grad_far, 0.0)
     (grad_features,) = call(
         fold_kernel,
         [((8, 32, 512), F32)],
-        faces,
-        [VMEM] * 5 + [SMEM] + [VMEM] * 4,
+        [vm(8, 16, 256), vm(8, 16, 256), vm(8, 64, 128), send_space, sems(1)],
+        [VMEM] * 5 + [HBM] + [VMEM] * 4,
         2 * 512 * 512 * 512,
         4 << 20,
-    )(grad_center, xg, yg, zg, voxel_mask, send_list, *grad_got)
+    )(grad_center, xg, yg, zg, voxel_mask, send, *grad_got)
+
+    part = keep + swap(give)
+    bit = 2
+    while bit < lax.axis_size(RANGE_AXES):
+        other = swap(part, bit)
+        if bit == 2:
+            other, conv = lax.optimization_barrier((other, conv))
+        if bit == 8:
+            other, grad_features = lax.optimization_barrier((other, grad_features))
+        part = part + other
+        bit *= 2
+    rest = swap(part)
 
     brick_count, _, voxels = features.shape
     scale = 1.0 / math.sqrt(brick_count * lax.axis_size(RANGE_AXES) * voxels)
-    (grad_weights,) = call(functools.partial(spread_kernel, scale), [((27, 32, 32), F32)], [], [VMEM])(grad_w)
+    (grad_weights,) = call(functools.partial(spread_kernel, scale), [((27, 32, 32), F32)], [], [VMEM] * 2)(part, rest)
     return conv, grad_features, grad_weights
 
 

time: 54.8 us -> 43.3 us (0.79)
  waiting for transfers between devices: 19 us -> 12.7 us
  local copies, waits for them, and re-layouts: 5.79 us -> 0.06 us
  starting transfers between devices: 13.1 us -> 14 us
    ppermute x12 -> x13, waiting for transfers between devices: 19 us -> 12.7 us  [permute(): lax.ppermute(value, RANGE_AXES, [(r, target(r, count)) for r in range(cou...]
    unnamed x15 -> x2, local copies, waits for them, and re-layouts: 5.71 us -> 0.01 us
    ppermute x12 -> x13, starting transfers between devices: 13.1 us -> 14 us  [permute(): lax.ppermute(value, RANGE_AXES, [(r, target(r, count)) for r in range(cou...]
    pallas_call x4 -> x5, Pallas kernels: 14.6 us -> 14.6 us  [the longest x1 4.77 us: body(): call(back_kernel, [((768, 1024), BF16), ((768, 640), BF16), center_shape]...]
  transfers between devices with their start and end apart: 12 -> 13, of which waited for: 6 -> 7; matrix products, arithmetic and copies ran while one was open for 0% -> 0% of each run, Pallas kernels for 24% -> 29%
where the time goes in v1:
time: 43.3 us; the launch traced here: 43.2 us
  Pallas kernels  15.5 us (36%)
  starting transfers between devices  14 us (32%)
  waiting for transfers between devices  12.7 us (29%)
  between operations  0.78 us (2%)
    ppermute x13, starting transfers between devices, permute(): lax.ppermute(value, RANGE_AXES, [(r, target(r, count)) for r in range(cou...  14 us
    ppermute x13, waiting for transfers between devices, permute(): lax.ppermute(value, RANGE_AXES, [(r, target(r, count)) for r in range(cou...  12.7 us
    pallas_call x1, Pallas kernels, body(): call(back_kernel, [((768, 1024), BF16), ((768, 640), BF16), center_shape]...  4.77 us
    pallas_call x1, Pallas kernels, body(): call(conv_kernel, [((8, 32, 512), BF16)], [], [VMEM] * 3, 2 * 640 * 768 *...  2.65 us
    pallas_call x1, Pallas kernels, body(): call(taps_kernel, [((640, 1024), BF16), ((16, 896), F32), ((16, 896), F32...  2.65 us
    pallas_call x1, Pallas kernels, body(): call(fold_kernel, [((8, 32, 512), F32)], [vm(8, 16, 256), vm(8, 16, 256),...  2.64 us
    pallas_call x1, Pallas kernels, body(): call(pack_kernel, [block(5), block(2), block(1), center_shape] + face_sha...  1.86 us
    pallas_call x1, Pallas kernels, body(): call(functools.partial(spread_kernel, scale), [((27, 32, 32), F32)], [],...  0.92 us
  transfers between devices with their start and end apart: 13, of which 7 were waited for; matrix products, arithmetic and copies ran while one was open for 0% of the time, Pallas kernels for 29%

profile of v1, /device:TPU:0, one launch (start us, length us, event | category | flops | bytes accessed | tf_op | source)
XLA Modules:
  0.0 43.2 jit_solution(13842493616660824196)
XLA Ops:
  0.6 1.9 %shard_map.85 = (bf16[5,192,128]{2,1,0:T(8,128)(2,1)S(1)}, bf16[2,192,128]{2,1,0:T(8,128)(2,1)S(1)}, bf16[1,192,128]{2,1,0:T(8,128)(2,1)S(1)}, f32[8,2,64,128]{3...) custom-call(bf16[8,32,512]{2,1,0:T(8,128)(2,1)} %feat_hbm.1, ...), custom_call_target="tpu_custom_call" | custom-call | flops 134217728 | bytes 2097152 | tf_op jit(solution)/shard_map/pallas_call | solution.py:488
  2.5 0.5 %collective-permute-start = (bf16[5,192,128]{2,1,0:T(8,128)(2,1)S(1)}, bf16[5,192,128]{2,1,0:T(8,128)(2,1)S(1)}, u32[]{:S(2)}, u32[]{:S(2)}) collective-permute-start(bf16[5,192,128]{2,1,0:T(8,128)(2,1)S(1)} %get-tuple-element.37), channel_id=1, source_target_pairs={{0,1},{1,0},{2,3},{3,2},{4,5},{5,4},{6,7},{7,6},{8,9},{9,8},{10,11... | collective-permute-start | bytes 737288 | tf_op jit(solution)/shard_map/ppermute | solution.py:451
  3.0 1.1 %collective-permute-done.first = bf16[5,192,128]{2,1,0:T(8,128)(2,1)S(1)} collective-permute-done((bf16[5,192,128]{2,1,0:T(8,128)(2,1)S(1)}, bf16[5,192,128]{2,1,0:T(8,128)(2,1)S(1)}, u32[]{:S(2)}, u32[]{:S(2)}) %collective-permute-start) | collective-permute-done | bytes 245792 | tf_op jit(solution)/shard_map/ppermute | solution.py:451
  4.2 2.7 %collective-permute-start.1 = (bf16[4,192,128]{2,1,0:T(8,128)(2,1)S(1)}, bf16[4,192,128]{2,1,0:T(8,128)(2,1)S(1)}, u32[]{:S(2)}, u32[]{:S(2)}) collective-permute-start(bf16[4,192,128]{2,1,0:T(8,128)(2,1)S(1)} %pad_maximum_fusion), channel_id=1, source_target_pairs={{0,3},{1,14},{2,5},{3,0},{4,7},{5,2},{6,9},{7,4},{8,11},{9,6},{10,... | collective-permute-start | bytes 589832 | tf_op jit(solution)/shard_map/ppermute | solution.py:451
  6.9 1.6 %collective-permute-start.2 = (bf16[3,192,128]{2,1,0:T(8,128)(2,1)S(1)}, bf16[3,192,128]{2,1,0:T(8,128)(2,1)S(1)}, u32[]{:S(2)}, u32[]{:S(2)}) collective-permute-start(bf16[3,192,128]{2,1,0:T(8,128)(2,1)S(1)} %pad_maximum_fusion.2), channel_id=1, source_target_pairs={{0,4},{1,13},{2,6},{3,15},{4,8},{5,1},{6,10},{7,3},{8,12},{9,5},{1... | collective-permute-start | bytes 442376 | tf_op jit(solution)/shard_map/ppermute | solution.py:451
  8.5 4.8 %shard_map.86 = (bf16[768,1024]{1,0:T(8,128)(2,1)S(1)}, bf16[768,640]{1,0:T(8,128)(2,1)S(1)}, f32[8,2,64,128]{3,2,1,0:T(8,128)S(1)}, f32[8,16,256]{2,1,0:T(8,128...) custom-call(bf16[8,32,512]{2,1,0:T(8,128)(2,1)} %cot_hbm.1, ...), custom_call_target="tpu_custom_call" | custom-call | flops 1006632960 | bytes 8388608 | tf_op jit(solution)/shard_map/pallas_call | solution.py:498
  13.3 2.0 %collective-permute-start.8 = (bf16[5,192,128]{2,1,0:T(8,128)(2,1)S(1)}, bf16[5,192,128]{2,1,0:T(8,128)(2,1)S(1)}, u32[]{:S(2)}, u32[]{:S(2)}) collective-permute-start(bf16[5,192,128]{2,1,0:T(8,128)(2,1)S(1)} %get-tuple-element.54), channel_id=1, source_target_pairs={{0,1},{1,0},{2,3},{3,2},{4,5},{5,4},{6,7},{7,6},{8,9},{9,8},{10,11... | collective-permute-start | bytes 737288 | tf_op jit(solution)/shard_map/ppermute | solution.py:451
  15.3 0.1 collective-permute-done.2.far
  15.4 0.0 collective-permute-done.1.near
  15.4 0.2 collective-permute-start.3
  15.7 0.8 %collective-permute-done.8.first = bf16[5,192,128]{2,1,0:T(8,128)(2,1)S(1)} collective-permute-done((bf16[5,192,128]{2,1,0:T(8,128)(2,1)S(1)}, bf16[5,192,128]{2,1,0:T(8,128)(2,1)S(1)}, u32[]{:S(2)}, u32[]{:S(2)}) %collective-permute-start.8) | collective-permute-done | bytes 245792 | tf_op jit(solution)/shard_map/ppermute | solution.py:451
  16.5 1.4 %collective-permute-start.9 = (bf16[4,192,128]{2,1,0:T(8,128)(2,1)S(1)}, bf16[4,192,128]{2,1,0:T(8,128)(2,1)S(1)}, u32[]{:S(2)}, u32[]{:S(2)}) collective-permute-start(bf16[4,192,128]{2,1,0:T(8,128)(2,1)S(1)} %pad_maximum_fusion.1), channel_id=1, source_target_pairs={{0,3},{1,14},{2,5},{3,0},{4,7},{5,2},{6,9},{7,4},{8,11},{9,6},{10,... | collective-permute-start | bytes 589832 | tf_op jit(solution)/shard_map/ppermute | solution.py:451
  17.9 0.3 collective-permute-start.10
  18.2 0.0 collective-permute-done.3.last
  18.2 2.6 %shard_map.87 = (bf16[640,1024]{1,0:T(8,128)(2,1)S(1)}, f32[16,896]{1,0:T(8,128)S(1)}, f32[16,896]{1,0:T(8,128)S(1)}) custom-call(f32[8,2,64,128]{3,2,1,0:T(8,128)S(1)} %get-tuple-element.32.center, f32[8,16,256]{2,1,0:T(8,128)S(1)} %get-tuple-element.33.xf, f32[8,16,256]{2,1,0:T(8,128)S(1)} %get-tuple-element.34.yf, ...), custom_call_target="tpu_custom_call" | custom-call | flops 1006632960 | bytes 8388608 | tf_op jit(solution)/shard_map/pallas_call | solution.py:512
  20.9 1.7 %collective-permute-start.4 = (f32[16,896]{1,0:T(8,128)S(1)}, f32[16,896]{1,0:T(8,128)S(1)}, u32[]{:S(2)}, u32[]{:S(2)}) collective-permute-start(f32[16,896]{1,0:T(8,128)S(1)} %get-tuple-element.45), channel_id=1, source_target_pairs={{0,1},{1,0},{2,3},{3,2},{4,5},{5,4},{6,7},{7,6},{8,9},{9,8},{10,11... | collective-permute-start | bytes 172040 | tf_op jit(solution)/shard_map/ppermute | solution.py:451
  22.6 3.7 %collective-permute-done.10.far = bf16[3,192,128]{2,1,0:T(8,128)(2,1)S(1)} collective-permute-done((bf16[3,192,128]{2,1,0:T(8,128)(2,1)S(1)}, bf16[3,192,128]{2,1,0:T(8,128)(2,1)S(1)}, u32[]{:S(2)}, u32[]{:S(2)}) %collective-permute-start.10) | collective-permute-done | bytes 147488 | tf_op jit(solution)/shard_map/ppermute | solution.py:451
  26.3 0.0 collective-permute-done.4
  26.3 1.8 %collective-permute-start.5 = (f32[16,896]{1,0:T(8,128)S(1)}, f32[16,896]{1,0:T(8,128)S(1)}, u32[]{:S(2)}, u32[]{:S(2)}) collective-permute-start(f32[16,896]{1,0:T(8,128)S(1)} %add.12), channel_id=1, source_target_pairs={{0,2},{1,3},{2,0},{3,1},{4,6},{5,7},{6,4},{7,5},{8,10},{9,11},{10,... | collective-permute-start | bytes 172040 | tf_op jit(solution)/shard_map/ppermute | solution.py:451
  28.1 0.0 collective-permute-done.9.near
  28.2 0.1 collective-permute-start.11
  28.3 2.7 %shard_map.88 = bf16[8,32,512]{2,1,0:T(8,128)(2,1)} custom-call(bf16[640,1024]{1,0:T(8,128)(2,1)S(1)} %get-tuple-element.46.taps, bf16[768,1024]{1,0:T(8,128)(2,1)S(1)} %get-tuple-element.47.wide, s32[8,512]{1,0:T(8,128)S(1)} %copy-done), custom_call_target="tpu_custom_call" | custom-call | flops 1006632960 | bytes 4194304 | tf_op jit(solution)/shard_map/pallas_call | solution.py:521
  30.9 0.0 collective-permute-done.5
  30.9 0.5 %collective-permute-start.6 = (f32[16,896]{1,0:T(8,128)S(1)}, f32[16,896]{1,0:T(8,128)S(1)}, u32[]{:S(2)}, u32[]{:S(2)}) collective-permute-start(f32[16,896]{1,0:T(8,128)S(1)} %add.13), channel_id=1, source_target_pairs={{0,4},{1,5},{2,6},{3,7},{4,0},{5,1},{6,2},{7,3},{8,12},{9,13},{10,... | collective-permute-start | bytes 172040 | tf_op jit(solution)/shard_map/ppermute | solution.py:451
  31.4 3.9 %collective-permute-done.6 = f32[16,896]{1,0:T(8,128)S(1)} collective-permute-done((f32[16,896]{1,0:T(8,128)S(1)}, f32[16,896]{1,0:T(8,128)S(1)}, u32[]{:S(2)}, u32[]{:S(2)}) %collective-permute-start.6) | collective-permute-done | bytes 57376 | tf_op jit(solution)/shard_map/ppermute | solution.py:451
  35.3 1.1 %collective-permute-start.7 = (f32[16,896]{1,0:T(8,128)S(1)}, f32[16,896]{1,0:T(8,128)S(1)}, u32[]{:S(2)}, u32[]{:S(2)}) collective-permute-start(f32[16,896]{1,0:T(8,128)S(1)} %add.14), channel_id=1, source_target_pairs={{0,8},{1,9},{2,10},{3,11},{4,12},{5,13},{6,14},{7,15},{8,0},{9,1},... | collective-permute-start | bytes 172040 | tf_op jit(solution)/shard_map/ppermute | solution.py:451
  36.4 0.0 collective-permute-done.11.last
  36.4 2.6 %shard_map.89 = f32[8,32,512]{2,1,0:T(8,128)} custom-call(f32[8,2,64,128]{3,2,1,0:T(8,128)S(1)} %get-tuple-element.50.center, f32[8,16,256]{2,1,0:T(8,128)S(1)} %get-tuple-element.51.xg, f32[8,16,256]{2,1,0:T(8,128)S(1)} %get-tuple-element.52.yg, f32[8,64,128]{2,1,0:T(8,128)S(1)} %get-tuple-element.53.zg, s32[8,512]{1,0:T(8,128)S(1)} %copy-done, ...), custom_call_target="tpu_custom_call" | custom-call | flops 268435456 | bytes 4194304 | tf_op jit(solution)/shard_map/pallas_call | solution.py:526
  39.0 1.9 %collective-permute-done.7 = f32[16,896]{1,0:T(8,128)S(1)} collective-permute-done((f32[16,896]{1,0:T(8,128)S(1)}, f32[16,896]{1,0:T(8,128)S(1)}, u32[]{:S(2)}, u32[]{:S(2)}) %collective-permute-start.7) | collective-permute-done | bytes 57376 | tf_op jit(solution)/shard_map/ppermute | solution.py:451
  40.9 0.1 collective-permute-start.12
  41.0 1.2 %collective-permute-done.12.other = f32[16,896]{1,0:T(8,128)S(1)} collective-permute-done((f32[16,896]{1,0:T(8,128)S(1)}, f32[16,896]{1,0:T(8,128)S(1)}, u32[]{:S(2)}, u32[]{:S(2)}) %collective-permute-start.12) | collective-permute-done | bytes 57376 | tf_op jit(solution)/shard_map/ppermute | solution.py:451
  42.2 0.9 %shard_map.90 = f32[27,32,32]{2,1,0:T(8,128)} custom-call(f32[16,896]{1,0:T(8,128)S(1)} %add.15.mine, f32[16,896]{1,0:T(8,128)S(1)} %collective-permute-done.12.other), custom_call_target="tpu_custom_call" | custom-call | tf_op jit(solution)/shard_map/pallas_call | solution.py:549
  (18 shorter events, 0.2 us)
Async XLA Ops:
  2.5 1.7 %collective-permute-start = (bf16[5,192,128]{2,1,0:T(8,128)(2,1)S(1)}, bf16[5,192,128]{2,1,0:T(8,128)(2,1)S(1)}, u32[]{:S(2)}, u32[]{:S(2)}) collective-permute-start(bf16[5,192,128]{2,1,0:T(8,128)(2,1)S(1)} %get-tuple-element.37), channel_id=1, source_target_pairs={{0,1},{1,0},{2,3},{3,2},{4,5},{5,4},{6,7},{7,6},{8,9},{9,8},{10,11... | collective-permute-start | bytes 737288 | tf_op jit(solution)/shard_map/ppermute | solution.py:451
  4.2 11.1 %collective-permute-start.1 = (bf16[4,192,128]{2,1,0:T(8,128)(2,1)S(1)}, bf16[4,192,128]{2,1,0:T(8,128)(2,1)S(1)}, u32[]{:S(2)}, u32[]{:S(2)}) collective-permute-start(bf16[4,192,128]{2,1,0:T(8,128)(2,1)S(1)} %pad_maximum_fusion), channel_id=1, source_target_pairs={{0,3},{1,14},{2,5},{3,0},{4,7},{5,2},{6,9},{7,4},{8,11},{9,6},{10,... | collective-permute-start | bytes 589832 | tf_op jit(solution)/shard_map/ppermute | solution.py:451
  6.9 8.5 %collective-permute-start.2 = (bf16[3,192,128]{2,1,0:T(8,128)(2,1)S(1)}, bf16[3,192,128]{2,1,0:T(8,128)(2,1)S(1)}, u32[]{:S(2)}, u32[]{:S(2)}) collective-permute-start(bf16[3,192,128]{2,1,0:T(8,128)(2,1)S(1)} %pad_maximum_fusion.2), channel_id=1, source_target_pairs={{0,4},{1,13},{2,6},{3,15},{4,8},{5,1},{6,10},{7,3},{8,12},{9,5},{1... | collective-permute-start | bytes 442376 | tf_op jit(solution)/shard_map/ppermute | solution.py:451
  13.3 3.2 %collective-permute-start.8 = (bf16[5,192,128]{2,1,0:T(8,128)(2,1)S(1)}, bf16[5,192,128]{2,1,0:T(8,128)(2,1)S(1)}, u32[]{:S(2)}, u32[]{:S(2)}) collective-permute-start(bf16[5,192,128]{2,1,0:T(8,128)(2,1)S(1)} %get-tuple-element.54), channel_id=1, source_target_pairs={{0,1},{1,0},{2,3},{3,2},{4,5},{5,4},{6,7},{7,6},{8,9},{9,8},{10,11... | collective-permute-start | bytes 737288 | tf_op jit(solution)/shard_map/ppermute | solution.py:451
  15.4 2.8 %collective-permute-start.3 = (bf16[3,192,128]{2,1,0:T(8,128)(2,1)S(1)}, bf16[3,192,128]{2,1,0:T(8,128)(2,1)S(1)}, u32[]{:S(2)}, u32[]{:S(2)}) collective-permute-start(bf16[3,192,128]{2,1,0:T(8,128)(2,1)S(1)} %pad_maximum_fusion.3), channel_id=1, source_target_pairs={{0,1},{1,0},{2,3},{3,2},{4,5},{5,4},{6,7},{7,6},{8,9},{9,8},{10,11... | collective-permute-start | bytes 442376 | tf_op jit(solution)/shard_map/ppermute | solution.py:451
  16.5 11.6 %collective-permute-start.9 = (bf16[4,192,128]{2,1,0:T(8,128)(2,1)S(1)}, bf16[4,192,128]{2,1,0:T(8,128)(2,1)S(1)}, u32[]{:S(2)}, u32[]{:S(2)}) collective-permute-start(bf16[4,192,128]{2,1,0:T(8,128)(2,1)S(1)} %pad_maximum_fusion.1), channel_id=1, source_target_pairs={{0,3},{1,14},{2,5},{3,0},{4,7},{5,2},{6,9},{7,4},{8,11},{9,6},{10,... | collective-permute-start | bytes 589832 | tf_op jit(solution)/shard_map/ppermute | solution.py:451
  17.9 8.3 %collective-permute-start.10 = (bf16[3,192,128]{2,1,0:T(8,128)(2,1)S(1)}, bf16[3,192,128]{2,1,0:T(8,128)(2,1)S(1)}, u32[]{:S(2)}, u32[]{:S(2)}) collective-permute-start(bf16[3,192,128]{2,1,0:T(8,128)(2,1)S(1)} %pad_maximum_fusion.4), channel_id=1, source_target_pairs={{0,4},{1,13},{2,6},{3,15},{4,8},{5,1},{6,10},{7,3},{8,12},{9,5},{1... | collective-permute-start | bytes 442376 | tf_op jit(solution)/shard_map/ppermute | solution.py:451
  18.2 10.1 %copy-start = (s32[8,512]{1,0:T(8,128)S(1)}, s32[8,512]{1,0:T(8,128)}, u32[]{:S(2)}) copy-start(s32[8,512]{1,0:T(8,128)} %mask.3) | copy-start | bytes 49156
  20.9 5.4 %collective-permute-start.4 = (f32[16,896]{1,0:T(8,128)S(1)}, f32[16,896]{1,0:T(8,128)S(1)}, u32[]{:S(2)}, u32[]{:S(2)}) collective-permute-start(f32[16,896]{1,0:T(8,128)S(1)} %get-tuple-element.45), channel_id=1, source_target_pairs={{0,1},{1,0},{2,3},{3,2},{4,5},{5,4},{6,7},{7,6},{8,9},{9,8},{10,11... | collective-permute-start | bytes 172040 | tf_op jit(solution)/shard_map/ppermute | solution.py:451
  26.3 4.6 %collective-permute-start.5 = (f32[16,896]{1,0:T(8,128)S(1)}, f32[16,896]{1,0:T(8,128)S(1)}, u32[]{:S(2)}, u32[]{:S(2)}) collective-permute-start(f32[16,896]{1,0:T(8,128)S(1)} %add.12), channel_id=1, source_target_pairs={{0,2},{1,3},{2,0},{3,1},{4,6},{5,7},{6,4},{7,5},{8,10},{9,11},{10,... | collective-permute-start | bytes 172040 | tf_op jit(solution)/shard_map/ppermute | solution.py:451
  28.2 8.2 %collective-permute-start.11 = (bf16[3,192,128]{2,1,0:T(8,128)(2,1)S(1)}, bf16[3,192,128]{2,1,0:T(8,128)(2,1)S(1)}, u32[]{:S(2)}, u32[]{:S(2)}) collective-permute-start(bf16[3,192,128]{2,1,0:T(8,128)(2,1)S(1)} %pad_maximum_fusion.5), channel_id=1, source_target_pairs={{0,1},{1,0},{2,3},{3,2},{4,5},{5,4},{6,7},{7,6},{8,9},{9,8},{10,11... | collective-permute-start | bytes 442376 | tf_op jit(solution)/shard_map/ppermute | solution.py:451
  30.9 4.4 %collective-permute-start.6 = (f32[16,896]{1,0:T(8,128)S(1)}, f32[16,896]{1,0:T(8,128)S(1)}, u32[]{:S(2)}, u32[]{:S(2)}) collective-permute-start(f32[16,896]{1,0:T(8,128)S(1)} %add.13), channel_id=1, source_target_pairs={{0,4},{1,5},{2,6},{3,7},{4,0},{5,1},{6,2},{7,3},{8,12},{9,13},{10,... | collective-permute-start | bytes 172040 | tf_op jit(solution)/shard_map/ppermute | solution.py:451
  35.3 5.6 %collective-permute-start.7 = (f32[16,896]{1,0:T(8,128)S(1)}, f32[16,896]{1,0:T(8,128)S(1)}, u32[]{:S(2)}, u32[]{:S(2)}) collective-permute-start(f32[16,896]{1,0:T(8,128)S(1)} %add.14), channel_id=1, source_target_pairs={{0,8},{1,9},{2,10},{3,11},{4,12},{5,13},{6,14},{7,15},{8,0},{9,1},... | collective-permute-start | bytes 172040 | tf_op jit(solution)/shard_map/ppermute | solution.py:451
  40.9 1.3 %collective-permute-start.12 = (f32[16,896]{1,0:T(8,128)S(1)}, f32[16,896]{1,0:T(8,128)S(1)}, u32[]{:S(2)}, u32[]{:S(2)}) collective-permute-start(f32[16,896]{1,0:T(8,128)S(1)} %add.15.mine), channel_id=1, source_target_pairs={{0,1},{1,0},{2,3},{3,2},{4,5},{5,4},{6,7},{7,6},{8,9},{9,8},{10,11... | collective-permute-start | bytes 172040 | tf_op jit(solution)/shard_map/ppermute | solution.py:451

commit v2 on v1

--- a/solution.py
+++ b/solution.py
@@ -120,18 +120,14 @@
 
 
 def back_kernel(
-    cot_hbm, mask_hbm, weights_hbm, kmap_hbm,
+    cot, mask, weights, kmap,
     wide, stack_t, center, xg, yg, zg, entries, first, own_near, own_far,
-    cot, mask, weights, kmap, stack, gp, xa, ya, za, table, sems,
+    stack, gp, xa, ya, za, table, sem,
 ):
-    copies = fetch(
-        (weights_hbm, weights, sems.at[0]),
-        (kmap_hbm, kmap, sems.at[1]),
-        (cot_hbm, cot, sems.at[2]),
-        (mask_hbm, mask, sems.at[3]),
-    )
+    e = kmap[...]
+    entries[...] = jnp.where(e < 0, DUMMY, jnp.where(e < 8, e, ((e - 8) ^ (parity() * 8)) + 8))
+    to_table = fetch((entries, table, sem.at[0]))[0]
     order = voxel_order()
-    copies[0].wait()
     tile = jnp.where((iota((32, 256), 1) & 31) == iota((32, 256), 0), 1.0, 0.0).astype(BF16)
     tiled = dot(weights[...].reshape(864, 32), tile, NN)
     block = iota((32, 256), 1) >> 5
@@ -155,13 +151,6 @@
                     w = jnp.where(block == 2 * dy + (z == 7), tap(dx, dy, 0 if z == 0 else 2), w)
             wide[rows, 768:1024] = w.astype(BF16)
 
-    copies[1].wait()
-    e = kmap[...]
-    entries[...] = jnp.where(e < 0, DUMMY, jnp.where(e < 8, e, ((e - 8) ^ (parity() * 8)) + 8))
-    to_table = fetch((entries, table, sems.at[1]))[0]
-
-    copies[2].wait()
-    copies[3].wait()
     bricks = to_rows(masked_values(cot[...], mask[...]), order)
     for b in range(8):
         c = bricks[b]
@@ -223,7 +212,7 @@
                 za[e(1, jy, jz), 0:8] += w[9]
         return carry
 
-    lax.fori_loop(0, 8, brick, 0)
+    lax.fori_loop(0, 8, brick, 0, unroll=2)
     for i in range(8):
         xg[i] = xa[i]
         yg[i] = ya[i]
@@ -322,7 +311,7 @@
         taps[pl.ds(base, 80), 896:1024] = jnp.where(left3, above, 0.0).reshape(80, 128).astype(BF16)
         return carry
 
-    lax.fori_loop(0, 8, brick, 0)
+    lax.fori_loop(0, 8, brick, 0, unroll=8)
 
     tap_lane = iota((32, 128), 1)
     pieces = []
@@ -467,10 +456,11 @@
     near = jnp.concatenate([near, first[0:2]], axis=0)
     far = jnp.concatenate([far, first[2:4]], axis=0)
     near, far, later = lax.optimization_barrier((near, far, later))
-    near = onward(near, 1, 1)
-    far = onward(far, 2, 0)
-    last = swap(jnp.concatenate([near[0:1], near[2:3], far[2:3]], axis=0))
-    return (first, near, far, last), later
+    return onward(near, 1, 1), onward(far, 2, 0), later
+
+
+def exchange_end(near, far):
+    return swap(jnp.concatenate([near[0:1], near[2:3], far[2:3]], axis=0))
 
 
 def body(features, voxel_mask, weights, grad_out, send_list, kernel_map):
@@ -493,51 +483,50 @@
         2 * 512 * 512 * 256,
         1 << 21,
     )(in_hbm(features), in_hbm(voxel_mask), send)
-    got, kernel_map = exchange(swap(first), own_near, own_far, kernel_map)
+    first = swap(first)
+    near, far, kernel_map = exchange(first, own_near, own_far, kernel_map)
+    last = exchange_end(near, far)
 
     wide, stack_t, grad_center, xg, yg, zg, entries, grad_first, grad_near, grad_far = call(
         back_kernel,
         [((768, 1024), BF16), ((768, 640), BF16), center_shape]
         + face_shapes
         + [((8, 27), jnp.int32), block(5), block(2), block(1)],
-        values
-        + [pltpu.VMEM((27, 32, 32), BF16), pltpu.VMEM((8, 27), jnp.int32), pltpu.VMEM((640, 768), BF16), vm(8, 640, 128)]
-        + accumulators
-        + [table, sems(4)],
-        [HBM] * 4,
+        [pltpu.VMEM((640, 768), BF16), vm(8, 640, 128)] + accumulators + [table, sems(1)],
+        [VMEM] * 4,
         2 * 640 * 768 * 1024,
         8 << 20,
-    )(*(in_hbm(v) for v in (grad_out, voxel_mask, weights, kernel_map)))
+    )(grad_out, voxel_mask, weights, kernel_map)
 
     taps, keep, give = call(
         taps_kernel,
         [((640, 1024), BF16), ((16, 896), F32), ((16, 896), F32)],
         accumulators + [table, sems(1)],
         [VMEM] * 10,
-        2 * 640 * 768 * 1024,
-        8 << 20,
-    )(center, xf, yf, zf, entries, stack_t, *got)
+    )(center, xf, yf, zf, entries, stack_t, first, near, far, last)
 
     (conv,) = call(
-        conv_kernel, [((8, 32, 512), BF16)], [], [VMEM] * 3, 2 * 640 * 768 * 1024, 4 << 20
+        conv_kernel, [((8, 32, 512), BF16)], [], [VMEM] * 3
     )(taps, wide, voxel_mask)
 
-    grad_got, _ = exchange(swap(grad_first), grad_near, grad_far, 0.0)
+    grad_first = swap(grad_first)
+    grad_near, grad_far, _ = exchange(grad_first, grad_near, grad_far, 0.0)
+
+    part = keep + swap(give)
+    other = swap(part, 2)
+    other, conv, grad_near, grad_far = lax.optimization_barrier((other, conv, grad_near, grad_far))
+    part = part + other
+    grad_last = exchange_end(grad_near, grad_far)
     (grad_features,) = call(
         fold_kernel,
         [((8, 32, 512), F32)],
         [vm(8, 16, 256), vm(8, 16, 256), vm(8, 64, 128), send_space, sems(1)],
         [VMEM] * 5 + [HBM] + [VMEM] * 4,
-        2 * 512 * 512 * 512,
-        4 << 20,
-    )(grad_center, xg, yg, zg, voxel_mask, send, *grad_got)
-
-    part = keep + swap(give)
-    bit = 2
+    )(grad_center, xg, yg, zg, voxel_mask, send, grad_first, grad_near, grad_far, grad_last)
+
+    bit = 4
     while bit < lax.axis_size(RANGE_AXES):
         other = swap(part, bit)
-        if bit == 2:
-            other, conv = lax.optimization_barrier((other, conv))
         if bit == 8:
             other, grad_features = lax.optimization_barrier((other, grad_features))
         part = part + other

time: 43.3 us -> 39.7 us (0.917)
  waiting for transfers between devices: 12.7 us -> 8.67 us
  starting transfers between devices: 14 us -> 15.4 us
  Pallas kernels: 15.5 us -> 14.5 us
    ppermute x13, waiting for transfers between devices: 12.7 us -> 8.67 us  [permute(): lax.ppermute(value, RANGE_AXES, [(r, target(r, count)) for r in range(cou...]
    ppermute x13, starting transfers between devices: 14 us -> 15.4 us  [permute(): lax.ppermute(value, RANGE_AXES, [(r, target(r, count)) for r in range(cou...]
    pallas_call x1, Pallas kernels: 4.77 us -> 3.99 us  [body(): call(back_kernel, [((768, 1024), BF16), ((768, 640), BF16), center_shape]...]
  transfers between devices with their start and end apart: 13 -> 13, of which waited for: 7 -> 6; matrix products, arithmetic and copies ran while one was open for 0% -> 0% of each run, Pallas kernels for 29% -> 29%
where the time goes in v2:
time: 39.7 us; the launch traced here: 39.5 us
  starting transfers between devices  15.4 us (39%)
  Pallas kernels  14.5 us (37%)
  waiting for transfers between devices  8.67 us (22%)
  between operations  0.81 us (2%)
    ppermute x13, starting transfers between devices, permute(): lax.ppermute(value, RANGE_AXES, [(r, target(r, count)) for r in range(cou...  15.4 us
    ppermute x13, waiting for transfers between devices, permute(): lax.ppermute(value, RANGE_AXES, [(r, target(r, count)) for r in range(cou...  8.67 us
    pallas_call x1, Pallas kernels, body(): call(back_kernel, [((768, 1024), BF16), ((768, 640), BF16), center_shape]...  3.99 us
    pallas_call x1, Pallas kernels, body(): call(conv_kernel, [((8, 32, 512), BF16)], [], [VMEM] * 3)  2.66 us
    pallas_call x1, Pallas kernels, body(): call(fold_kernel, [((8, 32, 512), F32)], [vm(8, 16, 256), vm(8, 16, 256),...  2.63 us
    pallas_call x1, Pallas kernels, body(): call(taps_kernel, [((640, 1024), BF16), ((16, 896), F32), ((16, 896), F32...  2.36 us
    pallas_call x1, Pallas kernels, body(): call(pack_kernel, [block(5), block(2), block(1), center_shape] + face_sha...  1.92 us
    pallas_call x1, Pallas kernels, body(): call(functools.partial(spread_kernel, scale), [((27, 32, 32), F32)], [],...  0.92 us
  transfers between devices with their start and end apart: 13, of which 6 were waited for; matrix products, arithmetic and copies ran while one was open for 0% of the time, Pallas kernels for 29%

profile of v2, /device:TPU:0, one launch (start us, length us, event | category | flops | bytes accessed | tf_op | source)
XLA Modules:
  0.0 39.5 jit_solution(8070852248738346341)
XLA Ops:
  0.7 1.9 %shard_map.85 = (bf16[5,192,128]{2,1,0:T(8,128)(2,1)S(1)}, bf16[2,192,128]{2,1,0:T(8,128)(2,1)S(1)}, bf16[1,192,128]{2,1,0:T(8,128)(2,1)S(1)}, f32[8,2,64,128]{3...) custom-call(bf16[8,32,512]{2,1,0:T(8,128)(2,1)} %feat_hbm.1, ...), custom_call_target="tpu_custom_call" | custom-call | flops 134217728 | bytes 2097152 | tf_op jit(solution)/shard_map/pallas_call | solution.py:478
  2.6 0.5 %collective-permute-start = (bf16[5,192,128]{2,1,0:T(8,128)(2,1)S(1)}, bf16[5,192,128]{2,1,0:T(8,128)(2,1)S(1)}, u32[]{:S(2)}, u32[]{:S(2)}) collective-permute-start(bf16[5,192,128]{2,1,0:T(8,128)(2,1)S(1)} %get-tuple-element.39), channel_id=1, source_target_pairs={{0,1},{1,0},{2,3},{3,2},{4,5},{5,4},{6,7},{7,6},{8,9},{9,8},{10,11... | collective-permute-start | bytes 737288 | tf_op jit(solution)/shard_map/ppermute | solution.py:440
  3.1 1.1 %collective-permute-done.first = bf16[5,192,128]{2,1,0:T(8,128)(2,1)S(1)} collective-permute-done((bf16[5,192,128]{2,1,0:T(8,128)(2,1)S(1)}, bf16[5,192,128]{2,1,0:T(8,128)(2,1)S(1)}, u32[]{:S(2)}, u32[]{:S(2)}) %collective-permute-start) | collective-permute-done | bytes 245792 | tf_op jit(solution)/shard_map/ppermute | solution.py:440
  4.3 2.7 %collective-permute-start.1 = (bf16[4,192,128]{2,1,0:T(8,128)(2,1)S(1)}, bf16[4,192,128]{2,1,0:T(8,128)(2,1)S(1)}, u32[]{:S(2)}, u32[]{:S(2)}) collective-permute-start(bf16[4,192,128]{2,1,0:T(8,128)(2,1)S(1)} %pad_maximum_fusion), channel_id=1, source_target_pairs={{0,3},{1,14},{2,5},{3,0},{4,7},{5,2},{6,9},{7,4},{8,11},{9,6},{10,... | collective-permute-start | bytes 589832 | tf_op jit(solution)/shard_map/ppermute | solution.py:440
  7.0 1.6 %collective-permute-start.2 = (bf16[3,192,128]{2,1,0:T(8,128)(2,1)S(1)}, bf16[3,192,128]{2,1,0:T(8,128)(2,1)S(1)}, u32[]{:S(2)}, u32[]{:S(2)}) collective-permute-start(bf16[3,192,128]{2,1,0:T(8,128)(2,1)S(1)} %pad_maximum_fusion.2), channel_id=1, source_target_pairs={{0,4},{1,13},{2,6},{3,15},{4,8},{5,1},{6,10},{7,3},{8,12},{9,5},{1... | collective-permute-start | bytes 442376 | tf_op jit(solution)/shard_map/ppermute | solution.py:440
  8.6 4.0 %shard_map.86 = (bf16[768,1024]{1,0:T(8,128)(2,1)S(1)}, bf16[768,640]{1,0:T(8,128)(2,1)S(1)}, f32[8,2,64,128]{3,2,1,0:T(8,128)S(1)}, f32[8,16,256]{2,1,0:T(8,128...) custom-call(bf16[8,32,512]{2,1,0:T(8,128)(2,1)S(1)} %copy-done.1, ...), custom_call_target="tpu_custom_call" | custom-call | flops 1006632960 | bytes 8388608 | tf_op jit(solution)/shard_map/pallas_call | solution.py:490
  12.6 2.1 %collective-permute-start.6 = (bf16[5,192,128]{2,1,0:T(8,128)(2,1)S(1)}, bf16[5,192,128]{2,1,0:T(8,128)(2,1)S(1)}, u32[]{:S(2)}, u32[]{:S(2)}) collective-permute-start(bf16[5,192,128]{2,1,0:T(8,128)(2,1)S(1)} %get-tuple-element.51), channel_id=1, source_target_pairs={{0,1},{1,0},{2,3},{3,2},{4,5},{5,4},{6,7},{7,6},{8,9},{9,8},{10,11... | collective-permute-start | bytes 737288 | tf_op jit(solution)/shard_map/ppermute | solution.py:440
  14.7 0.8 %collective-permute-done.2.far = bf16[3,192,128]{2,1,0:T(8,128)(2,1)S(1)} collective-permute-done((bf16[3,192,128]{2,1,0:T(8,128)(2,1)S(1)}, bf16[3,192,128]{2,1,0:T(8,128)(2,1)S(1)}, u32[]{:S(2)}, u32[]{:S(2)}) %collective-permute-start.2) | collective-permute-done | bytes 147488 | tf_op jit(solution)/shard_map/ppermute | solution.py:440
  15.5 0.0 collective-permute-done.1.near
  15.5 0.2 collective-permute-start.3
  15.8 0.0 collective-permute-done.6.first
  15.9 2.2 %collective-permute-start.7 = (bf16[4,192,128]{2,1,0:T(8,128)(2,1)S(1)}, bf16[4,192,128]{2,1,0:T(8,128)(2,1)S(1)}, u32[]{:S(2)}, u32[]{:S(2)}) collective-permute-start(bf16[4,192,128]{2,1,0:T(8,128)(2,1)S(1)} %pad_maximum_fusion.1), channel_id=1, source_target_pairs={{0,3},{1,14},{2,5},{3,0},{4,7},{5,2},{6,9},{7,4},{8,11},{9,6},{10,... | collective-permute-start | bytes 589832 | tf_op jit(solution)/shard_map/ppermute | solution.py:440
  18.0 0.0 collective-permute-start.8
  18.0 0.0 collective-permute-done.3.last
  18.0 2.4 %shard_map.87 = (bf16[640,1024]{1,0:T(8,128)(2,1)S(1)}, f32[16,896]{1,0:T(8,128)S(1)}, f32[16,896]{1,0:T(8,128)S(1)}) custom-call(f32[8,2,64,128]{3,2,1,0:T(8,128)S(1)} %get-tuple-element.34.center, f32[8,16,256]{2,1,0:T(8,128)S(1)} %get-tuple-element.35.xf, f32[8,16,256]{2,1,0:T(8,128)S(1)} %get-tuple-element.36.yf, ...), custom_call_target="tpu_custom_call" | custom-call | tf_op jit(solution)/shard_map/pallas_call | solution.py:501
  20.4 2.0 %collective-permute-start.4 = (f32[16,896]{1,0:T(8,128)S(1)}, f32[16,896]{1,0:T(8,128)S(1)}, u32[]{:S(2)}, u32[]{:S(2)}) collective-permute-start(f32[16,896]{1,0:T(8,128)S(1)} %get-tuple-element.47), channel_id=1, source_target_pairs={{0,1},{1,0},{2,3},{3,2},{4,5},{5,4},{6,7},{7,6},{8,9},{9,8},{10,11... | collective-permute-start | bytes 172040 | tf_op jit(solution)/shard_map/ppermute | solution.py:440
  22.4 0.9 %collective-permute-done.4 = f32[16,896]{1,0:T(8,128)S(1)} collective-permute-done((f32[16,896]{1,0:T(8,128)S(1)}, f32[16,896]{1,0:T(8,128)S(1)}, u32[]{:S(2)}, u32[]{:S(2)}) %collective-permute-start.4) | collective-permute-done | bytes 57376 | tf_op jit(solution)/shard_map/ppermute | solution.py:440
  23.3 1.6 %collective-permute-start.5 = (f32[16,896]{1,0:T(8,128)S(1)}, f32[16,896]{1,0:T(8,128)S(1)}, u32[]{:S(2)}, u32[]{:S(2)}) collective-permute-start(f32[16,896]{1,0:T(8,128)S(1)} %add.12), channel_id=1, source_target_pairs={{0,2},{1,3},{2,0},{3,1},{4,6},{5,7},{6,4},{7,5},{8,10},{9,11},{10,... | collective-permute-start | bytes 172040 | tf_op jit(solution)/shard_map/ppermute | solution.py:440
  24.9 2.7 %shard_map.88 = bf16[8,32,512]{2,1,0:T(8,128)(2,1)} custom-call(bf16[640,1024]{1,0:T(8,128)(2,1)S(1)} %get-tuple-element.48.taps, bf16[768,1024]{1,0:T(8,128)(2,1)S(1)} %get-tuple-element.49.wide, s32[8,512]{1,0:T(8,128)S(1)} %copy-done), custom_call_target="tpu_custom_call" | custom-call | tf_op jit(solution)/shard_map/pallas_call | solution.py:508
  27.6 0.0 collective-permute-done.8.far
  27.6 0.0 collective-permute-done.7.near
  27.6 0.0 collective-permute-done.5
  27.7 0.2 collective-permute-start.11
  27.9 1.2 %collective-permute-start.9 = (f32[16,896]{1,0:T(8,128)S(1)}, f32[16,896]{1,0:T(8,128)S(1)}, u32[]{:S(2)}, u32[]{:S(2)}) collective-permute-start(f32[16,896]{1,0:T(8,128)S(1)} %add.13), channel_id=1, source_target_pairs={{0,4},{1,5},{2,6},{3,7},{4,0},{5,1},{6,2},{7,3},{8,12},{9,13},{10,... | collective-permute-start | bytes 172040 | tf_op jit(solution)/shard_map/ppermute | solution.py:440
  29.1 3.1 %collective-permute-done.9 = f32[16,896]{1,0:T(8,128)S(1)} collective-permute-done((f32[16,896]{1,0:T(8,128)S(1)}, f32[16,896]{1,0:T(8,128)S(1)}, u32[]{:S(2)}, u32[]{:S(2)}) %collective-permute-start.9) | collective-permute-done | bytes 57376 | tf_op jit(solution)/shard_map/ppermute | solution.py:440
  32.2 1.1 %collective-permute-start.10 = (f32[16,896]{1,0:T(8,128)S(1)}, f32[16,896]{1,0:T(8,128)S(1)}, u32[]{:S(2)}, u32[]{:S(2)}) collective-permute-start(f32[16,896]{1,0:T(8,128)S(1)} %add.14), channel_id=1, source_target_pairs={{0,8},{1,9},{2,10},{3,11},{4,12},{5,13},{6,14},{7,15},{8,0},{9,1},... | collective-permute-start | bytes 172040 | tf_op jit(solution)/shard_map/ppermute | solution.py:440
  33.2 0.0 collective-permute-done.11.last
  33.2 2.6 %shard_map.89 = f32[8,32,512]{2,1,0:T(8,128)} custom-call(f32[8,2,64,128]{3,2,1,0:T(8,128)S(1)} %get-tuple-element.57.center, f32[8,16,256]{2,1,0:T(8,128)S(1)} %get-tuple-element.58.xg, f32[8,16,256]{2,1,0:T(8,128)S(1)} %get-tuple-element.59.yg, f32[8,64,128]{2,1,0:T(8,128)S(1)} %get-tuple-element.60.zg, s32[8,512]{1,0:T(8,128)S(1)} %copy-done, ...), custom_call_target="tpu_custom_call" | custom-call | tf_op jit(solution)/shard_map/pallas_call | solution.py:520
  35.8 1.5 %collective-permute-done.10 = f32[16,896]{1,0:T(8,128)S(1)} collective-permute-done((f32[16,896]{1,0:T(8,128)S(1)}, f32[16,896]{1,0:T(8,128)S(1)}, u32[]{:S(2)}, u32[]{:S(2)}) %collective-permute-start.10) | collective-permute-done | bytes 57376 | tf_op jit(solution)/shard_map/ppermute | solution.py:440
  37.3 0.1 collective-permute-start.12
  37.4 1.2 %collective-permute-done.12.other = f32[16,896]{1,0:T(8,128)S(1)} collective-permute-done((f32[16,896]{1,0:T(8,128)S(1)}, f32[16,896]{1,0:T(8,128)S(1)}, u32[]{:S(2)}, u32[]{:S(2)}) %collective-permute-start.12) | collective-permute-done | bytes 57376 | tf_op jit(solution)/shard_map/ppermute | solution.py:440
  38.6 0.9 %shard_map.90 = f32[27,32,32]{2,1,0:T(8,128)} custom-call(f32[16,896]{1,0:T(8,128)S(1)} %add.15.mine, f32[16,896]{1,0:T(8,128)S(1)} %collective-permute-done.12.other), custom_call_target="tpu_custom_call" | custom-call | tf_op jit(solution)/shard_map/pallas_call | solution.py:538
  (24 shorter events, 0.2 us)
Async XLA Ops:
  0.6 7.9 %copy-start = (s32[8,512]{1,0:T(8,128)S(1)}, s32[8,512]{1,0:T(8,128)}, u32[]{:S(2)}) copy-start(s32[8,512]{1,0:T(8,128)} %mask.5) | copy-start | bytes 49156
  0.6 7.9 %copy-start.3 = (s32[8,27]{1,0:T(8,128)S(1)}, s32[8,27]{1,0:T(8,128)}, u32[]{:S(2)}) copy-start(s32[8,27]{1,0:T(8,128)} %kmap) | copy-start | bytes 2596
  0.7 7.9 %copy-start.1 = (bf16[8,32,512]{2,1,0:T(8,128)(2,1)S(1)}, bf16[8,32,512]{2,1,0:T(8,128)(2,1)}, u32[]{:S(2)}) copy-start(bf16[8,32,512]{2,1,0:T(8,128)(2,1)} %cot.1) | copy-start | bytes 786436
  0.7 7.9 %copy-start.2 = (bf16[27,32,32]{2,1,0:T(8,128)(2,1)S(1)}, bf16[27,32,32]{2,1,0:T(8,128)(2,1)}, u32[]{:S(2)}) copy-start(bf16[27,32,32]{2,1,0:T(8,128)(2,1)} %weights.1) | copy-start | bytes 165892
  2.6 1.7 %collective-permute-start = (bf16[5,192,128]{2,1,0:T(8,128)(2,1)S(1)}, bf16[5,192,128]{2,1,0:T(8,128)(2,1)S(1)}, u32[]{:S(2)}, u32[]{:S(2)}) collective-permute-start(bf16[5,192,128]{2,1,0:T(8,128)(2,1)S(1)} %get-tuple-element.39), channel_id=1, source_target_pairs={{0,1},{1,0},{2,3},{3,2},{4,5},{5,4},{6,7},{7,6},{8,9},{9,8},{10,11... | collective-permute-start | bytes 737288 | tf_op jit(solution)/shard_map/ppermute | solution.py:440
  4.3 11.2 %collective-permute-start.1 = (bf16[4,192,128]{2,1,0:T(8,128)(2,1)S(1)}, bf16[4,192,128]{2,1,0:T(8,128)(2,1)S(1)}, u32[]{:S(2)}, u32[]{:S(2)}) collective-permute-start(bf16[4,192,128]{2,1,0:T(8,128)(2,1)S(1)} %pad_maximum_fusion), channel_id=1, source_target_pairs={{0,3},{1,14},{2,5},{3,0},{4,7},{5,2},{6,9},{7,4},{8,11},{9,6},{10,... | collective-permute-start | bytes 589832 | tf_op jit(solution)/shard_map/ppermute | solution.py:440
  7.0 8.5 %collective-permute-start.2 = (bf16[3,192,128]{2,1,0:T(8,128)(2,1)S(1)}, bf16[3,192,128]{2,1,0:T(8,128)(2,1)S(1)}, u32[]{:S(2)}, u32[]{:S(2)}) collective-permute-start(bf16[3,192,128]{2,1,0:T(8,128)(2,1)S(1)} %pad_maximum_fusion.2), channel_id=1, source_target_pairs={{0,4},{1,13},{2,6},{3,15},{4,8},{5,1},{6,10},{7,3},{8,12},{9,5},{1... | collective-permute-start | bytes 442376 | tf_op jit(solution)/shard_map/ppermute | solution.py:440
  12.6 3.2 %collective-permute-start.6 = (bf16[5,192,128]{2,1,0:T(8,128)(2,1)S(1)}, bf16[5,192,128]{2,1,0:T(8,128)(2,1)S(1)}, u32[]{:S(2)}, u32[]{:S(2)}) collective-permute-start(bf16[5,192,128]{2,1,0:T(8,128)(2,1)S(1)} %get-tuple-element.51), channel_id=1, source_target_pairs={{0,1},{1,0},{2,3},{3,2},{4,5},{5,4},{6,7},{7,6},{8,9},{9,8},{10,11... | collective-permute-start | bytes 737288 | tf_op jit(solution)/shard_map/ppermute | solution.py:440
  15.5 2.5 %collective-permute-start.3 = (bf16[3,192,128]{2,1,0:T(8,128)(2,1)S(1)}, bf16[3,192,128]{2,1,0:T(8,128)(2,1)S(1)}, u32[]{:S(2)}, u32[]{:S(2)}) collective-permute-start(bf16[3,192,128]{2,1,0:T(8,128)(2,1)S(1)} %pad_maximum_fusion.3), channel_id=1, source_target_pairs={{0,1},{1,0},{2,3},{3,2},{4,5},{5,4},{6,7},{7,6},{8,9},{9,8},{10,11... | collective-permute-start | bytes 442376 | tf_op jit(solution)/shard_map/ppermute | solution.py:440
  15.9 11.7 %collective-permute-start.7 = (bf16[4,192,128]{2,1,0:T(8,128)(2,1)S(1)}, bf16[4,192,128]{2,1,0:T(8,128)(2,1)S(1)}, u32[]{:S(2)}, u32[]{:S(2)}) collective-permute-start(bf16[4,192,128]{2,1,0:T(8,128)(2,1)S(1)} %pad_maximum_fusion.1), channel_id=1, source_target_pairs={{0,3},{1,14},{2,5},{3,0},{4,7},{5,2},{6,9},{7,4},{8,11},{9,6},{10,... | collective-permute-start | bytes 589832 | tf_op jit(solution)/shard_map/ppermute | solution.py:440
  18.0 9.6 %collective-permute-start.8 = (bf16[3,192,128]{2,1,0:T(8,128)(2,1)S(1)}, bf16[3,192,128]{2,1,0:T(8,128)(2,1)S(1)}, u32[]{:S(2)}, u32[]{:S(2)}) collective-permute-start(bf16[3,192,128]{2,1,0:T(8,128)(2,1)S(1)} %pad_maximum_fusion.4), channel_id=1, source_target_pairs={{0,4},{1,13},{2,6},{3,15},{4,8},{5,1},{6,10},{7,3},{8,12},{9,5},{1... | collective-permute-start | bytes 442376 | tf_op jit(solution)/shard_map/ppermute | solution.py:440
  20.4 2.9 %collective-permute-start.4 = (f32[16,896]{1,0:T(8,128)S(1)}, f32[16,896]{1,0:T(8,128)S(1)}, u32[]{:S(2)}, u32[]{:S(2)}) collective-permute-start(f32[16,896]{1,0:T(8,128)S(1)} %get-tuple-element.47), channel_id=1, source_target_pairs={{0,1},{1,0},{2,3},{3,2},{4,5},{5,4},{6,7},{7,6},{8,9},{9,8},{10,11... | collective-permute-start | bytes 172040 | tf_op jit(solution)/shard_map/ppermute | solution.py:440
  23.3 4.3 %collective-permute-start.5 = (f32[16,896]{1,0:T(8,128)S(1)}, f32[16,896]{1,0:T(8,128)S(1)}, u32[]{:S(2)}, u32[]{:S(2)}) collective-permute-start(f32[16,896]{1,0:T(8,128)S(1)} %add.12), channel_id=1, source_target_pairs={{0,2},{1,3},{2,0},{3,1},{4,6},{5,7},{6,4},{7,5},{8,10},{9,11},{10,... | collective-permute-start | bytes 172040 | tf_op jit(solution)/shard_map/ppermute | solution.py:440
  27.7 5.5 %collective-permute-start.11 = (bf16[3,192,128]{2,1,0:T(8,128)(2,1)S(1)}, bf16[3,192,128]{2,1,0:T(8,128)(2,1)S(1)}, u32[]{:S(2)}, u32[]{:S(2)}) collective-permute-start(bf16[3,192,128]{2,1,0:T(8,128)(2,1)S(1)} %pad_maximum_fusion.5), channel_id=1, source_target_pairs={{0,1},{1,0},{2,3},{3,2},{4,5},{5,4},{6,7},{7,6},{8,9},{9,8},{10,11... | collective-permute-start | bytes 442376 | tf_op jit(solution)/shard_map/ppermute | solution.py:440
  27.9 4.3 %collective-permute-start.9 = (f32[16,896]{1,0:T(8,128)S(1)}, f32[16,896]{1,0:T(8,128)S(1)}, u32[]{:S(2)}, u32[]{:S(2)}) collective-permute-start(f32[16,896]{1,0:T(8,128)S(1)} %add.13), channel_id=1, source_target_pairs={{0,4},{1,5},{2,6},{3,7},{4,0},{5,1},{6,2},{7,3},{8,12},{9,13},{10,... | collective-permute-start | bytes 172040 | tf_op jit(solution)/shard_map/ppermute | solution.py:440
  32.2 5.1 %collective-permute-start.10 = (f32[16,896]{1,0:T(8,128)S(1)}, f32[16,896]{1,0:T(8,128)S(1)}, u32[]{:S(2)}, u32[]{:S(2)}) collective-permute-start(f32[16,896]{1,0:T(8,128)S(1)} %add.14), channel_id=1, source_target_pairs={{0,8},{1,9},{2,10},{3,11},{4,12},{5,13},{6,14},{7,15},{8,0},{9,1},... | collective-permute-start | bytes 172040 | tf_op jit(solution)/shard_map/ppermute | solution.py:440
  37.3 1.3 %collective-permute-start.12 = (f32[16,896]{1,0:T(8,128)S(1)}, f32[16,896]{1,0:T(8,128)S(1)}, u32[]{:S(2)}, u32[]{:S(2)}) collective-permute-start(f32[16,896]{1,0:T(8,128)S(1)} %add.15.mine), channel_id=1, source_target_pairs={{0,1},{1,0},{2,3},{3,2},{4,5},{5,4},{6,7},{7,6},{8,9},{9,8},{10,11... | collective-permute-start | bytes 172040 | tf_op jit(solution)/shard_map/ppermute | solution.py:440

commit v3 on v2

--- a/solution.py
+++ b/solution.py
@@ -17,7 +17,7 @@
 NN = (((1,), (0,)), ((), ()))
 TN = (((0,), (0,)), ((), ()))
 
-BLOCK = 192
+BLOCK = 160
 DUMMY = 24
 
 
@@ -75,13 +75,46 @@
     return copies
 
 
-def pack_kernel(feat_hbm, mask_hbm, send_hbm, first, own_near, own_far, center, xf, yf, zf, feat, mask, send, sems):
+def z_planes(lo, hi):
+    lane = iota(lo.shape, 1)
+    even = jnp.where(lane < 64, pltpu.roll(hi, 32, 1), pltpu.roll(hi, 96, 1))
+    odd = jnp.where(lane < 64, pltpu.roll(lo, 32, 1), pltpu.roll(lo, 96, 1))
+    return jnp.where((lane & 32) == 0, even, odd)
+
+
+def half(h):
+    return slice(128 * h, 128 * h + 128)
+
+
+def put_block(out, at, x, y, z):
+    for k in range(2):
+        for h in range(2):
+            row = 32 * k + 16 * h
+            out[at, row : row + 16] = x[k][:, half(h)].astype(BF16)
+    pieces = [y[k][a : a + 6, half(h)] for k in range(2) for h in range(2) for a in (1, 9)]
+    out[at, 64:112] = jnp.concatenate(pieces, axis=0).astype(BF16)
+    out[at, 112:160] = z.astype(BF16)
+
+
+def get_block(ref, at):
+    x = [[ref[at, 32 * k + 16 * h : 32 * k + 16 * h + 16].astype(F32) for h in range(2)] for k in range(2)]
+    y = ref[at, 64:112].astype(F32)
+    y = [[[y[24 * k + 12 * h + 6 * a :][:6] for a in range(2)] for h in range(2)] for k in range(2)]
+    return x, y, ref[at, 112:160].astype(F32)
+
+
+def pack_kernel(
+    feat_hbm, mask_hbm, send_hbm, cot_hbm, weights_hbm, kmap_hbm,
+    first, own_near, own_far, center, xf, yf, zf, mask, cot, weights, kmap,
+    feat, send, sems,
+):
     copies = fetch((feat_hbm, feat, sems.at[0]), (mask_hbm, mask, sems.at[1]), (send_hbm, send, sems.at[2]))
+    later = fetch((cot_hbm, cot, sems.at[3]), (weights_hbm, weights, sems.at[4]), (kmap_hbm, kmap, sems.at[5]))
     order = voxel_order()
     for c in copies:
         c.wait()
     bricks = to_rows(masked_values(feat[...], mask[...]), order)
-    lane = iota((64, 128), 1)
+    lane = iota((48, 128), 1)
     for b in range(8):
         c = bricks[b]
         for h in range(2):
@@ -92,19 +125,13 @@
             s = slice(128 * h, 128 * h + 128)
             yf[b, 0:8, s] = center[b, h, pl.ds(0, 8, 8), :]
             yf[b, 8:16, s] = center[b, h, pl.ds(7, 8, 8), :]
-        lo, hi = c[:, :128], c[:, 128:]
-        even = jnp.where(lane < 64, pltpu.roll(hi, 32, 1), pltpu.roll(hi, 96, 1))
-        odd = jnp.where(lane < 64, pltpu.roll(lo, 32, 1), pltpu.roll(lo, 96, 1))
-        zf[b] = jnp.where((lane & 32) == 0, even, odd)
+        zf[b] = z_planes(c[:, :128], c[:, 128:])
     flip = parity() * 4
 
     def put(out, at, u):
         pick = [jnp.maximum(send[k, u], 0) for k in range(2)]
-        for k in range(2):
-            xy = jnp.concatenate([xf[pick[k]], yf[pick[k]]], axis=0).astype(BF16)
-            out[at, 64 * k : 64 * k + 32] = xy[:, :128]
-            out[at, 64 * k + 32 : 64 * k + 64] = xy[:, 128:]
-        out[at, 128:192] = jnp.where(lane < 64, zf[pick[0]], zf[pick[1]]).astype(BF16)
+        z = jnp.where(lane < 64, zf[pick[0], 8:56], zf[pick[1], 8:56])
+        put_block(out, at, [xf[p] for p in pick], [yf[p] for p in pick], z)
 
     for n in range(4):
         put(first, n, (4 + n) ^ flip)
@@ -112,6 +139,8 @@
     for n in range(2):
         put(own_near, n, (1 + n) ^ flip)
     put(own_far, 0, 3 ^ flip)
+    for c in later:
+        c.wait()
 
 
 def sublane_masks(rows):
@@ -121,7 +150,7 @@
 
 def back_kernel(
     cot, mask, weights, kmap,
-    wide, stack_t, center, xg, yg, zg, entries, first, own_near, own_far,
+    wide, keep_t, give_t, center, xg, yg, zg, entries, first, own_near, own_far,
     stack, gp, xa, ya, za, table, sem,
 ):
     e = kmap[...]
@@ -158,8 +187,12 @@
             before, after = jnp.zeros((8 * d, 256), F32), jnp.zeros((16 - 8 * d, 256), F32)
             pieces = [p for p in (before, c, after) if p.shape[0]]
             stack[80 * b : 80 * b + 80, 256 * d : 256 * d + 256] = jnp.concatenate(pieces, axis=0).astype(BF16)
+    odd = parity() == 1
     for d in range(3):
-        stack_t[256 * d : 256 * d + 256] = stack[:, 256 * d : 256 * d + 256].T
+        turned = stack[:, 256 * d : 256 * d + 256].T.reshape(8, 2, 16, 640)
+        top, bottom = turned[:, 0].reshape(128, 640), turned[:, 1].reshape(128, 640)
+        keep_t[128 * d : 128 * d + 128] = jnp.where(odd, bottom, top)
+        give_t[128 * d : 128 * d + 128] = jnp.where(odd, top, bottom)
 
     for n in range(4):
         s = slice(256 * n, 256 * n + 256)
@@ -218,15 +251,22 @@
         yg[i] = ya[i]
         zg[i] = za[i]
 
-    lane = iota((64, 128), 1)
+    lane = iota((48, 128), 1)
+    edge_lane = iota((16, 128), 1)
 
     def put(out, at, n):
         entry = 8 + 2 * (n ^ 4)
-        for k in range(2):
-            xy = jnp.concatenate([xa[entry + k], ya[entry + k]], axis=0).astype(BF16)
-            out[at, 64 * k : 64 * k + 32] = xy[:, :128]
-            out[at, 64 * k + 32 : 64 * k + 64] = xy[:, 128:]
-        out[at, 128:192] = jnp.where(lane < 64, za[entry], pltpu.roll(za[entry + 1], 64, 1)).astype(BF16)
+        x, y = [], []
+        for e in (entry, entry + 1):
+            for row, from_row in ((0, 0), (7, 8), (8, 7), (15, 15)):
+                xa[e, row : row + 1] += ya[e, from_row : from_row + 1]
+            z = pltpu.roll(jnp.concatenate([za[e, 0:8], za[e, 56:64]], axis=0), 96, 1)
+            lo = xa[e, :, :128] + jnp.where(edge_lane < 32, z, 0.0)
+            hi = xa[e, :, 128:] + jnp.where(edge_lane >= 96, z, 0.0)
+            x.append(jnp.concatenate([lo, hi], axis=1))
+            y.append(ya[e])
+        z = jnp.where(lane < 64, za[entry, 8:56], pltpu.roll(za[entry + 1, 8:56], 64, 1))
+        put_block(out, at, x, y, z)
 
     for n in range(4):
         put(first, n, 4 + n)
@@ -240,8 +280,44 @@
     return [(last, 1), (last, 0), (far, 1), (far, 0), (first, 4), (near, 3), (near, 1), (last, 2)]
 
 
+def band_product(half_t, taps):
+    product = dot(half_t, taps, NN)
+    lane = iota((16, 128), 1)
+    tiles = [jnp.zeros((16, 128), F32) for _ in range(7)]
+    for n in range(9):
+        dx, dy = n // 3, n % 3
+        total = jnp.zeros((16, 128), F32)
+        for z in range(8):
+            rows = product[128 * dx + 16 * z : 128 * dx + 16 * z + 16]
+            lo = rows[:, 256 * dy : 256 * dy + 128]
+            hi = rows[:, 256 * dy + 128 : 256 * dy + 256]
+            edge = rows[:, 768 + 128 * (dy // 2) : 896 + 128 * (dy // 2)]
+            at = 64 * (dy % 2)
+            if z == 0:
+                v = jnp.where(lane < 32, pltpu.roll(edge, (128 - at) % 128, 1), pltpu.roll(lo, 32, 1))
+            elif z == 7:
+                v = jnp.where(lane < 64, pltpu.roll(hi, 64, 1), pltpu.roll(edge, (32 - at) % 128, 1))
+            else:
+                q = 32 * (z - 1)
+                left, right = (lo, lo) if q < 64 else (lo, hi) if q < 128 else (hi, hi)
+                if left is right:
+                    v = pltpu.roll(left, (256 - q) % 128, 1) if q % 128 else left
+                else:
+                    v = jnp.where(lane < 128 - q, pltpu.roll(left, 128 - q, 1), pltpu.roll(right, 128 - q, 1))
+            total = total + v
+        piece = jnp.where(lane < 96, total, 0.0)
+        at, tile = 96 * n % 128, 96 * n // 128
+        turned = pltpu.roll(piece, at, 1) if at else piece
+        if at + 96 <= 128:
+            tiles[tile] = tiles[tile] + turned
+        else:
+            tiles[tile] = tiles[tile] + jnp.where(lane >= at, turned, 0.0)
+            tiles[tile + 1] = tiles[tile + 1] + jnp.where(lane < at, turned, 0.0)
+    return jnp.concatenate(tiles, axis=1)
+
+
 def taps_kernel(
-    center, xf, yf, zf, entries, stack_t, first, near, far, last, taps, keep, give, xt, yt, zt, table, sem
+    center, xf, yf, zf, entries, give_t, first, near, far, last, taps, give, xt, yt, zt, table, sem
 ):
     to_table = fetch((entries, table, sem.at[0]))[0]
     for i in range(8):
@@ -251,18 +327,24 @@
     xt[DUMMY] = jnp.zeros((16, 256), F32)
     yt[DUMMY] = jnp.zeros((16, 256), F32)
     zt[DUMMY] = jnp.zeros((64, 128), F32)
-    lane = iota((64, 128), 1)
+    lane = iota((48, 128), 1)
     for n, (ref, at) in enumerate(received(first, near, far, last)):
+        x, y, z = get_block(ref, at)
         for k in range(2):
             entry = 8 + 2 * n + k
             for h in range(2):
-                xy = ref[at, 64 * k + 32 * h : 64 * k + 32 * h + 32].astype(F32)
-                xt[entry, :, 128 * h : 128 * h + 128] = xy[:16]
-                yt[entry, :, 128 * h : 128 * h + 128] = xy[16:]
-        z = ref[at, 128:192].astype(F32)
+                plane = x[k][h]
+                xt[entry, :, half(h)] = plane
+                yt[entry, 1:7, half(h)] = y[k][h][0]
+                yt[entry, 9:15, half(h)] = y[k][h][1]
+                for row, from_row in ((0, 0), (8, 7), (7, 8), (15, 15)):
+                    yt[entry, row : row + 1, half(h)] = plane[from_row : from_row + 1]
+            edges = z_planes(x[k][0], x[k][1])
+            zt[entry, 0:8] = edges[0:8]
+            zt[entry, 56:64] = edges[8:16]
         turned = pltpu.roll(z, 64, 1)
-        zt[8 + 2 * n] = jnp.where(lane < 64, z, turned)
-        zt[9 + 2 * n] = jnp.where(lane < 64, turned, z)
+        zt[8 + 2 * n, 8:56] = jnp.where(lane < 64, z, turned)
+        zt[9 + 2 * n, 8:56] = jnp.where(lane < 64, turned, z)
 
     to_table.wait()
     low3 = (iota((8, 8, 128), 2) & 32) == 0
@@ -313,51 +395,11 @@
 
     lax.fori_loop(0, 8, brick, 0, unroll=8)
 
-    tap_lane = iota((32, 128), 1)
-    pieces = []
-    product = dot(stack_t[...], taps[...], NN)
-    for dx in range(3):
-        full = product[256 * dx : 256 * dx + 256]
-        for dy in range(3):
-            total = jnp.zeros((32, 128), F32)
-            for z in range(8):
-                rows = full[32 * z : 32 * z + 32]
-                lo = rows[:, 256 * dy : 256 * dy + 128]
-                hi = rows[:, 256 * dy + 128 : 256 * dy + 256]
-                edge_tile = rows[:, 768 + 128 * (dy // 2) : 896 + 128 * (dy // 2)]
-                at = 64 * (dy % 2)
-                if z == 0:
-                    v = jnp.where(tap_lane < 32, pltpu.roll(edge_tile, (128 - at) % 128, 1), pltpu.roll(lo, 32, 1))
-                elif z == 7:
-                    v = jnp.where(tap_lane < 64, pltpu.roll(hi, 64, 1), pltpu.roll(edge_tile, (32 - at) % 128, 1))
-                else:
-                    q = 32 * (z - 1)
-                    left, right = (lo, lo) if q < 64 else (lo, hi) if q < 128 else (hi, hi)
-                    if left is right:
-                        v = pltpu.roll(left, (256 - q) % 128, 1) if q % 128 else left
-                    else:
-                        v = jnp.where(
-                            tap_lane < 128 - q,
-                            pltpu.roll(left, 128 - q, 1),
-                            pltpu.roll(right, 128 - q, 1),
-                        )
-                total = total + v
-            pieces.append(jnp.where(tap_lane < 96, total, 0.0))
-    tiles = [jnp.zeros((32, 128), F32) for _ in range(7)]
-    for n, piece in enumerate(pieces):
-        start = 96 * n
-        at, tile = start % 128, start // 128
-        turned = pltpu.roll(piece, at, 1) if at else piece
-        if at + 96 <= 128:
-            tiles[tile] = tiles[tile] + turned
-        else:
-            tiles[tile] = tiles[tile] + jnp.where(tap_lane >= at, turned, 0.0)
-            tiles[tile + 1] = tiles[tile + 1] + jnp.where(tap_lane < at, turned, 0.0)
-    odd = parity() == 1
-    for n in range(7):
-        top, bottom = tiles[n][:16], tiles[n][16:]
-        keep[:, 128 * n : 128 * n + 128] = jnp.where(odd, bottom, top)
-        give[:, 128 * n : 128 * n + 128] = jnp.where(odd, top, bottom)
+    give[...] = band_product(give_t[...], taps[...])
+
+
+def keep_kernel(taps, keep_t, keep):
+    keep[...] = band_product(keep_t[...], taps[...])
 
 
 def conv_kernel(taps, wide, mask, conv):
@@ -380,14 +422,14 @@
     to_send.wait()
     for n, (ref, at) in enumerate(received(first, near, far, last)):
         u = n ^ 4 ^ flip
-        z = ref[at, 128:192].astype(F32)
+        x, y, z = get_block(ref, at)
         for k in range(2):
             i = jnp.maximum(send[k, u], 0)
             for h in range(2):
-                xy = ref[at, 64 * k + 32 * h : 64 * k + 32 * h + 32].astype(F32)
-                xa[i, :, 128 * h : 128 * h + 128] += xy[:16]
-                ya[i, :, 128 * h : 128 * h + 128] += xy[16:]
-            za[i] += pltpu.roll(z, 64, 1) if k else z
+                xa[i, :, half(h)] += x[k][h]
+                ya[i, 1:7, half(h)] += y[k][h][0]
+                ya[i, 9:15, half(h)] += y[k][h][1]
+            za[i, 8:56] += pltpu.roll(z, 64, 1) if k else z
     y0, y7 = sublane_masks(8)
     lane = iota((64, 128), 1)
     bricks = []
@@ -456,7 +498,8 @@
     near = jnp.concatenate([near, first[0:2]], axis=0)
     far = jnp.concatenate([far, first[2:4]], axis=0)
     near, far, later = lax.optimization_barrier((near, far, later))
-    return onward(near, 1, 1), onward(far, 2, 0), later
+    far = onward(far, 2, 0)
+    return onward(near, 1, 1), far, later
 
 
 def exchange_end(near, far):
@@ -469,49 +512,51 @@
     center_shape = ((8, 2, 64, 128), F32)
     face_shapes = [((8, 16, 256), F32), ((8, 16, 256), F32), ((8, 64, 128), F32)]
     accumulators = [vm(25, 16, 256), vm(25, 16, 256), vm(25, 64, 128)]
-    values = [pltpu.VMEM((8, 32, 512), BF16), pltpu.VMEM((8, 512), jnp.int32)]
     send_space = pltpu.SMEM((2, 8), jnp.int32)
     table = pltpu.SMEM((8, 27), jnp.int32)
     sems = lambda n: pltpu.SemaphoreType.DMA((n,))
     send = in_hbm(send_list[0].T)
 
-    first, own_near, own_far, center, xf, yf, zf = call(
+    first, own_near, own_far, center, xf, yf, zf, mask, cot, taps_w, kmap = call(
         pack_kernel,
-        [block(5), block(2), block(1), center_shape] + face_shapes,
-        values + [send_space, sems(3)],
-        [HBM] * 3,
+        [block(5), block(2), block(1), center_shape]
+        + face_shapes
+        + [((8, 512), jnp.int32), ((8, 32, 512), BF16), ((27, 32, 32), BF16), ((8, 27), jnp.int32)],
+        [pltpu.VMEM((8, 32, 512), BF16), send_space, sems(6)],
+        [HBM] * 6,
         2 * 512 * 512 * 256,
         1 << 21,
-    )(in_hbm(features), in_hbm(voxel_mask), send)
+    )(in_hbm(features), in_hbm(voxel_mask), send, in_hbm(grad_out), in_hbm(weights), in_hbm(kernel_map))
     first = swap(first)
-    near, far, kernel_map = exchange(first, own_near, own_far, kernel_map)
+    near, far, kmap = exchange(first, own_near, own_far, kmap)
     last = exchange_end(near, far)
 
-    wide, stack_t, grad_center, xg, yg, zg, entries, grad_first, grad_near, grad_far = call(
+    wide, keep_t, give_t, grad_center, xg, yg, zg, entries, grad_first, grad_near, grad_far = call(
         back_kernel,
-        [((768, 1024), BF16), ((768, 640), BF16), center_shape]
+        [((768, 1024), BF16), ((384, 640), BF16), ((384, 640), BF16), center_shape]
         + face_shapes
         + [((8, 27), jnp.int32), block(5), block(2), block(1)],
         [pltpu.VMEM((640, 768), BF16), vm(8, 640, 128)] + accumulators + [table, sems(1)],
         [VMEM] * 4,
         2 * 640 * 768 * 1024,
         8 << 20,
-    )(grad_out, voxel_mask, weights, kernel_map)
-
-    taps, keep, give = call(
+    )(cot, mask, taps_w, kmap)
+
+    taps, give = call(
         taps_kernel,
-        [((640, 1024), BF16), ((16, 896), F32), ((16, 896), F32)],
+        [((640, 1024), BF16), ((16, 896), F32)],
         accumulators + [table, sems(1)],
         [VMEM] * 10,
-    )(center, xf, yf, zf, entries, stack_t, first, near, far, last)
+    )(center, xf, yf, zf, entries, give_t, first, near, far, last)
 
     (conv,) = call(
         conv_kernel, [((8, 32, 512), BF16)], [], [VMEM] * 3
-    )(taps, wide, voxel_mask)
+    )(taps, wide, mask)
 
     grad_first = swap(grad_first)
     grad_near, grad_far, _ = exchange(grad_first, grad_near, grad_far, 0.0)
 
+    (keep,) = call(keep_kernel, [((16, 896), F32)], [], [VMEM] * 2)(taps, keep_t)
     part = keep + swap(give)
     other = swap(part, 2)
     other, conv, grad_near, grad_far = lax.optimization_barrier((other, conv, grad_near, grad_far))
@@ -522,7 +567,7 @@
         [((8, 32, 512), F32)],
         [vm(8, 16, 256), vm(8, 16, 256), vm(8, 64, 128), send_space, sems(1)],
         [VMEM] * 5 + [HBM] + [VMEM] * 4,
-    )(grad_center, xg, yg, zg, voxel_mask, send, grad_first, grad_near, grad_far, grad_last)
+    )(grad_center, xg, yg, zg, mask, send, grad_first, grad_near, grad_far, grad_last)
 
     bit = 4
     while bit < lax.axis_size(RANGE_AXES):

time: 39.7 us -> 38.2 us (0.962)
  waiting for transfers between devices: 8.67 us -> 7.43 us
  starting transfers between devices: 15.4 us -> 14.8 us
    ppermute x13, waiting for transfers between devices: 8.67 us -> 7.43 us  [permute(): lax.ppermute(value, RANGE_AXES, [(r, target(r, count)) for r in range(cou...]
    ppermute x13, starting transfers between devices: 15.4 us -> 14.8 us  [permute(): lax.ppermute(value, RANGE_AXES, [(r, target(r, count)) for r in range(cou...]
    pallas_call x3 -> x4, Pallas kernels: 9.02 us -> 9.37 us  [the longest x1 4.02 us: body(): call(back_kernel, [((768, 1024), BF16), ((384, 640), BF16), ((384, 640),...]
  transfers between devices with their start and end apart: 13 -> 13, of which waited for: 6 -> 6; matrix products, arithmetic and copies ran while one was open for 0% -> 0% of each run, Pallas kernels for 29% -> 32%
where the time goes in v3:
time: 38.2 us; the launch traced here: 38 us
  Pallas kernels  14.8 us (39%)
  starting transfers between devices  14.8 us (39%)
  waiting for transfers between devices  7.43 us (19%)
  between operations  0.78 us (2%)
    ppermute x13, starting transfers between devices, permute(): lax.ppermute(value, RANGE_AXES, [(r, target(r, count)) for r in range(cou...  14.8 us
    ppermute x13, waiting for transfers between devices, permute(): lax.ppermute(value, RANGE_AXES, [(r, target(r, count)) for r in range(cou...  7.43 us
    pallas_call x1, Pallas kernels, body(): call(back_kernel, [((768, 1024), BF16), ((384, 640), BF16), ((384, 640),...  4.02 us
    pallas_call x1, Pallas kernels, body(): call(conv_kernel, [((8, 32, 512), BF16)], [], [VMEM] * 3)(taps, wide, mask)  2.66 us
    pallas_call x1, Pallas kernels, body(): call(fold_kernel, [((8, 32, 512), F32)], [vm(8, 16, 256), vm(8, 16, 256),...  2.63 us
    pallas_call x1, Pallas kernels, body(): call(pack_kernel, [block(5), block(2), block(1), center_shape] + face_sha...  1.89 us
    pallas_call x1, Pallas kernels, body(): call(taps_kernel, [((640, 1024), BF16), ((16, 896), F32)], accumulators +...  1.76 us
    pallas_call x1, Pallas kernels, body(): keep, = call(keep_kernel, [((16, 896), F32)], [], [VMEM] * 2)(taps, keep_t)  0.93 us
  transfers between devices with their start and end apart: 13, of which 6 were waited for; matrix products, arithmetic and copies ran while one was open for 0% of the time, Pallas kernels for 32%

profile of v3, /device:TPU:0, one launch (start us, length us, event | category | flops | bytes accessed | tf_op | source)
XLA Modules:
  0.0 38.0 jit_solution(17082403181524406907)
XLA Ops:
  0.6 1.9 %shard_map.85 = (bf16[5,160,128]{2,1,0:T(8,128)(2,1)S(1)}, bf16[2,160,128]{2,1,0:T(8,128)(2,1)S(1)}, bf16[1,160,128]{2,1,0:T(8,128)(2,1)S(1)}, f32[8,2,64,128]{3...) custom-call(bf16[8,32,512]{2,1,0:T(8,128)(2,1)} %feat_hbm.1, ...), custom_call_target="tpu_custom_call" | custom-call | flops 134217728 | bytes 2097152 | tf_op jit(solution)/shard_map/pallas_call | solution.py:520
  2.5 0.5 %collective-permute-start = (bf16[5,160,128]{2,1,0:T(8,128)(2,1)S(1)}, bf16[5,160,128]{2,1,0:T(8,128)(2,1)S(1)}, u32[]{:S(2)}, u32[]{:S(2)}) collective-permute-start(bf16[5,160,128]{2,1,0:T(8,128)(2,1)S(1)} %get-tuple-element.46), channel_id=1, source_target_pairs={{0,1},{1,0},{2,3},{3,2},{4,5},{5,4},{6,7},{7,6},{8,9},{9,8},{10,11... | collective-permute-start | bytes 614408 | tf_op jit(solution)/shard_map/ppermute | solution.py:482
  3.1 1.1 %collective-permute-done.first = bf16[5,160,128]{2,1,0:T(8,128)(2,1)S(1)} collective-permute-done((bf16[5,160,128]{2,1,0:T(8,128)(2,1)S(1)}, bf16[5,160,128]{2,1,0:T(8,128)(2,1)S(1)}, u32[]{:S(2)}, u32[]{:S(2)}) %collective-permute-start) | collective-permute-done | bytes 204832 | tf_op jit(solution)/shard_map/ppermute | solution.py:482
  4.2 2.7 %collective-permute-start.1 = (bf16[4,160,128]{2,1,0:T(8,128)(2,1)S(1)}, bf16[4,160,128]{2,1,0:T(8,128)(2,1)S(1)}, u32[]{:S(2)}, u32[]{:S(2)}) collective-permute-start(bf16[4,160,128]{2,1,0:T(8,128)(2,1)S(1)} %pad_maximum_fusion), channel_id=1, source_target_pairs={{0,3},{1,14},{2,5},{3,0},{4,7},{5,2},{6,9},{7,4},{8,11},{9,6},{10,... | collective-permute-start | bytes 491528 | tf_op jit(solution)/shard_map/ppermute | solution.py:482
  6.9 1.6 %collective-permute-start.2 = (bf16[3,160,128]{2,1,0:T(8,128)(2,1)S(1)}, bf16[3,160,128]{2,1,0:T(8,128)(2,1)S(1)}, u32[]{:S(2)}, u32[]{:S(2)}) collective-permute-start(bf16[3,160,128]{2,1,0:T(8,128)(2,1)S(1)} %pad_maximum_fusion.2), channel_id=1, source_target_pairs={{0,4},{1,13},{2,6},{3,15},{4,8},{5,1},{6,10},{7,3},{8,12},{9,5},{1... | collective-permute-start | bytes 368648 | tf_op jit(solution)/shard_map/ppermute | solution.py:482
  8.4 4.0 %shard_map.86 = (bf16[768,1024]{1,0:T(8,128)(2,1)S(1)}, bf16[384,640]{1,0:T(8,128)(2,1)S(1)}, bf16[384,640]{1,0:T(8,128)(2,1)S(1)}, f32[8,2,64,128]{3,2,1,0:T(8,...) custom-call(bf16[8,32,512]{2,1,0:T(8,128)(2,1)S(1)} %get-tuple-eleme, ...), custom_call_target="tpu_custom_call" | custom-call | flops 1006632960 | bytes 8388608 | tf_op jit(solution)/shard_map/pallas_call | solution.py:534
  12.5 2.1 %collective-permute-start.6 = (bf16[5,160,128]{2,1,0:T(8,128)(2,1)S(1)}, bf16[5,160,128]{2,1,0:T(8,128)(2,1)S(1)}, u32[]{:S(2)}, u32[]{:S(2)}) collective-permute-start(bf16[5,160,128]{2,1,0:T(8,128)(2,1)S(1)} %get-tuple-element.59), channel_id=1, source_target_pairs={{0,1},{1,0},{2,3},{3,2},{4,5},{5,4},{6,7},{7,6},{8,9},{9,8},{10,11... | collective-permute-start | bytes 614408 | tf_op jit(solution)/shard_map/ppermute | solution.py:482
  14.5 0.3 collective-permute-done.2.far
  14.8 0.0 collective-permute-done.1.near
  14.9 0.2 collective-permute-start.3
  15.1 0.5 %collective-permute-done.6.first = bf16[5,160,128]{2,1,0:T(8,128)(2,1)S(1)} collective-permute-done((bf16[5,160,128]{2,1,0:T(8,128)(2,1)S(1)}, bf16[5,160,128]{2,1,0:T(8,128)(2,1)S(1)}, u32[]{:S(2)}, u32[]{:S(2)}) %collective-permute-start.6) | collective-permute-done | bytes 204832 | tf_op jit(solution)/shard_map/ppermute | solution.py:482
  15.7 1.3 %collective-permute-start.7 = (bf16[4,160,128]{2,1,0:T(8,128)(2,1)S(1)}, bf16[4,160,128]{2,1,0:T(8,128)(2,1)S(1)}, u32[]{:S(2)}, u32[]{:S(2)}) collective-permute-start(bf16[4,160,128]{2,1,0:T(8,128)(2,1)S(1)} %pad_maximum_fusion.1), channel_id=1, source_target_pairs={{0,3},{1,14},{2,5},{3,0},{4,7},{5,2},{6,9},{7,4},{8,11},{9,6},{10,... | collective-permute-start | bytes 491528 | tf_op jit(solution)/shard_map/ppermute | solution.py:482
  17.0 0.4 %collective-permute-start.8 = (bf16[3,160,128]{2,1,0:T(8,128)(2,1)S(1)}, bf16[3,160,128]{2,1,0:T(8,128)(2,1)S(1)}, u32[]{:S(2)}, u32[]{:S(2)}) collective-permute-start(bf16[3,160,128]{2,1,0:T(8,128)(2,1)S(1)} %pad_maximum_fusion.4), channel_id=1, source_target_pairs={{0,4},{1,13},{2,6},{3,15},{4,8},{5,1},{6,10},{7,3},{8,12},{9,5},{1... | collective-permute-start | bytes 368648 | tf_op jit(solution)/shard_map/ppermute | solution.py:482
  17.4 0.0 collective-permute-done.3.last
  17.4 1.8 %shard_map.87 = (bf16[640,1024]{1,0:T(8,128)(2,1)S(1)}, f32[16,896]{1,0:T(8,128)S(1)}) custom-call(f32[8,2,64,128]{3,2,1,0:T(8,128)S(1)} %get-tuple-element.38.center, f32[8,16,256]{2,1,0:T(8,128)S(1)} %get-tuple-element.39.xf, f32[8,16,256]{2,1,0:T(8,128)S(1)} %get-tuple-element.40.yf, f32[8,64,128]{2,1,0:T(8,128)S(1)} %get-tuple-element.41.zf, ...), custom_call_target="tpu_custom_call" | custom-call | tf_op jit(solution)/shard_map/pallas_call | solution.py:545
  19.2 1.6 %collective-permute-start.4 = (f32[16,896]{1,0:T(8,128)S(1)}, f32[16,896]{1,0:T(8,128)S(1)}, u32[]{:S(2)}, u32[]{:S(2)}) collective-permute-start(f32[16,896]{1,0:T(8,128)S(1)} %get-tuple-element.56), channel_id=1, source_target_pairs={{0,1},{1,0},{2,3},{3,2},{4,5},{5,4},{6,7},{7,6},{8,9},{9,8},{10,11... | collective-permute-start | bytes 172040 | tf_op jit(solution)/shard_map/ppermute | solution.py:482
  20.8 0.9 %shard_map.88 = f32[16,896]{1,0:T(8,128)S(1)} custom-call(bf16[640,1024]{1,0:T(8,128)(2,1)S(1)} %get-tuple-element.54.taps, bf16[384,640]{1,0:T(8,128)(2,1)S(1)} %get-tuple-element.55.keep_t), custom_call_target="tpu_custom_call" | custom-call | tf_op jit(solution)/shard_map/pallas_call | solution.py:559
  21.7 0.0 collective-permute-done.4
  21.7 1.7 %collective-permute-start.5 = (f32[16,896]{1,0:T(8,128)S(1)}, f32[16,896]{1,0:T(8,128)S(1)}, u32[]{:S(2)}, u32[]{:S(2)}) collective-permute-start(f32[16,896]{1,0:T(8,128)S(1)} %add.12), channel_id=1, source_target_pairs={{0,2},{1,3},{2,0},{3,1},{4,6},{5,7},{6,4},{7,5},{8,10},{9,11},{10,... | collective-permute-start | bytes 172040 | tf_op jit(solution)/shard_map/ppermute | solution.py:482
  23.4 2.7 %shard_map.89 = bf16[8,32,512]{2,1,0:T(8,128)(2,1)} custom-call(bf16[640,1024]{1,0:T(8,128)(2,1)S(1)} %get-tuple-element.54.taps, bf16[768,1024]{1,0:T(8,128)(2,1)S(1)} %get-tuple-element.57.wide, s32[8,512]{1,0:T(8,128)S(1)} %get-tuple-element.43.mask), custom_call_target="tpu_custom_call" | custom-call | tf_op jit(solution)/shard_map/pallas_call | solution.py:552
  26.1 0.0 collective-permute-done.8.far
  26.1 0.0 collective-permute-done.7.near
  26.1 0.1 collective-permute-start.11
  26.2 1.2 %collective-permute-start.9 = (f32[16,896]{1,0:T(8,128)S(1)}, f32[16,896]{1,0:T(8,128)S(1)}, u32[]{:S(2)}, u32[]{:S(2)}) collective-permute-start(f32[16,896]{1,0:T(8,128)S(1)} %add.13), channel_id=1, source_target_pairs={{0,4},{1,5},{2,6},{3,7},{4,0},{5,1},{6,2},{7,3},{8,12},{9,13},{10,... | collective-permute-start | bytes 172040 | tf_op jit(solution)/shard_map/ppermute | solution.py:482
  27.4 3.2 %collective-permute-done.9 = f32[16,896]{1,0:T(8,128)S(1)} collective-permute-done((f32[16,896]{1,0:T(8,128)S(1)}, f32[16,896]{1,0:T(8,128)S(1)}, u32[]{:S(2)}, u32[]{:S(2)}) %collective-permute-start.9) | collective-permute-done | bytes 57376 | tf_op jit(solution)/shard_map/ppermute | solution.py:482
  30.6 1.4 %collective-permute-start.10 = (f32[16,896]{1,0:T(8,128)S(1)}, f32[16,896]{1,0:T(8,128)S(1)}, u32[]{:S(2)}, u32[]{:S(2)}) collective-permute-start(f32[16,896]{1,0:T(8,128)S(1)} %add.14), channel_id=1, source_target_pairs={{0,8},{1,9},{2,10},{3,11},{4,12},{5,13},{6,14},{7,15},{8,0},{9,1},... | collective-permute-start | bytes 172040 | tf_op jit(solution)/shard_map/ppermute | solution.py:482
  32.0 0.0 collective-permute-done.11.last
  32.0 2.6 %shard_map.90 = f32[8,32,512]{2,1,0:T(8,128)} custom-call(f32[8,2,64,128]{3,2,1,0:T(8,128)S(1)} %get-tuple-element.65.center, f32[8,16,256]{2,1,0:T(8,128)S(1)} %get-tuple-element.66.xg, f32[8,16,256]{2,1,0:T(8,128)S(1)} %get-tuple-element.67.yg, f32[8,64,128]{2,1,0:T(8,128)S(1)} %get-tuple-element.68.zg, s32[8,512]{1,0:T(8,128)S(1)} %get-tuple-element.43.mask, ...), custom_call_target="tpu_custom_call" | custom-call | tf_op jit(solution)/shard_map/pallas_call | solution.py:565
  34.6 1.1 %collective-permute-done.10 = f32[16,896]{1,0:T(8,128)S(1)} collective-permute-done((f32[16,896]{1,0:T(8,128)S(1)}, f32[16,896]{1,0:T(8,128)S(1)}, u32[]{:S(2)}, u32[]{:S(2)}) %collective-permute-start.10) | collective-permute-done | bytes 57376 | tf_op jit(solution)/shard_map/ppermute | solution.py:482
  35.8 0.1 collective-permute-start.12
  35.8 1.2 %collective-permute-done.12.other = f32[16,896]{1,0:T(8,128)S(1)} collective-permute-done((f32[16,896]{1,0:T(8,128)S(1)}, f32[16,896]{1,0:T(8,128)S(1)}, u32[]{:S(2)}, u32[]{:S(2)}) %collective-permute-start.12) | collective-permute-done | bytes 57376 | tf_op jit(solution)/shard_map/ppermute | solution.py:482
  37.1 0.9 %shard_map.91 = f32[27,32,32]{2,1,0:T(8,128)} custom-call(f32[16,896]{1,0:T(8,128)S(1)} %add.15.mine, f32[16,896]{1,0:T(8,128)S(1)} %collective-permute-done.12.other), custom_call_target="tpu_custom_call" | custom-call | tf_op jit(solution)/shard_map/pallas_call | solution.py:583
  (17 shorter events, 0.2 us)
Async XLA Ops:
  2.5 1.6 %collective-permute-start = (bf16[5,160,128]{2,1,0:T(8,128)(2,1)S(1)}, bf16[5,160,128]{2,1,0:T(8,128)(2,1)S(1)}, u32[]{:S(2)}, u32[]{:S(2)}) collective-permute-start(bf16[5,160,128]{2,1,0:T(8,128)(2,1)S(1)} %get-tuple-element.46), channel_id=1, source_target_pairs={{0,1},{1,0},{2,3},{3,2},{4,5},{5,4},{6,7},{7,6},{8,9},{9,8},{10,11... | collective-permute-start | bytes 614408 | tf_op jit(solution)/shard_map/ppermute | solution.py:482
  4.2 10.6 %collective-permute-start.1 = (bf16[4,160,128]{2,1,0:T(8,128)(2,1)S(1)}, bf16[4,160,128]{2,1,0:T(8,128)(2,1)S(1)}, u32[]{:S(2)}, u32[]{:S(2)}) collective-permute-start(bf16[4,160,128]{2,1,0:T(8,128)(2,1)S(1)} %pad_maximum_fusion), channel_id=1, source_target_pairs={{0,3},{1,14},{2,5},{3,0},{4,7},{5,2},{6,9},{7,4},{8,11},{9,6},{10,... | collective-permute-start | bytes 491528 | tf_op jit(solution)/shard_map/ppermute | solution.py:482
  6.9 7.9 %collective-permute-start.2 = (bf16[3,160,128]{2,1,0:T(8,128)(2,1)S(1)}, bf16[3,160,128]{2,1,0:T(8,128)(2,1)S(1)}, u32[]{:S(2)}, u32[]{:S(2)}) collective-permute-start(bf16[3,160,128]{2,1,0:T(8,128)(2,1)S(1)} %pad_maximum_fusion.2), channel_id=1, source_target_pairs={{0,4},{1,13},{2,6},{3,15},{4,8},{5,1},{6,10},{7,3},{8,12},{9,5},{1... | collective-permute-start | bytes 368648 | tf_op jit(solution)/shard_map/ppermute | solution.py:482
  12.5 3.1 %collective-permute-start.6 = (bf16[5,160,128]{2,1,0:T(8,128)(2,1)S(1)}, bf16[5,160,128]{2,1,0:T(8,128)(2,1)S(1)}, u32[]{:S(2)}, u32[]{:S(2)}) collective-permute-start(bf16[5,160,128]{2,1,0:T(8,128)(2,1)S(1)} %get-tuple-element.59), channel_id=1, source_target_pairs={{0,1},{1,0},{2,3},{3,2},{4,5},{5,4},{6,7},{7,6},{8,9},{9,8},{10,11... | collective-permute-start | bytes 614408 | tf_op jit(solution)/shard_map/ppermute | solution.py:482
  14.9 2.5 %collective-permute-start.3 = (bf16[3,160,128]{2,1,0:T(8,128)(2,1)S(1)}, bf16[3,160,128]{2,1,0:T(8,128)(2,1)S(1)}, u32[]{:S(2)}, u32[]{:S(2)}) collective-permute-start(bf16[3,160,128]{2,1,0:T(8,128)(2,1)S(1)} %pad_maximum_fusion.3), channel_id=1, source_target_pairs={{0,1},{1,0},{2,3},{3,2},{4,5},{5,4},{6,7},{7,6},{8,9},{9,8},{10,11... | collective-permute-start | bytes 368648 | tf_op jit(solution)/shard_map/ppermute | solution.py:482
  15.7 10.4 %collective-permute-start.7 = (bf16[4,160,128]{2,1,0:T(8,128)(2,1)S(1)}, bf16[4,160,128]{2,1,0:T(8,128)(2,1)S(1)}, u32[]{:S(2)}, u32[]{:S(2)}) collective-permute-start(bf16[4,160,128]{2,1,0:T(8,128)(2,1)S(1)} %pad_maximum_fusion.1), channel_id=1, source_target_pairs={{0,3},{1,14},{2,5},{3,0},{4,7},{5,2},{6,9},{7,4},{8,11},{9,6},{10,... | collective-permute-start | bytes 491528 | tf_op jit(solution)/shard_map/ppermute | solution.py:482
  17.0 9.1 %collective-permute-start.8 = (bf16[3,160,128]{2,1,0:T(8,128)(2,1)S(1)}, bf16[3,160,128]{2,1,0:T(8,128)(2,1)S(1)}, u32[]{:S(2)}, u32[]{:S(2)}) collective-permute-start(bf16[3,160,128]{2,1,0:T(8,128)(2,1)S(1)} %pad_maximum_fusion.4), channel_id=1, source_target_pairs={{0,4},{1,13},{2,6},{3,15},{4,8},{5,1},{6,10},{7,3},{8,12},{9,5},{1... | collective-permute-start | bytes 368648 | tf_op jit(solution)/shard_map/ppermute | solution.py:482
  19.2 2.5 %collective-permute-start.4 = (f32[16,896]{1,0:T(8,128)S(1)}, f32[16,896]{1,0:T(8,128)S(1)}, u32[]{:S(2)}, u32[]{:S(2)}) collective-permute-start(f32[16,896]{1,0:T(8,128)S(1)} %get-tuple-element.56), channel_id=1, source_target_pairs={{0,1},{1,0},{2,3},{3,2},{4,5},{5,4},{6,7},{7,6},{8,9},{9,8},{10,11... | collective-permute-start | bytes 172040 | tf_op jit(solution)/shard_map/ppermute | solution.py:482
  21.7 4.3 %collective-permute-start.5 = (f32[16,896]{1,0:T(8,128)S(1)}, f32[16,896]{1,0:T(8,128)S(1)}, u32[]{:S(2)}, u32[]{:S(2)}) collective-permute-start(f32[16,896]{1,0:T(8,128)S(1)} %add.12), channel_id=1, source_target_pairs={{0,2},{1,3},{2,0},{3,1},{4,6},{5,7},{6,4},{7,5},{8,10},{9,11},{10,... | collective-permute-start | bytes 172040 | tf_op jit(solution)/shard_map/ppermute | solution.py:482
  26.1 5.9 %collective-permute-start.11 = (bf16[3,160,128]{2,1,0:T(8,128)(2,1)S(1)}, bf16[3,160,128]{2,1,0:T(8,128)(2,1)S(1)}, u32[]{:S(2)}, u32[]{:S(2)}) collective-permute-start(bf16[3,160,128]{2,1,0:T(8,128)(2,1)S(1)} %pad_maximum_fusion.5), channel_id=1, source_target_pairs={{0,1},{1,0},{2,3},{3,2},{4,5},{5,4},{6,7},{7,6},{8,9},{9,8},{10,11... | collective-permute-start | bytes 368648 | tf_op jit(solution)/shard_map/ppermute | solution.py:482
  26.2 4.4 %collective-permute-start.9 = (f32[16,896]{1,0:T(8,128)S(1)}, f32[16,896]{1,0:T(8,128)S(1)}, u32[]{:S(2)}, u32[]{:S(2)}) collective-permute-start(f32[16,896]{1,0:T(8,128)S(1)} %add.13), channel_id=1, source_target_pairs={{0,4},{1,5},{2,6},{3,7},{4,0},{5,1},{6,2},{7,3},{8,12},{9,13},{10,... | collective-permute-start | bytes 172040 | tf_op jit(solution)/shard_map/ppermute | solution.py:482
  30.6 5.2 %collective-permute-start.10 = (f32[16,896]{1,0:T(8,128)S(1)}, f32[16,896]{1,0:T(8,128)S(1)}, u32[]{:S(2)}, u32[]{:S(2)}) collective-permute-start(f32[16,896]{1,0:T(8,128)S(1)} %add.14), channel_id=1, source_target_pairs={{0,8},{1,9},{2,10},{3,11},{4,12},{5,13},{6,14},{7,15},{8,0},{9,1},... | collective-permute-start | bytes 172040 | tf_op jit(solution)/shard_map/ppermute | solution.py:482
  35.8 1.3 %collective-permute-start.12 = (f32[16,896]{1,0:T(8,128)S(1)}, f32[16,896]{1,0:T(8,128)S(1)}, u32[]{:S(2)}, u32[]{:S(2)}) collective-permute-start(f32[16,896]{1,0:T(8,128)S(1)} %add.15.mine), channel_id=1, source_target_pairs={{0,1},{1,0},{2,3},{3,2},{4,5},{5,4},{6,7},{7,6},{8,9},{9,8},{10,11... | collective-permute-start | bytes 172040 | tf_op jit(solution)/shard_map/ppermute | solution.py:482

commit v4 on v3

--- a/solution.py
+++ b/solution.py
@@ -13,6 +13,7 @@
 RANGE_AXES = ("curve", "slab")
 VMEM = pl.BlockSpec(memory_space=pltpu.VMEM)
 HBM = pl.BlockSpec(memory_space=pltpu.HBM)
+SMEM = pl.BlockSpec(memory_space=pltpu.SMEM)
 NT = (((1,), (1,)), ((), ()))
 NN = (((1,), (0,)), ((), ()))
 TN = (((0,), (0,)), ((), ()))
@@ -108,8 +109,9 @@
     first, own_near, own_far, center, xf, yf, zf, mask, cot, weights, kmap,
     feat, send, sems,
 ):
-    copies = fetch((feat_hbm, feat, sems.at[0]), (mask_hbm, mask, sems.at[1]), (send_hbm, send, sems.at[2]))
-    later = fetch((cot_hbm, cot, sems.at[3]), (weights_hbm, weights, sems.at[4]), (kmap_hbm, kmap, sems.at[5]))
+    bricks = [(feat_hbm.at[pl.ds(b, 1)], feat.at[pl.ds(b, 1)], sems.at[5 + b]) for b in range(8)]
+    copies = fetch(*bricks, (mask_hbm, mask, sems.at[0]), (send_hbm, send, sems.at[1]))
+    later = fetch((cot_hbm, cot, sems.at[2]), (weights_hbm, weights, sems.at[3]), (kmap_hbm, kmap, sems.at[4]))
     order = voxel_order()
     for c in copies:
         c.wait()
@@ -148,15 +150,25 @@
     return y == 0, y == 7
 
 
+def stack_kernel(cot, mask, stack):
+    order = voxel_order()
+    bricks = to_rows(masked_values(cot[...], mask[...]), order)
+    for b in range(8):
+        c = bricks[b]
+        for d in range(3):
+            before, after = jnp.zeros((8 * d, 256), F32), jnp.zeros((16 - 8 * d, 256), F32)
+            pieces = [p for p in (before, c, after) if p.shape[0]]
+            stack[80 * b : 80 * b + 80, 256 * d : 256 * d + 256] = jnp.concatenate(pieces, axis=0).astype(BF16)
+
+
 def back_kernel(
-    cot, mask, weights, kmap,
-    wide, keep_t, give_t, center, xg, yg, zg, entries, first, own_near, own_far,
-    stack, gp, xa, ya, za, table, sem,
+    stack, weights, kmap,
+    wide, keep_t, give_t, center, xg, yg, zg, table, first, own_near, own_far,
+    gp, xa, ya, za, entries, sem,
 ):
     e = kmap[...]
     entries[...] = jnp.where(e < 0, DUMMY, jnp.where(e < 8, e, ((e - 8) ^ (parity() * 8)) + 8))
     to_table = fetch((entries, table, sem.at[0]))[0]
-    order = voxel_order()
     tile = jnp.where((iota((32, 256), 1) & 31) == iota((32, 256), 0), 1.0, 0.0).astype(BF16)
     tiled = dot(weights[...].reshape(864, 32), tile, NN)
     block = iota((32, 256), 1) >> 5
@@ -180,13 +192,6 @@
                     w = jnp.where(block == 2 * dy + (z == 7), tap(dx, dy, 0 if z == 0 else 2), w)
             wide[rows, 768:1024] = w.astype(BF16)
 
-    bricks = to_rows(masked_values(cot[...], mask[...]), order)
-    for b in range(8):
-        c = bricks[b]
-        for d in range(3):
-            before, after = jnp.zeros((8 * d, 256), F32), jnp.zeros((16 - 8 * d, 256), F32)
-            pieces = [p for p in (before, c, after) if p.shape[0]]
-            stack[80 * b : 80 * b + 80, 256 * d : 256 * d + 256] = jnp.concatenate(pieces, axis=0).astype(BF16)
     odd = parity() == 1
     for d in range(3):
         turned = stack[:, 256 * d : 256 * d + 256].T.reshape(8, 2, 16, 640)
@@ -317,9 +322,8 @@
 
 
 def taps_kernel(
-    center, xf, yf, zf, entries, give_t, first, near, far, last, taps, give, xt, yt, zt, table, sem
+    center, xf, yf, zf, table, give_t, first, near, far, last, taps, give, xt, yt, zt
 ):
-    to_table = fetch((entries, table, sem.at[0]))[0]
     for i in range(8):
         xt[i] = xf[i]
         yt[i] = yf[i]
@@ -346,7 +350,6 @@
         zt[8 + 2 * n, 8:56] = jnp.where(lane < 64, z, turned)
         zt[9 + 2 * n, 8:56] = jnp.where(lane < 64, turned, z)
 
-    to_table.wait()
     low3 = (iota((8, 8, 128), 2) & 32) == 0
     low2 = (iota((8, 128), 1) & 32) == 0
     left3 = iota((10, 8, 128), 2) < 64
@@ -468,9 +471,9 @@
 def call(kernel, outs, scratch, ins, flops=0, size=0):
     return pl.pallas_call(
         kernel,
-        out_shape=[jax.ShapeDtypeStruct(s, d) for s, d in outs],
+        out_shape=[jax.ShapeDtypeStruct(*o) if isinstance(o, tuple) else o for o in outs],
         in_specs=ins,
-        out_specs=[VMEM] * len(outs),
+        out_specs=[VMEM if isinstance(o, tuple) else SMEM for o in outs],
         scratch_shapes=scratch,
         compiler_params=pltpu.CompilerParams(vmem_limit_bytes=40 * 1024 * 1024),
         cost_estimate=pl.CostEstimate(flops=flops, bytes_accessed=size, transcendentals=0),
@@ -494,12 +497,12 @@
     return permute(value, lambda r, count: ((r + (-2 * pairs if r & 1 else 2 * pairs)) % count) ^ cross)
 
 
-def exchange(first, near, far, later):
+def exchange(first, near, far, *later):
     near = jnp.concatenate([near, first[0:2]], axis=0)
     far = jnp.concatenate([far, first[2:4]], axis=0)
-    near, far, later = lax.optimization_barrier((near, far, later))
-    far = onward(far, 2, 0)
-    return onward(near, 1, 1), far, later
+    near, far, *later = lax.optimization_barrier((near, far, *later))
+    near = onward(near, 1, 1)
+    return near, onward(far, 2, 0), *later
 
 
 def exchange_end(near, far):
@@ -513,7 +516,6 @@
     face_shapes = [((8, 16, 256), F32), ((8, 16, 256), F32), ((8, 64, 128), F32)]
     accumulators = [vm(25, 16, 256), vm(25, 16, 256), vm(25, 64, 128)]
     send_space = pltpu.SMEM((2, 8), jnp.int32)
-    table = pltpu.SMEM((8, 27), jnp.int32)
     sems = lambda n: pltpu.SemaphoreType.DMA((n,))
     send = in_hbm(send_list[0].T)
 
@@ -522,39 +524,40 @@
         [block(5), block(2), block(1), center_shape]
         + face_shapes
         + [((8, 512), jnp.int32), ((8, 32, 512), BF16), ((27, 32, 32), BF16), ((8, 27), jnp.int32)],
-        [pltpu.VMEM((8, 32, 512), BF16), send_space, sems(6)],
+        [pltpu.VMEM((8, 32, 512), BF16), send_space, sems(13)],
         [HBM] * 6,
         2 * 512 * 512 * 256,
         1 << 21,
     )(in_hbm(features), in_hbm(voxel_mask), send, in_hbm(grad_out), in_hbm(weights), in_hbm(kernel_map))
     first = swap(first)
-    near, far, kmap = exchange(first, own_near, own_far, kmap)
+    (stack,) = call(stack_kernel, [((640, 768), BF16)], [], [VMEM] * 2, 1 << 28, 2 << 20)(cot, mask)
+    near, far, kmap, stack = exchange(first, own_near, own_far, kmap, stack)
     last = exchange_end(near, far)
 
-    wide, keep_t, give_t, grad_center, xg, yg, zg, entries, grad_first, grad_near, grad_far = call(
+    wide, keep_t, give_t, grad_center, xg, yg, zg, table, grad_first, grad_near, grad_far = call(
         back_kernel,
         [((768, 1024), BF16), ((384, 640), BF16), ((384, 640), BF16), center_shape]
         + face_shapes
-        + [((8, 27), jnp.int32), block(5), block(2), block(1)],
-        [pltpu.VMEM((640, 768), BF16), vm(8, 640, 128)] + accumulators + [table, sems(1)],
-        [VMEM] * 4,
+        + [pltpu.SMEM((8, 27), jnp.int32), block(5), block(2), block(1)],
+        [vm(8, 640, 128)] + accumulators + [pltpu.VMEM((8, 27), jnp.int32), sems(1)],
+        [VMEM] * 3,
         2 * 640 * 768 * 1024,
         8 << 20,
-    )(cot, mask, taps_w, kmap)
+    )(stack, taps_w, kmap)
 
     taps, give = call(
         taps_kernel,
         [((640, 1024), BF16), ((16, 896), F32)],
-        accumulators + [table, sems(1)],
-        [VMEM] * 10,
-    )(center, xf, yf, zf, entries, give_t, first, near, far, last)
+        accumulators,
+        [VMEM] * 4 + [SMEM] + [VMEM] * 5,
+    )(center, xf, yf, zf, pltpu.with_memory_space_constraint(table, pltpu.SMEM), give_t, first, near, far, last)
 
     (conv,) = call(
         conv_kernel, [((8, 32, 512), BF16)], [], [VMEM] * 3
     )(taps, wide, mask)
 
     grad_first = swap(grad_first)
-    grad_near, grad_far, _ = exchange(grad_first, grad_near, grad_far, 0.0)
+    grad_near, grad_far = exchange(grad_first, grad_near, grad_far)
 
     (keep,) = call(keep_kernel, [((16, 896), F32)], [], [VMEM] * 2)(taps, keep_t)
     part = keep + swap(give)

time: 38.2 us -> 37.6 us (0.984)
  Pallas kernels: 14.8 us -> 14.1 us
    pallas_call x1, Pallas kernels: 4.02 us -> 3.31 us  [body(): call(back_kernel, [((768, 1024), BF16), ((384, 640), BF16), ((384, 640),...]
    pallas_call x1 -> x2, Pallas kernels: 1.76 us -> 1.75 us  [the longest x1 1.26 us: body(): call(taps_kernel, [((640, 1024), BF16), ((16, 896), F32)], accumulators,...]
  transfers between devices with their start and end apart: 13 -> 13, of which waited for: 6 -> 5; matrix products, arithmetic and copies ran while one was open for 0% -> 0% of each run, Pallas kernels for 32% -> 30%
where the time goes in v4:
time: 37.6 us; the launch traced here: 37.5 us
  starting transfers between devices  14.9 us (40%)
  Pallas kernels  14.1 us (38%)
  waiting for transfers between devices  7.52 us (20%)
  between operations  0.77 us (2%)
    ppermute x13, starting transfers between devices, permute(): lax.ppermute(value, RANGE_AXES, [(r, target(r, count)) for r in range(cou...  14.9 us
    ppermute x13, waiting for transfers between devices, permute(): lax.ppermute(value, RANGE_AXES, [(r, target(r, count)) for r in range(cou...  7.52 us
    pallas_call x1, Pallas kernels, body(): call(back_kernel, [((768, 1024), BF16), ((384, 640), BF16), ((384, 640),...  3.31 us
    pallas_call x1, Pallas kernels, body(): call(conv_kernel, [((8, 32, 512), BF16)], [], [VMEM] * 3)(taps, wide, mask)  2.67 us
    pallas_call x1, Pallas kernels, body(): call(fold_kernel, [((8, 32, 512), F32)], [vm(8, 16, 256), vm(8, 16, 256),...  2.64 us
    pallas_call x1, Pallas kernels, body(): call(pack_kernel, [block(5), block(2), block(1), center_shape] + face_sha...  1.88 us
    pallas_call x1, Pallas kernels, body(): call(taps_kernel, [((640, 1024), BF16), ((16, 896), F32)], accumulators,...  1.26 us
    pallas_call x1, Pallas kernels, body(): call(functools.partial(spread_kernel, scale), [((27, 32, 32), F32)], [],...  0.92 us
  transfers between devices with their start and end apart: 13, of which 5 were waited for; matrix products, arithmetic and copies ran while one was open for 0% of the time, Pallas kernels for 30%

profile of v4, /device:TPU:0, one launch (start us, length us, event | category | flops | bytes accessed | tf_op | source)
XLA Modules:
  0.0 37.5 jit_solution(8440976376860045501)
XLA Ops:
  0.6 1.9 %shard_map.85 = (bf16[5,160,128]{2,1,0:T(8,128)(2,1)S(1)}, bf16[2,160,128]{2,1,0:T(8,128)(2,1)S(1)}, bf16[1,160,128]{2,1,0:T(8,128)(2,1)S(1)}, f32[8,2,64,128]{3...) custom-call(bf16[8,32,512]{2,1,0:T(8,128)(2,1)} %feat_hbm.1, ...), custom_call_target="tpu_custom_call" | custom-call | flops 134217728 | bytes 2097152 | tf_op jit(solution)/shard_map/pallas_call | solution.py:522
  2.5 0.5 %collective-permute-start = (bf16[5,160,128]{2,1,0:T(8,128)(2,1)S(1)}, bf16[5,160,128]{2,1,0:T(8,128)(2,1)S(1)}, u32[]{:S(2)}, u32[]{:S(2)}) collective-permute-start(bf16[5,160,128]{2,1,0:T(8,128)(2,1)S(1)} %get-tuple-element.44), channel_id=1, source_target_pairs={{0,1},{1,0},{2,3},{3,2},{4,5},{5,4},{6,7},{7,6},{8,9},{9,8},{10,11... | collective-permute-start | bytes 614408 | tf_op jit(solution)/shard_map/ppermute | solution.py:485
  3.0 0.5 %shard_map.86.stack = bf16[640,768]{1,0:T(8,128)(2,1)S(1)} custom-call(bf16[8,32,512]{2,1,0:T(8,128)(2,1)S(1)} %get-tuple-element.47.cot, s32[8,512]{1,0:T(8,128)S(1)} %get-tuple-element.48.mask), custom_call_target="tpu_custom_call" | custom-call | flops 268435456 | bytes 2097152 | tf_op jit(solution)/shard_map/pallas_call | solution.py:533
  3.5 0.6 %collective-permute-done.first = bf16[5,160,128]{2,1,0:T(8,128)(2,1)S(1)} collective-permute-done((bf16[5,160,128]{2,1,0:T(8,128)(2,1)S(1)}, bf16[5,160,128]{2,1,0:T(8,128)(2,1)S(1)}, u32[]{:S(2)}, u32[]{:S(2)}) %collective-permute-start) | collective-permute-done | bytes 204832 | tf_op jit(solution)/shard_map/ppermute | solution.py:485
  4.2 2.7 %collective-permute-start.1 = (bf16[4,160,128]{2,1,0:T(8,128)(2,1)S(1)}, bf16[4,160,128]{2,1,0:T(8,128)(2,1)S(1)}, u32[]{:S(2)}, u32[]{:S(2)}) collective-permute-start(bf16[4,160,128]{2,1,0:T(8,128)(2,1)S(1)} %pad_maximum_fusion), channel_id=1, source_target_pairs={{0,3},{1,14},{2,5},{3,0},{4,7},{5,2},{6,9},{7,4},{8,11},{9,6},{10,... | collective-permute-start | bytes 491528 | tf_op jit(solution)/shard_map/ppermute | solution.py:485
  6.8 1.6 %collective-permute-start.2 = (bf16[3,160,128]{2,1,0:T(8,128)(2,1)S(1)}, bf16[3,160,128]{2,1,0:T(8,128)(2,1)S(1)}, u32[]{:S(2)}, u32[]{:S(2)}) collective-permute-start(bf16[3,160,128]{2,1,0:T(8,128)(2,1)S(1)} %pad_maximum_fusion.2), channel_id=1, source_target_pairs={{0,4},{1,13},{2,6},{3,15},{4,8},{5,1},{6,10},{7,3},{8,12},{9,5},{1... | collective-permute-start | bytes 368648 | tf_op jit(solution)/shard_map/ppermute | solution.py:485
  8.4 3.3 %shard_map.87 = (bf16[768,1024]{1,0:T(8,128)(2,1)S(1)}, bf16[384,640]{1,0:T(8,128)(2,1)S(1)}, bf16[384,640]{1,0:T(8,128)(2,1)S(1)}, f32[8,2,64,128]{3,2,1,0:T(8,...) custom-call(bf16[640,768]{1,0:T(8,128)(2,1)S(1)} %shard_map.86.stack, ...), custom_call_target="tpu_custom_call" | custom-call | flops 1006632960 | bytes 8388608 | tf_op jit(solution)/shard_map/pallas_call | solution.py:537
  11.7 2.1 %collective-permute-start.6 = (bf16[5,160,128]{2,1,0:T(8,128)(2,1)S(1)}, bf16[5,160,128]{2,1,0:T(8,128)(2,1)S(1)}, u32[]{:S(2)}, u32[]{:S(2)}) collective-permute-start(bf16[5,160,128]{2,1,0:T(8,128)(2,1)S(1)} %get-tuple-element.61), channel_id=1, source_target_pairs={{0,1},{1,0},{2,3},{3,2},{4,5},{5,4},{6,7},{7,6},{8,9},{9,8},{10,11... | collective-permute-start | bytes 614408 | tf_op jit(solution)/shard_map/ppermute | solution.py:485
  13.8 1.0 %collective-permute-done.2.far = bf16[3,160,128]{2,1,0:T(8,128)(2,1)S(1)} collective-permute-done((bf16[3,160,128]{2,1,0:T(8,128)(2,1)S(1)}, bf16[3,160,128]{2,1,0:T(8,128)(2,1)S(1)}, u32[]{:S(2)}, u32[]{:S(2)}) %collective-permute-start.2) | collective-permute-done | bytes 122912 | tf_op jit(solution)/shard_map/ppermute | solution.py:485
  14.8 0.0 collective-permute-done.1.near
  14.8 0.2 collective-permute-start.3
  15.1 0.0 collective-permute-done.6.first
  15.1 1.9 %collective-permute-start.7 = (bf16[4,160,128]{2,1,0:T(8,128)(2,1)S(1)}, bf16[4,160,128]{2,1,0:T(8,128)(2,1)S(1)}, u32[]{:S(2)}, u32[]{:S(2)}) collective-permute-start(bf16[4,160,128]{2,1,0:T(8,128)(2,1)S(1)} %pad_maximum_fusion.1), channel_id=1, source_target_pairs={{0,3},{1,14},{2,5},{3,0},{4,7},{5,2},{6,9},{7,4},{8,11},{9,6},{10,... | collective-permute-start | bytes 491528 | tf_op jit(solution)/shard_map/ppermute | solution.py:485
  17.0 0.0 collective-permute-start.8
  17.0 1.3 %shard_map.88 = (bf16[640,1024]{1,0:T(8,128)(2,1)S(1)}, f32[16,896]{1,0:T(8,128)S(1)}) custom-call(f32[8,2,64,128]{3,2,1,0:T(8,128)S(1)} %get-tuple-element.39.center, f32[8,16,256]{2,1,0:T(8,128)S(1)} %get-tuple-element.40.xf, f32[8,16,256]{2,1,0:T(8,128)S(1)} %get-tuple-element.41.yf, f32[8,64,128]{2,1,0:T(8,128)S(1)} %get-tuple-element.42.zf, ...), custom_call_target="tpu_custom_call" | custom-call | tf_op jit(solution)/shard_map/pallas_call | solution.py:548
  18.3 2.0 %collective-permute-start.4 = (f32[16,896]{1,0:T(8,128)S(1)}, f32[16,896]{1,0:T(8,128)S(1)}, u32[]{:S(2)}, u32[]{:S(2)}) collective-permute-start(f32[16,896]{1,0:T(8,128)S(1)} %get-tuple-element.58), channel_id=1, source_target_pairs={{0,1},{1,0},{2,3},{3,2},{4,5},{5,4},{6,7},{7,6},{8,9},{9,8},{10,11... | collective-permute-start | bytes 172040 | tf_op jit(solution)/shard_map/ppermute | solution.py:485
  20.3 0.9 %shard_map.89 = f32[16,896]{1,0:T(8,128)S(1)} custom-call(bf16[640,1024]{1,0:T(8,128)(2,1)S(1)} %get-tuple-element.56.taps, bf16[384,640]{1,0:T(8,128)(2,1)S(1)} %get-tuple-element.57.keep_t), custom_call_target="tpu_custom_call" | custom-call | tf_op jit(solution)/shard_map/pallas_call | solution.py:562
  21.2 0.0 collective-permute-done.4
  21.2 1.7 %collective-permute-start.5 = (f32[16,896]{1,0:T(8,128)S(1)}, f32[16,896]{1,0:T(8,128)S(1)}, u32[]{:S(2)}, u32[]{:S(2)}) collective-permute-start(f32[16,896]{1,0:T(8,128)S(1)} %add.12), channel_id=1, source_target_pairs={{0,2},{1,3},{2,0},{3,1},{4,6},{5,7},{6,4},{7,5},{8,10},{9,11},{10,... | collective-permute-start | bytes 172040 | tf_op jit(solution)/shard_map/ppermute | solution.py:485
  22.9 2.7 %shard_map.90 = bf16[8,32,512]{2,1,0:T(8,128)(2,1)} custom-call(bf16[640,1024]{1,0:T(8,128)(2,1)S(1)} %get-tuple-element.56.taps, bf16[768,1024]{1,0:T(8,128)(2,1)S(1)} %get-tuple-element.59.wide, s32[8,512]{1,0:T(8,128)S(1)} %get-tuple-element.48.mask), custom_call_target="tpu_custom_call" | custom-call | tf_op jit(solution)/shard_map/pallas_call | solution.py:555
  25.5 0.0 collective-permute-done.8.far
  25.5 0.0 collective-permute-done.7.near
  25.6 0.0 collective-permute-done.5
  25.6 0.1 collective-permute-start.11
  25.7 1.2 %collective-permute-start.9 = (f32[16,896]{1,0:T(8,128)S(1)}, f32[16,896]{1,0:T(8,128)S(1)}, u32[]{:S(2)}, u32[]{:S(2)}) collective-permute-start(f32[16,896]{1,0:T(8,128)S(1)} %add.13), channel_id=1, source_target_pairs={{0,4},{1,5},{2,6},{3,7},{4,0},{5,1},{6,2},{7,3},{8,12},{9,13},{10,... | collective-permute-start | bytes 172040 | tf_op jit(solution)/shard_map/ppermute | solution.py:485
  26.9 3.2 %collective-permute-done.9 = f32[16,896]{1,0:T(8,128)S(1)} collective-permute-done((f32[16,896]{1,0:T(8,128)S(1)}, f32[16,896]{1,0:T(8,128)S(1)}, u32[]{:S(2)}, u32[]{:S(2)}) %collective-permute-start.9) | collective-permute-done | bytes 57376 | tf_op jit(solution)/shard_map/ppermute | solution.py:485
  30.1 1.0 %collective-permute-start.10 = (f32[16,896]{1,0:T(8,128)S(1)}, f32[16,896]{1,0:T(8,128)S(1)}, u32[]{:S(2)}, u32[]{:S(2)}) collective-permute-start(f32[16,896]{1,0:T(8,128)S(1)} %add.14), channel_id=1, source_target_pairs={{0,8},{1,9},{2,10},{3,11},{4,12},{5,13},{6,14},{7,15},{8,0},{9,1},... | collective-permute-start | bytes 172040 | tf_op jit(solution)/shard_map/ppermute | solution.py:485
  31.1 2.6 %shard_map.91 = f32[8,32,512]{2,1,0:T(8,128)} custom-call(f32[8,2,64,128]{3,2,1,0:T(8,128)S(1)} %get-tuple-element.67.center, f32[8,16,256]{2,1,0:T(8,128)S(1)} %get-tuple-element.68.xg, f32[8,16,256]{2,1,0:T(8,128)S(1)} %get-tuple-element.69.yg, f32[8,64,128]{2,1,0:T(8,128)S(1)} %get-tuple-element.70.zg, s32[8,512]{1,0:T(8,128)S(1)} %get-tuple-element.48.mask, ...), custom_call_target="tpu_custom_call" | custom-call | tf_op jit(solution)/shard_map/pallas_call | solution.py:568
  33.7 1.5 %collective-permute-done.10 = f32[16,896]{1,0:T(8,128)S(1)} collective-permute-done((f32[16,896]{1,0:T(8,128)S(1)}, f32[16,896]{1,0:T(8,128)S(1)}, u32[]{:S(2)}, u32[]{:S(2)}) %collective-permute-start.10) | collective-permute-done | bytes 57376 | tf_op jit(solution)/shard_map/ppermute | solution.py:485
  35.3 0.1 collective-permute-start.12
  35.3 1.2 %collective-permute-done.12.other = f32[16,896]{1,0:T(8,128)S(1)} collective-permute-done((f32[16,896]{1,0:T(8,128)S(1)}, f32[16,896]{1,0:T(8,128)S(1)}, u32[]{:S(2)}, u32[]{:S(2)}) %collective-permute-start.12) | collective-permute-done | bytes 57376 | tf_op jit(solution)/shard_map/ppermute | solution.py:485
  36.6 0.9 %shard_map.92 = f32[27,32,32]{2,1,0:T(8,128)} custom-call(f32[16,896]{1,0:T(8,128)S(1)} %add.15.mine, f32[16,896]{1,0:T(8,128)S(1)} %collective-permute-done.12.other), custom_call_target="tpu_custom_call" | custom-call | tf_op jit(solution)/shard_map/pallas_call | solution.py:586
  (18 shorter events, 0.2 us)
Async XLA Ops:
  2.5 1.6 %collective-permute-start = (bf16[5,160,128]{2,1,0:T(8,128)(2,1)S(1)}, bf16[5,160,128]{2,1,0:T(8,128)(2,1)S(1)}, u32[]{:S(2)}, u32[]{:S(2)}) collective-permute-start(bf16[5,160,128]{2,1,0:T(8,128)(2,1)S(1)} %get-tuple-element.44), channel_id=1, source_target_pairs={{0,1},{1,0},{2,3},{3,2},{4,5},{5,4},{6,7},{7,6},{8,9},{9,8},{10,11... | collective-permute-start | bytes 614408 | tf_op jit(solution)/shard_map/ppermute | solution.py:485
  4.2 10.6 %collective-permute-start.1 = (bf16[4,160,128]{2,1,0:T(8,128)(2,1)S(1)}, bf16[4,160,128]{2,1,0:T(8,128)(2,1)S(1)}, u32[]{:S(2)}, u32[]{:S(2)}) collective-permute-start(bf16[4,160,128]{2,1,0:T(8,128)(2,1)S(1)} %pad_maximum_fusion), channel_id=1, source_target_pairs={{0,3},{1,14},{2,5},{3,0},{4,7},{5,2},{6,9},{7,4},{8,11},{9,6},{10,... | collective-permute-start | bytes 491528 | tf_op jit(solution)/shard_map/ppermute | solution.py:485
  6.8 7.9 %collective-permute-start.2 = (bf16[3,160,128]{2,1,0:T(8,128)(2,1)S(1)}, bf16[3,160,128]{2,1,0:T(8,128)(2,1)S(1)}, u32[]{:S(2)}, u32[]{:S(2)}) collective-permute-start(bf16[3,160,128]{2,1,0:T(8,128)(2,1)S(1)} %pad_maximum_fusion.2), channel_id=1, source_target_pairs={{0,4},{1,13},{2,6},{3,15},{4,8},{5,1},{6,10},{7,3},{8,12},{9,5},{1... | collective-permute-start | bytes 368648 | tf_op jit(solution)/shard_map/ppermute | solution.py:485
  11.7 3.3 %collective-permute-start.6 = (bf16[5,160,128]{2,1,0:T(8,128)(2,1)S(1)}, bf16[5,160,128]{2,1,0:T(8,128)(2,1)S(1)}, u32[]{:S(2)}, u32[]{:S(2)}) collective-permute-start(bf16[5,160,128]{2,1,0:T(8,128)(2,1)S(1)} %get-tuple-element.61), channel_id=1, source_target_pairs={{0,1},{1,0},{2,3},{3,2},{4,5},{5,4},{6,7},{7,6},{8,9},{9,8},{10,11... | collective-permute-start | bytes 614408 | tf_op jit(solution)/shard_map/ppermute | solution.py:485
  14.8 2.2 %collective-permute-start.3 = (bf16[3,160,128]{2,1,0:T(8,128)(2,1)S(1)}, bf16[3,160,128]{2,1,0:T(8,128)(2,1)S(1)}, u32[]{:S(2)}, u32[]{:S(2)}) collective-permute-start(bf16[3,160,128]{2,1,0:T(8,128)(2,1)S(1)} %pad_maximum_fusion.3), channel_id=1, source_target_pairs={{0,1},{1,0},{2,3},{3,2},{4,5},{5,4},{6,7},{7,6},{8,9},{9,8},{10,11... | collective-permute-start | bytes 368648 | tf_op jit(solution)/shard_map/ppermute | solution.py:485
  15.1 10.4 %collective-permute-start.7 = (bf16[4,160,128]{2,1,0:T(8,128)(2,1)S(1)}, bf16[4,160,128]{2,1,0:T(8,128)(2,1)S(1)}, u32[]{:S(2)}, u32[]{:S(2)}) collective-permute-start(bf16[4,160,128]{2,1,0:T(8,128)(2,1)S(1)} %pad_maximum_fusion.1), channel_id=1, source_target_pairs={{0,3},{1,14},{2,5},{3,0},{4,7},{5,2},{6,9},{7,4},{8,11},{9,6},{10,... | collective-permute-start | bytes 491528 | tf_op jit(solution)/shard_map/ppermute | solution.py:485
  17.0 8.5 %collective-permute-start.8 = (bf16[3,160,128]{2,1,0:T(8,128)(2,1)S(1)}, bf16[3,160,128]{2,1,0:T(8,128)(2,1)S(1)}, u32[]{:S(2)}, u32[]{:S(2)}) collective-permute-start(bf16[3,160,128]{2,1,0:T(8,128)(2,1)S(1)} %pad_maximum_fusion.4), channel_id=1, source_target_pairs={{0,4},{1,13},{2,6},{3,15},{4,8},{5,1},{6,10},{7,3},{8,12},{9,5},{1... | collective-permute-start | bytes 368648 | tf_op jit(solution)/shard_map/ppermute | solution.py:485
  18.3 2.9 %collective-permute-start.4 = (f32[16,896]{1,0:T(8,128)S(1)}, f32[16,896]{1,0:T(8,128)S(1)}, u32[]{:S(2)}, u32[]{:S(2)}) collective-permute-start(f32[16,896]{1,0:T(8,128)S(1)} %get-tuple-element.58), channel_id=1, source_target_pairs={{0,1},{1,0},{2,3},{3,2},{4,5},{5,4},{6,7},{7,6},{8,9},{9,8},{10,11... | collective-permute-start | bytes 172040 | tf_op jit(solution)/shard_map/ppermute | solution.py:485
  21.2 4.4 %collective-permute-start.5 = (f32[16,896]{1,0:T(8,128)S(1)}, f32[16,896]{1,0:T(8,128)S(1)}, u32[]{:S(2)}, u32[]{:S(2)}) collective-permute-start(f32[16,896]{1,0:T(8,128)S(1)} %add.12), channel_id=1, source_target_pairs={{0,2},{1,3},{2,0},{3,1},{4,6},{5,7},{6,4},{7,5},{8,10},{9,11},{10,... | collective-permute-start | bytes 172040 | tf_op jit(solution)/shard_map/ppermute | solution.py:485
  25.6 5.5 %collective-permute-start.11 = (bf16[3,160,128]{2,1,0:T(8,128)(2,1)S(1)}, bf16[3,160,128]{2,1,0:T(8,128)(2,1)S(1)}, u32[]{:S(2)}, u32[]{:S(2)}) collective-permute-start(bf16[3,160,128]{2,1,0:T(8,128)(2,1)S(1)} %pad_maximum_fusion.5), channel_id=1, source_target_pairs={{0,1},{1,0},{2,3},{3,2},{4,5},{5,4},{6,7},{7,6},{8,9},{9,8},{10,11... | collective-permute-start | bytes 368648 | tf_op jit(solution)/shard_map/ppermute | solution.py:485
  25.7 4.4 %collective-permute-start.9 = (f32[16,896]{1,0:T(8,128)S(1)}, f32[16,896]{1,0:T(8,128)S(1)}, u32[]{:S(2)}, u32[]{:S(2)}) collective-permute-start(f32[16,896]{1,0:T(8,128)S(1)} %add.13), channel_id=1, source_target_pairs={{0,4},{1,5},{2,6},{3,7},{4,0},{5,1},{6,2},{7,3},{8,12},{9,13},{10,... | collective-permute-start | bytes 172040 | tf_op jit(solution)/shard_map/ppermute | solution.py:485
  30.1 5.2 %collective-permute-start.10 = (f32[16,896]{1,0:T(8,128)S(1)}, f32[16,896]{1,0:T(8,128)S(1)}, u32[]{:S(2)}, u32[]{:S(2)}) collective-permute-start(f32[16,896]{1,0:T(8,128)S(1)} %add.14), channel_id=1, source_target_pairs={{0,8},{1,9},{2,10},{3,11},{4,12},{5,13},{6,14},{7,15},{8,0},{9,1},... | collective-permute-start | bytes 172040 | tf_op jit(solution)/shard_map/ppermute | solution.py:485
  35.3 1.3 %collective-permute-start.12 = (f32[16,896]{1,0:T(8,128)S(1)}, f32[16,896]{1,0:T(8,128)S(1)}, u32[]{:S(2)}, u32[]{:S(2)}) collective-permute-start(f32[16,896]{1,0:T(8,128)S(1)} %add.15.mine), channel_id=1, source_target_pairs={{0,1},{1,0},{2,3},{3,2},{4,5},{5,4},{6,7},{7,6},{8,9},{9,8},{10,11... | collective-permute-start | bytes 172040 | tf_op jit(solution)/shard_map/ppermute | solution.py:485

commit v5 on v4

--- a/solution.py
+++ b/solution.py
@@ -107,7 +107,7 @@
 def pack_kernel(
     feat_hbm, mask_hbm, send_hbm, cot_hbm, weights_hbm, kmap_hbm,
     first, own_near, own_far, center, xf, yf, zf, mask, cot, weights, kmap,
-    feat, send, sems,
+    feat, send, padded, sems,
 ):
     bricks = [(feat_hbm.at[pl.ds(b, 1)], feat.at[pl.ds(b, 1)], sems.at[5 + b]) for b in range(8)]
     copies = fetch(*bricks, (mask_hbm, mask, sems.at[0]), (send_hbm, send, sems.at[1]))
@@ -121,12 +121,13 @@
         c = bricks[b]
         for h in range(2):
             center[b, h] = c[:, 128 * h : 128 * h + 128]
+            padded[b, h, 0:64] = c[:, 128 * h : 128 * h + 128]
         xf[b, 0:8] = c[0:8]
         xf[b, 8:16] = c[56:64]
         for h in range(2):
             s = slice(128 * h, 128 * h + 128)
-            yf[b, 0:8, s] = center[b, h, pl.ds(0, 8, 8), :]
-            yf[b, 8:16, s] = center[b, h, pl.ds(7, 8, 8), :]
+            yf[b, 0:8, s] = padded[b, h, pl.ds(0, 8, 8), :]
+            yf[b, 8:16, s] = padded[b, h, pl.ds(7, 8, 8), :]
         zf[b] = z_planes(c[:, :128], c[:, 128:])
     flip = parity() * 4
 
@@ -524,7 +525,7 @@
         [block(5), block(2), block(1), center_shape]
         + face_shapes
         + [((8, 512), jnp.int32), ((8, 32, 512), BF16), ((27, 32, 32), BF16), ((8, 27), jnp.int32)],
-        [pltpu.VMEM((8, 32, 512), BF16), send_space, sems(13)],
+        [pltpu.VMEM((8, 32, 512), BF16), send_space, vm(8, 2, 72, 128), sems(13)],
         [HBM] * 6,
         2 * 512 * 512 * 256,
         1 << 21,

time: 37.6 us -> 37.6 us (level)
  no operation moved by 1% of the time
where the time goes in v5:
time: 37.6 us; the launch traced here: 37.5 us
  starting transfers between devices  14.9 us (40%)
  Pallas kernels  14.1 us (38%)
  waiting for transfers between devices  7.54 us (20%)
  between operations  0.77 us (2%)
    ppermute x13, starting transfers between devices, permute(): lax.ppermute(value, RANGE_AXES, [(r, target(r, count)) for r in range(cou...  14.9 us
    ppermute x13, waiting for transfers between devices, permute(): lax.ppermute(value, RANGE_AXES, [(r, target(r, count)) for r in range(cou...  7.54 us
    pallas_call x1, Pallas kernels, body(): call(back_kernel, [((768, 1024), BF16), ((384, 640), BF16), ((384, 640),...  3.3 us
    pallas_call x1, Pallas kernels, body(): call(conv_kernel, [((8, 32, 512), BF16)], [], [VMEM] * 3)(taps, wide, mask)  2.67 us
    pallas_call x1, Pallas kernels, body(): call(fold_kernel, [((8, 32, 512), F32)], [vm(8, 16, 256), vm(8, 16, 256),...  2.63 us
    pallas_call x1, Pallas kernels, body(): call(pack_kernel, [block(5), block(2), block(1), center_shape] + face_sha...  1.88 us
    pallas_call x1, Pallas kernels, body(): call(taps_kernel, [((640, 1024), BF16), ((16, 896), F32)], accumulators,...  1.26 us
    pallas_call x1, Pallas kernels, body(): call(functools.partial(spread_kernel, scale), [((27, 32, 32), F32)], [],...  0.92 us
  transfers between devices with their start and end apart: 13, of which 5 were waited for; matrix products, arithmetic and copies ran while one was open for 0% of the time, Pallas kernels for 30%

profile of v5, /device:TPU:0, one launch (start us, length us, event | category | flops | bytes accessed | tf_op | source)
XLA Modules:
  0.0 37.5 jit_solution(5760211125474742353)
XLA Ops:
  0.6 1.9 %shard_map.85 = (bf16[5,160,128]{2,1,0:T(8,128)(2,1)S(1)}, bf16[2,160,128]{2,1,0:T(8,128)(2,1)S(1)}, bf16[1,160,128]{2,1,0:T(8,128)(2,1)S(1)}, f32[8,2,64,128]{3...) custom-call(bf16[8,32,512]{2,1,0:T(8,128)(2,1)} %feat_hbm.1, ...), custom_call_target="tpu_custom_call" | custom-call | flops 134217728 | bytes 2097152 | tf_op jit(solution)/shard_map/pallas_call | solution.py:523
  2.5 0.5 %collective-permute-start = (bf16[5,160,128]{2,1,0:T(8,128)(2,1)S(1)}, bf16[5,160,128]{2,1,0:T(8,128)(2,1)S(1)}, u32[]{:S(2)}, u32[]{:S(2)}) collective-permute-start(bf16[5,160,128]{2,1,0:T(8,128)(2,1)S(1)} %get-tuple-element.44), channel_id=1, source_target_pairs={{0,1},{1,0},{2,3},{3,2},{4,5},{5,4},{6,7},{7,6},{8,9},{9,8},{10,11... | collective-permute-start | bytes 614408 | tf_op jit(solution)/shard_map/ppermute | solution.py:486
  3.0 0.5 %shard_map.86.stack = bf16[640,768]{1,0:T(8,128)(2,1)S(1)} custom-call(bf16[8,32,512]{2,1,0:T(8,128)(2,1)S(1)} %get-tuple-element.47.cot, s32[8,512]{1,0:T(8,128)S(1)} %get-tuple-element.48.mask), custom_call_target="tpu_custom_call" | custom-call | flops 268435456 | bytes 2097152 | tf_op jit(solution)/shard_map/pallas_call | solution.py:534
  3.5 0.6 %collective-permute-done.first = bf16[5,160,128]{2,1,0:T(8,128)(2,1)S(1)} collective-permute-done((bf16[5,160,128]{2,1,0:T(8,128)(2,1)S(1)}, bf16[5,160,128]{2,1,0:T(8,128)(2,1)S(1)}, u32[]{:S(2)}, u32[]{:S(2)}) %collective-permute-start) | collective-permute-done | bytes 204832 | tf_op jit(solution)/shard_map/ppermute | solution.py:486
  4.2 2.7 %collective-permute-start.1 = (bf16[4,160,128]{2,1,0:T(8,128)(2,1)S(1)}, bf16[4,160,128]{2,1,0:T(8,128)(2,1)S(1)}, u32[]{:S(2)}, u32[]{:S(2)}) collective-permute-start(bf16[4,160,128]{2,1,0:T(8,128)(2,1)S(1)} %pad_maximum_fusion), channel_id=1, source_target_pairs={{0,3},{1,14},{2,5},{3,0},{4,7},{5,2},{6,9},{7,4},{8,11},{9,6},{10,... | collective-permute-start | bytes 491528 | tf_op jit(solution)/shard_map/ppermute | solution.py:486
  6.8 1.6 %collective-permute-start.2 = (bf16[3,160,128]{2,1,0:T(8,128)(2,1)S(1)}, bf16[3,160,128]{2,1,0:T(8,128)(2,1)S(1)}, u32[]{:S(2)}, u32[]{:S(2)}) collective-permute-start(bf16[3,160,128]{2,1,0:T(8,128)(2,1)S(1)} %pad_maximum_fusion.2), channel_id=1, source_target_pairs={{0,4},{1,13},{2,6},{3,15},{4,8},{5,1},{6,10},{7,3},{8,12},{9,5},{1... | collective-permute-start | bytes 368648 | tf_op jit(solution)/shard_map/ppermute | solution.py:486
  8.4 3.3 %shard_map.87 = (bf16[768,1024]{1,0:T(8,128)(2,1)S(1)}, bf16[384,640]{1,0:T(8,128)(2,1)S(1)}, bf16[384,640]{1,0:T(8,128)(2,1)S(1)}, f32[8,2,64,128]{3,2,1,0:T(8,...) custom-call(bf16[640,768]{1,0:T(8,128)(2,1)S(1)} %shard_map.86.stack, ...), custom_call_target="tpu_custom_call" | custom-call | flops 1006632960 | bytes 8388608 | tf_op jit(solution)/shard_map/pallas_call | solution.py:538
  11.7 2.1 %collective-permute-start.6 = (bf16[5,160,128]{2,1,0:T(8,128)(2,1)S(1)}, bf16[5,160,128]{2,1,0:T(8,128)(2,1)S(1)}, u32[]{:S(2)}, u32[]{:S(2)}) collective-permute-start(bf16[5,160,128]{2,1,0:T(8,128)(2,1)S(1)} %get-tuple-element.61), channel_id=1, source_target_pairs={{0,1},{1,0},{2,3},{3,2},{4,5},{5,4},{6,7},{7,6},{8,9},{9,8},{10,11... | collective-permute-start | bytes 614408 | tf_op jit(solution)/shard_map/ppermute | solution.py:486
  13.8 1.0 %collective-permute-done.2.far = bf16[3,160,128]{2,1,0:T(8,128)(2,1)S(1)} collective-permute-done((bf16[3,160,128]{2,1,0:T(8,128)(2,1)S(1)}, bf16[3,160,128]{2,1,0:T(8,128)(2,1)S(1)}, u32[]{:S(2)}, u32[]{:S(2)}) %collective-permute-start.2) | collective-permute-done | bytes 122912 | tf_op jit(solution)/shard_map/ppermute | solution.py:486
  14.8 0.0 collective-permute-done.1.near
  14.8 0.2 collective-permute-start.3
  15.1 0.0 collective-permute-done.6.first
  15.2 1.9 %collective-permute-start.7 = (bf16[4,160,128]{2,1,0:T(8,128)(2,1)S(1)}, bf16[4,160,128]{2,1,0:T(8,128)(2,1)S(1)}, u32[]{:S(2)}, u32[]{:S(2)}) collective-permute-start(bf16[4,160,128]{2,1,0:T(8,128)(2,1)S(1)} %pad_maximum_fusion.1), channel_id=1, source_target_pairs={{0,3},{1,14},{2,5},{3,0},{4,7},{5,2},{6,9},{7,4},{8,11},{9,6},{10,... | collective-permute-start | bytes 491528 | tf_op jit(solution)/shard_map/ppermute | solution.py:486
  17.0 0.0 collective-permute-start.8
  17.0 0.0 collective-permute-done.3.last
  17.0 1.3 %shard_map.88 = (bf16[640,1024]{1,0:T(8,128)(2,1)S(1)}, f32[16,896]{1,0:T(8,128)S(1)}) custom-call(f32[8,2,64,128]{3,2,1,0:T(8,128)S(1)} %get-tuple-element.39.center, f32[8,16,256]{2,1,0:T(8,128)S(1)} %get-tuple-element.40.xf, f32[8,16,256]{2,1,0:T(8,128)S(1)} %get-tuple-element.41.yf, f32[8,64,128]{2,1,0:T(8,128)S(1)} %get-tuple-element.42.zf, ...), custom_call_target="tpu_custom_call" | custom-call | tf_op jit(solution)/shard_map/pallas_call | solution.py:549
  18.3 2.0 %collective-permute-start.4 = (f32[16,896]{1,0:T(8,128)S(1)}, f32[16,896]{1,0:T(8,128)S(1)}, u32[]{:S(2)}, u32[]{:S(2)}) collective-permute-start(f32[16,896]{1,0:T(8,128)S(1)} %get-tuple-element.58), channel_id=1, source_target_pairs={{0,1},{1,0},{2,3},{3,2},{4,5},{5,4},{6,7},{7,6},{8,9},{9,8},{10,11... | collective-permute-start | bytes 172040 | tf_op jit(solution)/shard_map/ppermute | solution.py:486
  20.3 0.9 %shard_map.89 = f32[16,896]{1,0:T(8,128)S(1)} custom-call(bf16[640,1024]{1,0:T(8,128)(2,1)S(1)} %get-tuple-element.56.taps, bf16[384,640]{1,0:T(8,128)(2,1)S(1)} %get-tuple-element.57.keep_t), custom_call_target="tpu_custom_call" | custom-call | tf_op jit(solution)/shard_map/pallas_call | solution.py:563
  21.2 0.0 collective-permute-done.4
  21.2 1.7 %collective-permute-start.5 = (f32[16,896]{1,0:T(8,128)S(1)}, f32[16,896]{1,0:T(8,128)S(1)}, u32[]{:S(2)}, u32[]{:S(2)}) collective-permute-start(f32[16,896]{1,0:T(8,128)S(1)} %add.12), channel_id=1, source_target_pairs={{0,2},{1,3},{2,0},{3,1},{4,6},{5,7},{6,4},{7,5},{8,10},{9,11},{10,... | collective-permute-start | bytes 172040 | tf_op jit(solution)/shard_map/ppermute | solution.py:486
  22.9 2.7 %shard_map.90 = bf16[8,32,512]{2,1,0:T(8,128)(2,1)} custom-call(bf16[640,1024]{1,0:T(8,128)(2,1)S(1)} %get-tuple-element.56.taps, bf16[768,1024]{1,0:T(8,128)(2,1)S(1)} %get-tuple-element.59.wide, s32[8,512]{1,0:T(8,128)S(1)} %get-tuple-element.48.mask), custom_call_target="tpu_custom_call" | custom-call | tf_op jit(solution)/shard_map/pallas_call | solution.py:556
  25.6 0.0 collective-permute-done.5
  25.6 0.1 collective-permute-start.11
  25.7 1.2 %collective-permute-start.9 = (f32[16,896]{1,0:T(8,128)S(1)}, f32[16,896]{1,0:T(8,128)S(1)}, u32[]{:S(2)}, u32[]{:S(2)}) collective-permute-start(f32[16,896]{1,0:T(8,128)S(1)} %add.13), channel_id=1, source_target_pairs={{0,4},{1,5},{2,6},{3,7},{4,0},{5,1},{6,2},{7,3},{8,12},{9,13},{10,... | collective-permute-start | bytes 172040 | tf_op jit(solution)/shard_map/ppermute | solution.py:486
  26.9 3.2 %collective-permute-done.9 = f32[16,896]{1,0:T(8,128)S(1)} collective-permute-done((f32[16,896]{1,0:T(8,128)S(1)}, f32[16,896]{1,0:T(8,128)S(1)}, u32[]{:S(2)}, u32[]{:S(2)}) %collective-permute-start.9) | collective-permute-done | bytes 57376 | tf_op jit(solution)/shard_map/ppermute | solution.py:486
  30.1 1.0 %collective-permute-start.10 = (f32[16,896]{1,0:T(8,128)S(1)}, f32[16,896]{1,0:T(8,128)S(1)}, u32[]{:S(2)}, u32[]{:S(2)}) collective-permute-start(f32[16,896]{1,0:T(8,128)S(1)} %add.14), channel_id=1, source_target_pairs={{0,8},{1,9},{2,10},{3,11},{4,12},{5,13},{6,14},{7,15},{8,0},{9,1},... | collective-permute-start | bytes 172040 | tf_op jit(solution)/shard_map/ppermute | solution.py:486
  31.1 0.0 collective-permute-done.11.last
  31.1 2.6 %shard_map.91 = f32[8,32,512]{2,1,0:T(8,128)} custom-call(f32[8,2,64,128]{3,2,1,0:T(8,128)S(1)} %get-tuple-element.67.center, f32[8,16,256]{2,1,0:T(8,128)S(1)} %get-tuple-element.68.xg, f32[8,16,256]{2,1,0:T(8,128)S(1)} %get-tuple-element.69.yg, f32[8,64,128]{2,1,0:T(8,128)S(1)} %get-tuple-element.70.zg, s32[8,512]{1,0:T(8,128)S(1)} %get-tuple-element.48.mask, ...), custom_call_target="tpu_custom_call" | custom-call | tf_op jit(solution)/shard_map/pallas_call | solution.py:569
  33.7 1.5 %collective-permute-done.10 = f32[16,896]{1,0:T(8,128)S(1)} collective-permute-done((f32[16,896]{1,0:T(8,128)S(1)}, f32[16,896]{1,0:T(8,128)S(1)}, u32[]{:S(2)}, u32[]{:S(2)}) %collective-permute-start.10) | collective-permute-done | bytes 57376 | tf_op jit(solution)/shard_map/ppermute | solution.py:486
  35.3 0.1 collective-permute-start.12
  35.3 1.2 %collective-permute-done.12.other = f32[16,896]{1,0:T(8,128)S(1)} collective-permute-done((f32[16,896]{1,0:T(8,128)S(1)}, f32[16,896]{1,0:T(8,128)S(1)}, u32[]{:S(2)}, u32[]{:S(2)}) %collective-permute-start.12) | collective-permute-done | bytes 57376 | tf_op jit(solution)/shard_map/ppermute | solution.py:486
  36.6 0.9 %shard_map.92 = f32[27,32,32]{2,1,0:T(8,128)} custom-call(f32[16,896]{1,0:T(8,128)S(1)} %add.15.mine, f32[16,896]{1,0:T(8,128)S(1)} %collective-permute-done.12.other), custom_call_target="tpu_custom_call" | custom-call | tf_op jit(solution)/shard_map/pallas_call | solution.py:587
  (18 shorter events, 0.2 us)
Async XLA Ops:
  2.5 1.6 %collective-permute-start = (bf16[5,160,128]{2,1,0:T(8,128)(2,1)S(1)}, bf16[5,160,128]{2,1,0:T(8,128)(2,1)S(1)}, u32[]{:S(2)}, u32[]{:S(2)}) collective-permute-start(bf16[5,160,128]{2,1,0:T(8,128)(2,1)S(1)} %get-tuple-element.44), channel_id=1, source_target_pairs={{0,1},{1,0},{2,3},{3,2},{4,5},{5,4},{6,7},{7,6},{8,9},{9,8},{10,11... | collective-permute-start | bytes 614408 | tf_op jit(solution)/shard_map/ppermute | solution.py:486
  4.2 10.6 %collective-permute-start.1 = (bf16[4,160,128]{2,1,0:T(8,128)(2,1)S(1)}, bf16[4,160,128]{2,1,0:T(8,128)(2,1)S(1)}, u32[]{:S(2)}, u32[]{:S(2)}) collective-permute-start(bf16[4,160,128]{2,1,0:T(8,128)(2,1)S(1)} %pad_maximum_fusion), channel_id=1, source_target_pairs={{0,3},{1,14},{2,5},{3,0},{4,7},{5,2},{6,9},{7,4},{8,11},{9,6},{10,... | collective-permute-start | bytes 491528 | tf_op jit(solution)/shard_map/ppermute | solution.py:486
  6.8 7.9 %collective-permute-start.2 = (bf16[3,160,128]{2,1,0:T(8,128)(2,1)S(1)}, bf16[3,160,128]{2,1,0:T(8,128)(2,1)S(1)}, u32[]{:S(2)}, u32[]{:S(2)}) collective-permute-start(bf16[3,160,128]{2,1,0:T(8,128)(2,1)S(1)} %pad_maximum_fusion.2), channel_id=1, source_target_pairs={{0,4},{1,13},{2,6},{3,15},{4,8},{5,1},{6,10},{7,3},{8,12},{9,5},{1... | collective-permute-start | bytes 368648 | tf_op jit(solution)/shard_map/ppermute | solution.py:486
  11.7 3.4 %collective-permute-start.6 = (bf16[5,160,128]{2,1,0:T(8,128)(2,1)S(1)}, bf16[5,160,128]{2,1,0:T(8,128)(2,1)S(1)}, u32[]{:S(2)}, u32[]{:S(2)}) collective-permute-start(bf16[5,160,128]{2,1,0:T(8,128)(2,1)S(1)} %get-tuple-element.61), channel_id=1, source_target_pairs={{0,1},{1,0},{2,3},{3,2},{4,5},{5,4},{6,7},{7,6},{8,9},{9,8},{10,11... | collective-permute-start | bytes 614408 | tf_op jit(solution)/shard_map/ppermute | solution.py:486
  14.8 2.2 %collective-permute-start.3 = (bf16[3,160,128]{2,1,0:T(8,128)(2,1)S(1)}, bf16[3,160,128]{2,1,0:T(8,128)(2,1)S(1)}, u32[]{:S(2)}, u32[]{:S(2)}) collective-permute-start(bf16[3,160,128]{2,1,0:T(8,128)(2,1)S(1)} %pad_maximum_fusion.3), channel_id=1, source_target_pairs={{0,1},{1,0},{2,3},{3,2},{4,5},{5,4},{6,7},{7,6},{8,9},{9,8},{10,11... | collective-permute-start | bytes 368648 | tf_op jit(solution)/shard_map/ppermute | solution.py:486
  15.2 10.4 %collective-permute-start.7 = (bf16[4,160,128]{2,1,0:T(8,128)(2,1)S(1)}, bf16[4,160,128]{2,1,0:T(8,128)(2,1)S(1)}, u32[]{:S(2)}, u32[]{:S(2)}) collective-permute-start(bf16[4,160,128]{2,1,0:T(8,128)(2,1)S(1)} %pad_maximum_fusion.1), channel_id=1, source_target_pairs={{0,3},{1,14},{2,5},{3,0},{4,7},{5,2},{6,9},{7,4},{8,11},{9,6},{10,... | collective-permute-start | bytes 491528 | tf_op jit(solution)/shard_map/ppermute | solution.py:486
  17.0 8.5 %collective-permute-start.8 = (bf16[3,160,128]{2,1,0:T(8,128)(2,1)S(1)}, bf16[3,160,128]{2,1,0:T(8,128)(2,1)S(1)}, u32[]{:S(2)}, u32[]{:S(2)}) collective-permute-start(bf16[3,160,128]{2,1,0:T(8,128)(2,1)S(1)} %pad_maximum_fusion.4), channel_id=1, source_target_pairs={{0,4},{1,13},{2,6},{3,15},{4,8},{5,1},{6,10},{7,3},{8,12},{9,5},{1... | collective-permute-start | bytes 368648 | tf_op jit(solution)/shard_map/ppermute | solution.py:486
  18.3 2.9 %collective-permute-start.4 = (f32[16,896]{1,0:T(8,128)S(1)}, f32[16,896]{1,0:T(8,128)S(1)}, u32[]{:S(2)}, u32[]{:S(2)}) collective-permute-start(f32[16,896]{1,0:T(8,128)S(1)} %get-tuple-element.58), channel_id=1, source_target_pairs={{0,1},{1,0},{2,3},{3,2},{4,5},{5,4},{6,7},{7,6},{8,9},{9,8},{10,11... | collective-permute-start | bytes 172040 | tf_op jit(solution)/shard_map/ppermute | solution.py:486
  21.2 4.4 %collective-permute-start.5 = (f32[16,896]{1,0:T(8,128)S(1)}, f32[16,896]{1,0:T(8,128)S(1)}, u32[]{:S(2)}, u32[]{:S(2)}) collective-permute-start(f32[16,896]{1,0:T(8,128)S(1)} %add.12), channel_id=1, source_target_pairs={{0,2},{1,3},{2,0},{3,1},{4,6},{5,7},{6,4},{7,5},{8,10},{9,11},{10,... | collective-permute-start | bytes 172040 | tf_op jit(solution)/shard_map/ppermute | solution.py:486
  25.6 5.5 %collective-permute-start.11 = (bf16[3,160,128]{2,1,0:T(8,128)(2,1)S(1)}, bf16[3,160,128]{2,1,0:T(8,128)(2,1)S(1)}, u32[]{:S(2)}, u32[]{:S(2)}) collective-permute-start(bf16[3,160,128]{2,1,0:T(8,128)(2,1)S(1)} %pad_maximum_fusion.5), channel_id=1, source_target_pairs={{0,1},{1,0},{2,3},{3,2},{4,5},{5,4},{6,7},{7,6},{8,9},{9,8},{10,11... | collective-permute-start | bytes 368648 | tf_op jit(solution)/shard_map/ppermute | solution.py:486
  25.7 4.4 %collective-permute-start.9 = (f32[16,896]{1,0:T(8,128)S(1)}, f32[16,896]{1,0:T(8,128)S(1)}, u32[]{:S(2)}, u32[]{:S(2)}) collective-permute-start(f32[16,896]{1,0:T(8,128)S(1)} %add.13), channel_id=1, source_target_pairs={{0,4},{1,5},{2,6},{3,7},{4,0},{5,1},{6,2},{7,3},{8,12},{9,13},{10,... | collective-permute-start | bytes 172040 | tf_op jit(solution)/shard_map/ppermute | solution.py:486
  30.1 5.2 %collective-permute-start.10 = (f32[16,896]{1,0:T(8,128)S(1)}, f32[16,896]{1,0:T(8,128)S(1)}, u32[]{:S(2)}, u32[]{:S(2)}) collective-permute-start(f32[16,896]{1,0:T(8,128)S(1)} %add.14), channel_id=1, source_target_pairs={{0,8},{1,9},{2,10},{3,11},{4,12},{5,13},{6,14},{7,15},{8,0},{9,1},... | collective-permute-start | bytes 172040 | tf_op jit(solution)/shard_map/ppermute | solution.py:486
  35.3 1.3 %collective-permute-start.12 = (f32[16,896]{1,0:T(8,128)S(1)}, f32[16,896]{1,0:T(8,128)S(1)}, u32[]{:S(2)}, u32[]{:S(2)}) collective-permute-start(f32[16,896]{1,0:T(8,128)S(1)} %add.15.mine), channel_id=1, source_target_pairs={{0,1},{1,0},{2,3},{3,2},{4,5},{5,4},{6,7},{7,6},{8,9},{9,8},{10,11... | collective-permute-start | bytes 172040 | tf_op jit(solution)/shard_map/ppermute | solution.py:486

commit v6 on v5

--- a/solution.py
+++ b/solution.py
@@ -151,7 +151,7 @@
     return y == 0, y == 7
 
 
-def stack_kernel(cot, mask, stack):
+def stack_kernel(cot, mask, weights, stack, wide):
     order = voxel_order()
     bricks = to_rows(masked_values(cot[...], mask[...]), order)
     for b in range(8):
@@ -161,15 +161,6 @@
             pieces = [p for p in (before, c, after) if p.shape[0]]
             stack[80 * b : 80 * b + 80, 256 * d : 256 * d + 256] = jnp.concatenate(pieces, axis=0).astype(BF16)
 
-
-def back_kernel(
-    stack, weights, kmap,
-    wide, keep_t, give_t, center, xg, yg, zg, table, first, own_near, own_far,
-    gp, xa, ya, za, entries, sem,
-):
-    e = kmap[...]
-    entries[...] = jnp.where(e < 0, DUMMY, jnp.where(e < 8, e, ((e - 8) ^ (parity() * 8)) + 8))
-    to_table = fetch((entries, table, sem.at[0]))[0]
     tile = jnp.where((iota((32, 256), 1) & 31) == iota((32, 256), 0), 1.0, 0.0).astype(BF16)
     tiled = dot(weights[...].reshape(864, 32), tile, NN)
     block = iota((32, 256), 1) >> 5
@@ -193,6 +184,15 @@
                     w = jnp.where(block == 2 * dy + (z == 7), tap(dx, dy, 0 if z == 0 else 2), w)
             wide[rows, 768:1024] = w.astype(BF16)
 
+
+def back_kernel(
+    stack, wide, kmap,
+    keep_t, give_t, center, xg, yg, zg, table, first, own_near, own_far,
+    gp, xa, ya, za, entries, sem,
+):
+    e = kmap[...]
+    entries[...] = jnp.where(e < 0, DUMMY, jnp.where(e < 8, e, ((e - 8) ^ (parity() * 8)) + 8))
+    to_table = fetch((entries, table, sem.at[0]))[0]
     odd = parity() == 1
     for d in range(3):
         turned = stack[:, 256 * d : 256 * d + 256].T.reshape(8, 2, 16, 640)
@@ -531,20 +531,22 @@
         1 << 21,
     )(in_hbm(features), in_hbm(voxel_mask), send, in_hbm(grad_out), in_hbm(weights), in_hbm(kernel_map))
     first = swap(first)
-    (stack,) = call(stack_kernel, [((640, 768), BF16)], [], [VMEM] * 2, 1 << 28, 2 << 20)(cot, mask)
-    near, far, kmap, stack = exchange(first, own_near, own_far, kmap, stack)
+    stack, wide = call(
+        stack_kernel, [((640, 768), BF16), ((768, 1024), BF16)], [], [VMEM] * 3, 1 << 28, 2 << 20
+    )(cot, mask, taps_w)
+    near, far, kmap, stack, wide = exchange(first, own_near, own_far, kmap, stack, wide)
     last = exchange_end(near, far)
 
-    wide, keep_t, give_t, grad_center, xg, yg, zg, table, grad_first, grad_near, grad_far = call(
+    keep_t, give_t, grad_center, xg, yg, zg, table, grad_first, grad_near, grad_far = call(
         back_kernel,
-        [((768, 1024), BF16), ((384, 640), BF16), ((384, 640), BF16), center_shape]
+        [((384, 640), BF16), ((384, 640), BF16), center_shape]
         + face_shapes
         + [pltpu.SMEM((8, 27), jnp.int32), block(5), block(2), block(1)],
         [vm(8, 640, 128)] + accumulators + [pltpu.VMEM((8, 27), jnp.int32), sems(1)],
         [VMEM] * 3,
         2 * 640 * 768 * 1024,
         8 << 20,
-    )(stack, taps_w, kmap)
+    )(stack, wide, kmap)
 
     taps, give = call(
         taps_kernel,

time: 37.6 us -> 37.7 us (level)
  no operation moved by 1% of the time
where the time goes in v6:
time: 37.7 us; the launch traced here: 37.5 us
  starting transfers between devices  14.9 us (40%)
  Pallas kernels  14 us (37%)
  waiting for transfers between devices  7.62 us (20%)
  between operations  0.78 us (2%)
    ppermute x13, starting transfers between devices, permute(): lax.ppermute(value, RANGE_AXES, [(r, target(r, count)) for r in range(cou...  14.9 us
    ppermute x13, waiting for transfers between devices, permute(): lax.ppermute(value, RANGE_AXES, [(r, target(r, count)) for r in range(cou...  7.62 us
    pallas_call x1, Pallas kernels, body(): call(back_kernel, [((384, 640), BF16), ((384, 640), BF16), center_shape]...  2.85 us
    pallas_call x1, Pallas kernels, body(): call(conv_kernel, [((8, 32, 512), BF16)], [], [VMEM] * 3)(taps, wide, mask)  2.67 us
    pallas_call x1, Pallas kernels, body(): call(fold_kernel, [((8, 32, 512), F32)], [vm(8, 16, 256), vm(8, 16, 256),...  2.63 us
    pallas_call x1, Pallas kernels, body(): call(pack_kernel, [block(5), block(2), block(1), center_shape] + face_sha...  1.88 us
    pallas_call x1, Pallas kernels, body(): call(taps_kernel, [((640, 1024), BF16), ((16, 896), F32)], accumulators,...  1.26 us
    pallas_call x1, Pallas kernels, body(): keep, = call(keep_kernel, [((16, 896), F32)], [], [VMEM] * 2)(taps, keep_t)  0.93 us
  transfers between devices with their start and end apart: 13, of which 5 were waited for; matrix products, arithmetic and copies ran while one was open for 0% of the time, Pallas kernels for 30%

profile of v6, /device:TPU:0, one launch (start us, length us, event | category | flops | bytes accessed | tf_op | source)
XLA Modules:
  0.0 37.5 jit_solution(7262736803302876434)
XLA Ops:
  0.6 1.9 %shard_map.85 = (bf16[5,160,128]{2,1,0:T(8,128)(2,1)S(1)}, bf16[2,160,128]{2,1,0:T(8,128)(2,1)S(1)}, bf16[1,160,128]{2,1,0:T(8,128)(2,1)S(1)}, f32[8,2,64,128]{3...) custom-call(bf16[8,32,512]{2,1,0:T(8,128)(2,1)} %feat_hbm.1, ...), custom_call_target="tpu_custom_call" | custom-call | flops 134217728 | bytes 2097152 | tf_op jit(solution)/shard_map/pallas_call | solution.py:523
  2.5 0.5 %collective-permute-start = (bf16[5,160,128]{2,1,0:T(8,128)(2,1)S(1)}, bf16[5,160,128]{2,1,0:T(8,128)(2,1)S(1)}, u32[]{:S(2)}, u32[]{:S(2)}) collective-permute-start(bf16[5,160,128]{2,1,0:T(8,128)(2,1)S(1)} %get-tuple-element.46), channel_id=1, source_target_pairs={{0,1},{1,0},{2,3},{3,2},{4,5},{5,4},{6,7},{7,6},{8,9},{9,8},{10,11... | collective-permute-start | bytes 614408 | tf_op jit(solution)/shard_map/ppermute | solution.py:486
  3.0 0.9 %shard_map.86 = (bf16[640,768]{1,0:T(8,128)(2,1)S(1)}, bf16[768,1024]{1,0:T(8,128)(2,1)S(1)}) custom-call(bf16[8,32,512]{2,1,0:T(8,128)(2,1)S(1)} %get-tuple-element.49.cot, s32[8,512]{1,0:T(8,128)S(1)} %get-tuple-element.50.mask, bf16[27,32,32]{2,1,0:T(8,128)(2,1)S(1)} %get-tuple-element.51.weights), custom_call_target="tpu_custom_call" | custom-call | flops 268435456 | bytes 2097152 | tf_op jit(solution)/shard_map/pallas_call | solution.py:534
  3.9 0.2 collective-permute-done.first
  4.2 2.7 %collective-permute-start.1 = (bf16[4,160,128]{2,1,0:T(8,128)(2,1)S(1)}, bf16[4,160,128]{2,1,0:T(8,128)(2,1)S(1)}, u32[]{:S(2)}, u32[]{:S(2)}) collective-permute-start(bf16[4,160,128]{2,1,0:T(8,128)(2,1)S(1)} %pad_maximum_fusion), channel_id=1, source_target_pairs={{0,3},{1,14},{2,5},{3,0},{4,7},{5,2},{6,9},{7,4},{8,11},{9,6},{10,... | collective-permute-start | bytes 491528 | tf_op jit(solution)/shard_map/ppermute | solution.py:486
  6.8 1.6 %collective-permute-start.2 = (bf16[3,160,128]{2,1,0:T(8,128)(2,1)S(1)}, bf16[3,160,128]{2,1,0:T(8,128)(2,1)S(1)}, u32[]{:S(2)}, u32[]{:S(2)}) collective-permute-start(bf16[3,160,128]{2,1,0:T(8,128)(2,1)S(1)} %pad_maximum_fusion.2), channel_id=1, source_target_pairs={{0,4},{1,13},{2,6},{3,15},{4,8},{5,1},{6,10},{7,3},{8,12},{9,5},{1... | collective-permute-start | bytes 368648 | tf_op jit(solution)/shard_map/ppermute | solution.py:486
  8.4 2.8 %shard_map.87 = (bf16[384,640]{1,0:T(8,128)(2,1)S(1)}, bf16[384,640]{1,0:T(8,128)(2,1)S(1)}, f32[8,2,64,128]{3,2,1,0:T(8,128)S(1)}, f32[8,16,256]{2,1,0:T(8,128)...) custom-call(bf16[640,768]{1,0:T(8,128)(2,1)S(1)} %get-tuple-element., ...), custom_call_target="tpu_custom_call" | custom-call | flops 1006632960 | bytes 8388608 | tf_op jit(solution)/shard_map/pallas_call | solution.py:540
  11.3 2.1 %collective-permute-start.6 = (bf16[5,160,128]{2,1,0:T(8,128)(2,1)S(1)}, bf16[5,160,128]{2,1,0:T(8,128)(2,1)S(1)}, u32[]{:S(2)}, u32[]{:S(2)}) collective-permute-start(bf16[5,160,128]{2,1,0:T(8,128)(2,1)S(1)} %get-tuple-element.65), channel_id=1, source_target_pairs={{0,1},{1,0},{2,3},{3,2},{4,5},{5,4},{6,7},{7,6},{8,9},{9,8},{10,11... | collective-permute-start | bytes 614408 | tf_op jit(solution)/shard_map/ppermute | solution.py:486
  13.4 1.4 %collective-permute-done.2.far = bf16[3,160,128]{2,1,0:T(8,128)(2,1)S(1)} collective-permute-done((bf16[3,160,128]{2,1,0:T(8,128)(2,1)S(1)}, bf16[3,160,128]{2,1,0:T(8,128)(2,1)S(1)}, u32[]{:S(2)}, u32[]{:S(2)}) %collective-permute-start.2) | collective-permute-done | bytes 122912 | tf_op jit(solution)/shard_map/ppermute | solution.py:486
  14.8 0.0 collective-permute-done.1.near
  14.8 0.2 collective-permute-start.3
  15.1 0.0 collective-permute-done.6.first
  15.2 1.9 %collective-permute-start.7 = (bf16[4,160,128]{2,1,0:T(8,128)(2,1)S(1)}, bf16[4,160,128]{2,1,0:T(8,128)(2,1)S(1)}, u32[]{:S(2)}, u32[]{:S(2)}) collective-permute-start(bf16[4,160,128]{2,1,0:T(8,128)(2,1)S(1)} %pad_maximum_fusion.1), channel_id=1, source_target_pairs={{0,3},{1,14},{2,5},{3,0},{4,7},{5,2},{6,9},{7,4},{8,11},{9,6},{10,... | collective-permute-start | bytes 491528 | tf_op jit(solution)/shard_map/ppermute | solution.py:486
  17.0 0.0 collective-permute-start.8
  17.0 1.3 %shard_map.88 = (bf16[640,1024]{1,0:T(8,128)(2,1)S(1)}, f32[16,896]{1,0:T(8,128)S(1)}) custom-call(f32[8,2,64,128]{3,2,1,0:T(8,128)S(1)} %get-tuple-element.41.center, f32[8,16,256]{2,1,0:T(8,128)S(1)} %get-tuple-element.42.xf, f32[8,16,256]{2,1,0:T(8,128)S(1)} %get-tuple-element.43.yf, f32[8,64,128]{2,1,0:T(8,128)S(1)} %get-tuple-element.44.zf, ...), custom_call_target="tpu_custom_call" | custom-call | tf_op jit(solution)/shard_map/pallas_call | solution.py:551
  18.3 2.0 %collective-permute-start.4 = (f32[16,896]{1,0:T(8,128)S(1)}, f32[16,896]{1,0:T(8,128)S(1)}, u32[]{:S(2)}, u32[]{:S(2)}) collective-permute-start(f32[16,896]{1,0:T(8,128)S(1)} %get-tuple-element.63), channel_id=1, source_target_pairs={{0,1},{1,0},{2,3},{3,2},{4,5},{5,4},{6,7},{7,6},{8,9},{9,8},{10,11... | collective-permute-start | bytes 172040 | tf_op jit(solution)/shard_map/ppermute | solution.py:486
  20.3 0.9 %shard_map.89 = f32[16,896]{1,0:T(8,128)S(1)} custom-call(bf16[640,1024]{1,0:T(8,128)(2,1)S(1)} %get-tuple-element.61.taps, bf16[384,640]{1,0:T(8,128)(2,1)S(1)} %get-tuple-element.62.keep_t), custom_call_target="tpu_custom_call" | custom-call | tf_op jit(solution)/shard_map/pallas_call | solution.py:565
  21.2 1.7 %collective-permute-start.5 = (f32[16,896]{1,0:T(8,128)S(1)}, f32[16,896]{1,0:T(8,128)S(1)}, u32[]{:S(2)}, u32[]{:S(2)}) collective-permute-start(f32[16,896]{1,0:T(8,128)S(1)} %add.12), channel_id=1, source_target_pairs={{0,2},{1,3},{2,0},{3,1},{4,6},{5,7},{6,4},{7,5},{8,10},{9,11},{10,... | collective-permute-start | bytes 172040 | tf_op jit(solution)/shard_map/ppermute | solution.py:486
  22.9 2.7 %shard_map.90 = bf16[8,32,512]{2,1,0:T(8,128)(2,1)} custom-call(bf16[640,1024]{1,0:T(8,128)(2,1)S(1)} %get-tuple-element.61.taps, bf16[768,1024]{1,0:T(8,128)(2,1)S(1)} %get-tuple-element.55.wide, s32[8,512]{1,0:T(8,128)S(1)} %get-tuple-element.50.mask), custom_call_target="tpu_custom_call" | custom-call | tf_op jit(solution)/shard_map/pallas_call | solution.py:558
  25.6 0.0 collective-permute-done.8.far
  25.6 0.0 collective-permute-done.7.near
  25.6 0.0 collective-permute-done.5
  25.6 0.1 collective-permute-start.11
  25.7 1.2 %collective-permute-start.9 = (f32[16,896]{1,0:T(8,128)S(1)}, f32[16,896]{1,0:T(8,128)S(1)}, u32[]{:S(2)}, u32[]{:S(2)}) collective-permute-start(f32[16,896]{1,0:T(8,128)S(1)} %add.13), channel_id=1, source_target_pairs={{0,4},{1,5},{2,6},{3,7},{4,0},{5,1},{6,2},{7,3},{8,12},{9,13},{10,... | collective-permute-start | bytes 172040 | tf_op jit(solution)/shard_map/ppermute | solution.py:486
  26.9 3.2 %collective-permute-done.9 = f32[16,896]{1,0:T(8,128)S(1)} collective-permute-done((f32[16,896]{1,0:T(8,128)S(1)}, f32[16,896]{1,0:T(8,128)S(1)}, u32[]{:S(2)}, u32[]{:S(2)}) %collective-permute-start.9) | collective-permute-done | bytes 57376 | tf_op jit(solution)/shard_map/ppermute | solution.py:486
  30.1 1.0 %collective-permute-start.10 = (f32[16,896]{1,0:T(8,128)S(1)}, f32[16,896]{1,0:T(8,128)S(1)}, u32[]{:S(2)}, u32[]{:S(2)}) collective-permute-start(f32[16,896]{1,0:T(8,128)S(1)} %add.14), channel_id=1, source_target_pairs={{0,8},{1,9},{2,10},{3,11},{4,12},{5,13},{6,14},{7,15},{8,0},{9,1},... | collective-permute-start | bytes 172040 | tf_op jit(solution)/shard_map/ppermute | solution.py:486
  31.1 0.0 collective-permute-done.11.last
  31.1 2.6 %shard_map.91 = f32[8,32,512]{2,1,0:T(8,128)} custom-call(f32[8,2,64,128]{3,2,1,0:T(8,128)S(1)} %get-tuple-element.71.center, f32[8,16,256]{2,1,0:T(8,128)S(1)} %get-tuple-element.72.xg, f32[8,16,256]{2,1,0:T(8,128)S(1)} %get-tuple-element.73.yg, f32[8,64,128]{2,1,0:T(8,128)S(1)} %get-tuple-element.74.zg, s32[8,512]{1,0:T(8,128)S(1)} %get-tuple-element.50.mask, ...), custom_call_target="tpu_custom_call" | custom-call | tf_op jit(solution)/shard_map/pallas_call | solution.py:571
  33.7 1.6 %collective-permute-done.10 = f32[16,896]{1,0:T(8,128)S(1)} collective-permute-done((f32[16,896]{1,0:T(8,128)S(1)}, f32[16,896]{1,0:T(8,128)S(1)}, u32[]{:S(2)}, u32[]{:S(2)}) %collective-permute-start.10) | collective-permute-done | bytes 57376 | tf_op jit(solution)/shard_map/ppermute | solution.py:486
  35.3 0.1 collective-permute-start.12
  35.3 1.2 %collective-permute-done.12.other = f32[16,896]{1,0:T(8,128)S(1)} collective-permute-done((f32[16,896]{1,0:T(8,128)S(1)}, f32[16,896]{1,0:T(8,128)S(1)}, u32[]{:S(2)}, u32[]{:S(2)}) %collective-permute-start.12) | collective-permute-done | bytes 57376 | tf_op jit(solution)/shard_map/ppermute | solution.py:486
  36.6 0.9 %shard_map.92 = f32[27,32,32]{2,1,0:T(8,128)} custom-call(f32[16,896]{1,0:T(8,128)S(1)} %add.15.mine, f32[16,896]{1,0:T(8,128)S(1)} %collective-permute-done.12.other), custom_call_target="tpu_custom_call" | custom-call | tf_op jit(solution)/shard_map/pallas_call | solution.py:589
  (18 shorter events, 0.2 us)
Async XLA Ops:
  2.5 1.6 %collective-permute-start = (bf16[5,160,128]{2,1,0:T(8,128)(2,1)S(1)}, bf16[5,160,128]{2,1,0:T(8,128)(2,1)S(1)}, u32[]{:S(2)}, u32[]{:S(2)}) collective-permute-start(bf16[5,160,128]{2,1,0:T(8,128)(2,1)S(1)} %get-tuple-element.46), channel_id=1, source_target_pairs={{0,1},{1,0},{2,3},{3,2},{4,5},{5,4},{6,7},{7,6},{8,9},{9,8},{10,11... | collective-permute-start | bytes 614408 | tf_op jit(solution)/shard_map/ppermute | solution.py:486
  4.2 10.6 %collective-permute-start.1 = (bf16[4,160,128]{2,1,0:T(8,128)(2,1)S(1)}, bf16[4,160,128]{2,1,0:T(8,128)(2,1)S(1)}, u32[]{:S(2)}, u32[]{:S(2)}) collective-permute-start(bf16[4,160,128]{2,1,0:T(8,128)(2,1)S(1)} %pad_maximum_fusion), channel_id=1, source_target_pairs={{0,3},{1,14},{2,5},{3,0},{4,7},{5,2},{6,9},{7,4},{8,11},{9,6},{10,... | collective-permute-start | bytes 491528 | tf_op jit(solution)/shard_map/ppermute | solution.py:486
  6.8 7.9 %collective-permute-start.2 = (bf16[3,160,128]{2,1,0:T(8,128)(2,1)S(1)}, bf16[3,160,128]{2,1,0:T(8,128)(2,1)S(1)}, u32[]{:S(2)}, u32[]{:S(2)}) collective-permute-start(bf16[3,160,128]{2,1,0:T(8,128)(2,1)S(1)} %pad_maximum_fusion.2), channel_id=1, source_target_pairs={{0,4},{1,13},{2,6},{3,15},{4,8},{5,1},{6,10},{7,3},{8,12},{9,5},{1... | collective-permute-start | bytes 368648 | tf_op jit(solution)/shard_map/ppermute | solution.py:486
  11.3 3.8 %collective-permute-start.6 = (bf16[5,160,128]{2,1,0:T(8,128)(2,1)S(1)}, bf16[5,160,128]{2,1,0:T(8,128)(2,1)S(1)}, u32[]{:S(2)}, u32[]{:S(2)}) collective-permute-start(bf16[5,160,128]{2,1,0:T(8,128)(2,1)S(1)} %get-tuple-element.65), channel_id=1, source_target_pairs={{0,1},{1,0},{2,3},{3,2},{4,5},{5,4},{6,7},{7,6},{8,9},{9,8},{10,11... | collective-permute-start | bytes 614408 | tf_op jit(solution)/shard_map/ppermute | solution.py:486
  14.8 2.2 %collective-permute-start.3 = (bf16[3,160,128]{2,1,0:T(8,128)(2,1)S(1)}, bf16[3,160,128]{2,1,0:T(8,128)(2,1)S(1)}, u32[]{:S(2)}, u32[]{:S(2)}) collective-permute-start(bf16[3,160,128]{2,1,0:T(8,128)(2,1)S(1)} %pad_maximum_fusion.3), channel_id=1, source_target_pairs={{0,1},{1,0},{2,3},{3,2},{4,5},{5,4},{6,7},{7,6},{8,9},{9,8},{10,11... | collective-permute-start | bytes 368648 | tf_op jit(solution)/shard_map/ppermute | solution.py:486
  15.2 10.4 %collective-permute-start.7 = (bf16[4,160,128]{2,1,0:T(8,128)(2,1)S(1)}, bf16[4,160,128]{2,1,0:T(8,128)(2,1)S(1)}, u32[]{:S(2)}, u32[]{:S(2)}) collective-permute-start(bf16[4,160,128]{2,1,0:T(8,128)(2,1)S(1)} %pad_maximum_fusion.1), channel_id=1, source_target_pairs={{0,3},{1,14},{2,5},{3,0},{4,7},{5,2},{6,9},{7,4},{8,11},{9,6},{10,... | collective-permute-start | bytes 491528 | tf_op jit(solution)/shard_map/ppermute | solution.py:486
  17.0 8.5 %collective-permute-start.8 = (bf16[3,160,128]{2,1,0:T(8,128)(2,1)S(1)}, bf16[3,160,128]{2,1,0:T(8,128)(2,1)S(1)}, u32[]{:S(2)}, u32[]{:S(2)}) collective-permute-start(bf16[3,160,128]{2,1,0:T(8,128)(2,1)S(1)} %pad_maximum_fusion.4), channel_id=1, source_target_pairs={{0,4},{1,13},{2,6},{3,15},{4,8},{5,1},{6,10},{7,3},{8,12},{9,5},{1... | collective-permute-start | bytes 368648 | tf_op jit(solution)/shard_map/ppermute | solution.py:486
  18.3 2.9 %collective-permute-start.4 = (f32[16,896]{1,0:T(8,128)S(1)}, f32[16,896]{1,0:T(8,128)S(1)}, u32[]{:S(2)}, u32[]{:S(2)}) collective-permute-start(f32[16,896]{1,0:T(8,128)S(1)} %get-tuple-element.63), channel_id=1, source_target_pairs={{0,1},{1,0},{2,3},{3,2},{4,5},{5,4},{6,7},{7,6},{8,9},{9,8},{10,11... | collective-permute-start | bytes 172040 | tf_op jit(solution)/shard_map/ppermute | solution.py:486
  21.2 4.3 %collective-permute-start.5 = (f32[16,896]{1,0:T(8,128)S(1)}, f32[16,896]{1,0:T(8,128)S(1)}, u32[]{:S(2)}, u32[]{:S(2)}) collective-permute-start(f32[16,896]{1,0:T(8,128)S(1)} %add.12), channel_id=1, source_target_pairs={{0,2},{1,3},{2,0},{3,1},{4,6},{5,7},{6,4},{7,5},{8,10},{9,11},{10,... | collective-permute-start | bytes 172040 | tf_op jit(solution)/shard_map/ppermute | solution.py:486
  25.6 5.4 %collective-permute-start.11 = (bf16[3,160,128]{2,1,0:T(8,128)(2,1)S(1)}, bf16[3,160,128]{2,1,0:T(8,128)(2,1)S(1)}, u32[]{:S(2)}, u32[]{:S(2)}) collective-permute-start(bf16[3,160,128]{2,1,0:T(8,128)(2,1)S(1)} %pad_maximum_fusion.5), channel_id=1, source_target_pairs={{0,1},{1,0},{2,3},{3,2},{4,5},{5,4},{6,7},{7,6},{8,9},{9,8},{10,11... | collective-permute-start | bytes 368648 | tf_op jit(solution)/shard_map/ppermute | solution.py:486
  25.7 4.4 %collective-permute-start.9 = (f32[16,896]{1,0:T(8,128)S(1)}, f32[16,896]{1,0:T(8,128)S(1)}, u32[]{:S(2)}, u32[]{:S(2)}) collective-permute-start(f32[16,896]{1,0:T(8,128)S(1)} %add.13), channel_id=1, source_target_pairs={{0,4},{1,5},{2,6},{3,7},{4,0},{5,1},{6,2},{7,3},{8,12},{9,13},{10,... | collective-permute-start | bytes 172040 | tf_op jit(solution)/shard_map/ppermute | solution.py:486
  30.1 5.2 %collective-permute-start.10 = (f32[16,896]{1,0:T(8,128)S(1)}, f32[16,896]{1,0:T(8,128)S(1)}, u32[]{:S(2)}, u32[]{:S(2)}) collective-permute-start(f32[16,896]{1,0:T(8,128)S(1)} %add.14), channel_id=1, source_target_pairs={{0,8},{1,9},{2,10},{3,11},{4,12},{5,13},{6,14},{7,15},{8,0},{9,1},... | collective-permute-start | bytes 172040 | tf_op jit(solution)/shard_map/ppermute | solution.py:486
  35.3 1.3 %collective-permute-start.12 = (f32[16,896]{1,0:T(8,128)S(1)}, f32[16,896]{1,0:T(8,128)S(1)}, u32[]{:S(2)}, u32[]{:S(2)}) collective-permute-start(f32[16,896]{1,0:T(8,128)S(1)} %add.15.mine), channel_id=1, source_target_pairs={{0,1},{1,0},{2,3},{3,2},{4,5},{5,4},{6,7},{7,6},{8,9},{9,8},{10,11... | collective-permute-start | bytes 172040 | tf_op jit(solution)/shard_map/ppermute | solution.py:486
